TPU v7x, 128 devices: a whole 4x4x4 slice. The times are simulated.
128 devices in a mesh: ctx: 32 (over y, z, core), head: 4 (over x).
Axes of the slice: x: 4, y: 4, z: 4, core: 2. Of those that a mesh axis runs over, the one named last changes fastest.
Arguments:
- query_rows: bfloat16 [32768, 4096], P('ctx', 'head'), may hold values from -6 to 6
- key_rows: bfloat16 [32768, 4096], P('ctx', 'head'), may hold values from -6 to 6
- value_rows: bfloat16 [32768, 4096], P('ctx', 'head'), may hold values from -6 to 6
- level_gate: float32 [8, 32, 32768], P(None, 'head', 'ctx'), may hold values from 0 to 2.5, as said below
- out_weight: bfloat16 [4096, 4096], P('head'), may hold values from -0.09375 to 0.09375
Outputs:
- output: bfloat16 [32768, 4096], P(('ctx', 'head'))
Inputs may be any that keep to these rules, and one draw needn't show every extreme that they name: `level_gate`: every gate weight is positive.
All inputs are finite; a program needn't handle non-finite values.
Results may differ from a plain program's by a relative error of at most 0.015.
Values may be sent and summed in bfloat16 or wider, within the bound.
No kernel may reach another device: no remote copies, remote signals or barrier semaphores. Data moves between devices by JAX's collectives and lax.ppermute only.
A program may use at most 128 MiB of HBM per device.

v0:
```python
import jax
import jax.numpy as jnp
from jax import lax
from jax.sharding import PartitionSpec as P

C = 256


EPS = 1e-06


def on_device(query_rows, key_rows, value_rows, level_gate, out_weight):
    tokens = query_rows.shape[0]
    local_heads = level_gate.shape[1]
    width = query_rows.shape[1] // local_heads
    stretches = tokens // C
    stretch_bits = stretches.bit_length() - 1
    ctx_bits = lax.axis_size("ctx").bit_length() - 1
    query_stretches = query_rows.reshape(stretches, C, local_heads, width)
    key_stretches = key_rows.reshape(stretches, C, local_heads, width)
    value_stretches = value_rows.reshape(stretches, C, local_heads, width)
    gate_rows = jnp.transpose(level_gate, (0, 2, 1)).reshape(
        level_gate.shape[0], stretches, C, local_heads, 1
    )
    scores = jnp.einsum(
        "cthi,cshi->chts", query_stretches, key_stretches, preferred_element_type=jnp.float32
    )
    row_ids = lax.broadcasted_iota(jnp.int32, (C, C), 0)
    col_ids = lax.broadcasted_iota(jnp.int32, (C, C), 1)
    first_gate = jnp.transpose(gate_rows[0][..., 0], (0, 2, 1))[:, :, :, None]
    weights = (jnp.where(row_ids >= col_ids, scores, 0.0) * first_gate).astype(jnp.bfloat16)
    combined = jnp.einsum(
        "chts,cshj->cthj", weights, value_stretches, preferred_element_type=jnp.float32
    )
    stretch_state = jnp.einsum(
        "cshi,cshj->chij", key_stretches, value_stretches, preferred_element_type=jnp.float32
    )
    stretch_ids = jnp.arange(stretches, dtype=jnp.int32)
    for level_bit in range(stretch_bits):
        span_size = 2**level_bit
        grouped = stretch_state.reshape(
            stretches // span_size, span_size, local_heads, width, width
        ).sum(axis=1)
        owner_block = stretch_ids // span_size
        block_ids = jnp.arange(stretches // span_size, dtype=jnp.int32)
        picker = (
            (owner_block[:, None] - 1 == block_ids[None, :]) & (owner_block[:, None] % 2 == 1)
        ).astype(jnp.float32)
        bucket = jnp.einsum(
            "cb,bhij->chij", picker, grouped, precision=lax.Precision.HIGHEST
        ).astype(jnp.bfloat16)
        readout = jnp.einsum(
            "cthi,chij->cthj", query_stretches, bucket, preferred_element_type=jnp.float32
        )
        combined = combined + readout * gate_rows[level_bit + 1]
    device_total = stretch_state.sum(axis=0)
    my_index = lax.axis_index("ctx")
    empty = jnp.zeros((ctx_bits, local_heads, width, width), jnp.float32)
    piece = lax.all_gather(
        device_total[None].astype(jnp.bfloat16), "ctx", axis=0, tiled=True
    ).astype(jnp.float32)
    sources = jnp.arange(piece.shape[0], dtype=jnp.int32)
    differ = jnp.bitwise_xor(sources, my_index)
    level_ids = jnp.arange(ctx_bits, dtype=jnp.int32)
    powers = jnp.left_shift(jnp.ones_like(level_ids), level_ids)
    picker = ((sources[:, None] < my_index) & (differ[:, None] // powers[None, :] == 1)).astype(
        jnp.float32
    )
    gathered = empty + jnp.einsum("nl,nhij->lhij", picker, piece, precision=lax.Precision.HIGHEST)
    far_states = [gathered[level_bit] for level_bit in range(ctx_bits)]
    for level_bit in range(ctx_bits):
        bucket = far_states[level_bit].astype(jnp.bfloat16)
        readout = jnp.einsum(
            "cthi,hij->cthj", query_stretches, bucket, preferred_element_type=jnp.float32
        )
        combined = combined + readout * gate_rows[stretch_bits + 1 + level_bit]
    normed = (
        combined * lax.rsqrt(jnp.mean(combined * combined, axis=-1, keepdims=True) + EPS)
    ).astype(jnp.bfloat16)
    normed = normed.reshape(tokens, local_heads * width)
    partial_sum = jnp.dot(normed, out_weight, preferred_element_type=jnp.float32)
    return lax.psum_scatter(
        lax.optimization_barrier(partial_sum.astype(jnp.bfloat16))
        .astype(jnp.float32)
        .astype(jnp.bfloat16),
        "head",
        scatter_dimension=0,
        tiled=True,
    )


def solution(mesh):
    in_specs = (
        P("ctx", "head"),
        P("ctx", "head"),
        P("ctx", "head"),
        P(None, "head", "ctx"),
        P("head", None),
    )
    out_specs = P(("ctx", "head"), None)
    return jax.shard_map(
        on_device, mesh=mesh, in_specs=in_specs, out_specs=out_specs, check_vma=False
    )
```

profile of v0, /device:TPU:1, one launch (start us, length us, event | category | flops | bytes accessed | tf_op | source)
XLA Modules:
  0.0 221.4 jit_solution(11025088033426333601)
XLA Ops:
  6.5 3.5 %copy.112 = bf16[128,8,8,128]{3,2,1,0:T(8,128)(2,1)} copy(bf16[128,8,8,128]{3,1,2,0:T(8,128)(2,1)} %bitcast.125) | data formatting | bytes 4194304
  10.1 3.0 %copy.73 = bf16[4,256,8,128]{1,3,2,0:T(8,128)(2,1)S(1)} copy(bf16[4,256,8,128]{3,2,1,0:T(8,128)(2,1)} %bitcast.124) | data formatting | bytes 4194304 | tf_op jit(solution)/shard_map/reshape | solution.py:20
  13.1 3.0 %copy.113 = bf16[128,8,8,128]{3,2,1,0:T(8,128)(2,1)S(1)} copy(bf16[128,8,8,128]{3,1,2,0:T(8,128)(2,1)} %bitcast.126) | data formatting | bytes 4194304
  16.1 2.8 %fusion.93 = (bf16[8,128,128]{2,1,0:T(8,128)(2,1)}, f32[4,8,128,128]{3,2,1,0:T(8,128)}) fusion(bf16[4,256,8,128]{1,3,2,0:T(8,128)(2,1)S(1)} %copy.73, bf16[4,256,8,128]{3,2,1,0:T(8,128)(2,1)S(1)} %bitcast.121), kind=kOutput, calls=%fused_computation.114 | convolution fusion | flops 268828672 | bytes 6553600 | tf_op jit(solution)/shard_map/cshi,cshj->chij/dot_general | solution.py:35
  19.0 2.4 %copy.111 = bf16[128,8,8,128]{3,2,1,0:T(8,128)(2,1)S(1)} copy(bf16[128,8,8,128]{3,1,2,0:T(8,128)(2,1)} %bitcast.127) | data formatting | bytes 4194304
  21.5 0.1 bitcast_reduce_fusion
  21.6 0.7 copy-done.3
  22.3 3.0 %convolution_convert_fusion.1 = bf16[4,8,128,128]{3,0,2,1:T(4,128)(2,1)S(1)} fusion(f32[2,8,128,128]{3,2,1,0:T(8,128)S(1)} %bitcast_reduce_fusion, pred[4]{0:T(512)(128)(4,1)S(1)} %fusion.82, s32[4]{0:T(128)S(1)} %broadcast_add_fusion), kind=kOutput, calls=%fused_computation.35 | convolution fusion | flops 13107216 | bytes 2097172 | tf_op jit(solution)/shard_map/cb,bhij->chij/dot_general | solution.py:49
  25.3 3.3 %fusion.25 = bf16[4,8,128,128]{3,0,2,1:T(4,128)(2,1)S(1)} fusion(f32[4,8,128,128]{3,2,1,0:T(8,128)S(1)} %copy-done.2, s32[4]{0:T(128)S(1)} %iota_add_fusion, pred[4]{0:T(512)(128)(4,1)S(1)} %fusion.81), kind=kOutput, calls=%fused_computation.34 | convolution fusion | flops 25690144 | bytes 3145748 | tf_op jit(solution)/shard_map/cb,bhij->chij/dot_general | solution.py:49
  28.6 2.7 %fusion.28 = f32[4,8,128,256]{3,2,1,0:T(8,128)} fusion(bf16[4,8,128,128]{3,0,2,1:T(4,128)(2,1)S(1)} %convolution_convert_fusion.1, bf16[4,256,8,128]{3,2,1,0:T(8,128)(2,1)S(1)} %bitcast.113), kind=kOutput, calls=%fused_computation.36 | convolution fusion | flops 268435456 | bytes 7340032 | tf_op jit(solution)/shard_map/cthi,chij->cthj/dot_general | solution.py:52
  31.3 2.7 %fusion.31 = f32[4,8,128,256]{3,2,1,0:T(8,128)} fusion(bf16[4,8,128,128]{3,0,2,1:T(4,128)(2,1)S(1)} %fusion.25, bf16[4,256,8,128]{3,2,1,0:T(8,128)(2,1)S(1)} %bitcast.114), kind=kOutput, calls=%fused_computation.39 | convolution fusion | flops 268435456 | bytes 7340032 | tf_op jit(solution)/shard_map/cthi,chij->cthj/dot_general | solution.py:52
  34.0 41.7 %all-gather.3.cloned.1.call-done = bf16[256,128,128]{2,1,0:T(8,128)(2,1)} async-done(((bf16[8,128,128]{2,1,0:T(8,128)(2,1)}), bf16[256,128,128]{2,1,0:T(8,128)(2,1)}) %all-gather.3.cloned.1.call-update) | async-done | bytes 8388624 | tf_op jit(solution)/shard_map/all_gather | solution.py:59
  75.7 8.1 %fusion.19 = bf16[5,8,128,128]{3,0,2,1:T(8,128)(2,1)S(1)} fusion(bf16[32,8,128,128]{3,2,1,0:T(8,128)(2,1)} %bitcast.123, s32[5]{0:T(128)S(1)} %get-tuple-element.24, s32[32]{0:T(128)S(1)} %get-tuple-element.22, s32[32]{0:T(128)S(1)} %get-tuple-element.23, s32[5]{0:T(128)S(1)} %get-tuple-element.25, pred[32]{0:T(512)(128)(4,1)S(1)} %iota_compare_fusion.2), kind=kOutput, calls=%fused_computation.30 | convolution fusion | flops 42599840 | bytes 9699656 | tf_op jit(solution)/shard_map/nl,nhij->lhij/dot_general | solution.py:69
  83.9 2.8 %fusion.91 = (bf16[1,8,128,128]{3,0,2,1:T(2,128)(2,1)S(1)}, bf16[1,8,128,128]{3,0,2,1:T(2,128)(2,1)S(1)}, bf16[1,8,128,128]{3,0,2,1:T(2,128)(2,1)S(1)}, bf16[1,8...) fusion(bf16[5,8,128,128]{3,0,2,1:T(8,128)(2,1)S(1)} %fusion.19), kind=kLoop, calls=%fused_computation.112 | loop fusion | bytes 2621440 | tf_op jit(solution)/shard_map/slice | solution.py:70
  86.7 2.7 %fusion.41 = f32[8,128,4,256]{3,1,0,2:T(8,128)} fusion(bf16[4,256,8,128]{3,2,1,0:T(8,128)(2,1)S(1)} %bitcast.115, bf16[1,8,128,128]{3,0,2,1:T(2,128)(2,1)S(1)} %get-tuple-element.5), kind=kOutput, calls=%fused_computation.49 | convolution fusion | flops 268435456 | bytes 6553600 | tf_op jit(solution)/shard_map/cthi,hij->cthj/dot_general | solution.py:73
  89.4 2.7 %fusion.33 = f32[8,128,4,256]{3,1,0,2:T(8,128)} fusion(bf16[4,256,8,128]{3,2,1,0:T(8,128)(2,1)S(1)} %bitcast.116, bf16[1,8,128,128]{3,0,2,1:T(2,128)(2,1)S(1)} %get-tuple-element.6), kind=kOutput, calls=%fused_computation.41 | convolution fusion | flops 268435456 | bytes 6553600 | tf_op jit(solution)/shard_map/cthi,hij->cthj/dot_general | solution.py:73
  92.1 2.7 %fusion.35 = f32[8,128,4,256]{3,1,0,2:T(8,128)} fusion(bf16[4,256,8,128]{3,2,1,0:T(8,128)(2,1)S(1)} %bitcast.117, bf16[1,8,128,128]{3,0,2,1:T(2,128)(2,1)S(1)} %get-tuple-element.7), kind=kOutput, calls=%fused_computation.43 | convolution fusion | flops 268435456 | bytes 6553600 | tf_op jit(solution)/shard_map/cthi,hij->cthj/dot_general | solution.py:73
  94.8 2.7 %fusion.37 = f32[8,128,4,256]{3,1,0,2:T(8,128)} fusion(bf16[4,256,8,128]{3,2,1,0:T(8,128)(2,1)S(1)} %bitcast.118, bf16[1,8,128,128]{3,0,2,1:T(2,128)(2,1)S(1)} %get-tuple-element.8), kind=kOutput, calls=%fused_computation.45 | convolution fusion | flops 268435456 | bytes 6553600 | tf_op jit(solution)/shard_map/cthi,hij->cthj/dot_general | solution.py:73
  97.5 2.7 %fusion.39 = f32[8,128,4,256]{3,1,0,2:T(8,128)} fusion(bf16[4,256,8,128]{3,2,1,0:T(8,128)(2,1)S(1)} %bitcast.119, bf16[1,8,128,128]{3,0,2,1:T(2,128)(2,1)S(1)} %get-tuple-element.9), kind=kOutput, calls=%fused_computation.47 | convolution fusion | flops 268435456 | bytes 6553600 | tf_op jit(solution)/shard_map/cthi,hij->cthj/dot_general | solution.py:73
  100.3 14.5 %multiply_reduce_fusion = (f32[4,256,8]{1,2,0:T(8,128)S(1)}, f32[4,256,8,128]{1,3,2,0:T(8,128)}) fusion(f32[4,256,8]{1,2,0:T(8,128)S(1)} %bitcast.131, f32[8,128,4,256]{3,1,0,2:T(8,128)} %fusion.33, f32[4,256,8]{1,2,0:T(8,128)S(1)} %bitcast.132, f32[8,128,4,256]{3,1,0,2:T(8,128)} %fusion.35, f32[4,256,8]{1,2,0:T(8,128)S(1)} %bitcast.133, ...), kind=kOutput, calls=%fused_computation.20 | convolution fusion | flops 1096802304 | bytes 40206336 | tf_op jit(solution)/shard_map/chts,cshj->cthj/dot_general | solution.py:32
  114.8 2.7 %multiply_convert_fusion.2 = bf16[4,256,8,128]{1,3,2,0:T(8,128)(2,1)S(1)} fusion(f32[4,256,8,128]{1,3,2,0:T(8,128)} %get-tuple-element.21, f32[4,256,8]{1,2,0:T(8,128)S(1)} %add_rsqrt_fusion), kind=kLoop, calls=%fused_computation.19 | loop fusion | flops 2097152 | bytes 6324224 | tf_op jit(solution)/shard_map/convert_element_type | solution.py:79
  117.5 2.6 %copy.92 = bf16[4,256,8,128]{3,2,1,0:T(8,128)(2,1)} copy(bf16[4,256,8,128]{1,3,2,0:T(8,128)(2,1)S(1)} %multiply_convert_fusion.2) | data formatting | bytes 4194304 | tf_op jit(solution)/shard_map/convert_element_type | solution.py:79
  120.1 14.7 %convolution_convert_fusion = bf16[1024,4096]{1,0:T(8,128)(2,1)} fusion(bf16[1024,4096]{1,0:T(8,128)(2,1)} %param.9, bf16[128,8,8,128]{3,2,1,0:T(8,128)(2,1)} %bitcast.128), kind=kOutput, calls=%fused_computation.3 | convolution fusion | flops 8594128896 | bytes 18874368 | tf_op jit(solution)/shard_map/dot_general | solution.py:81
  134.8 79.8 %reduce-scatter.2.cloned.1.call-done = bf16[256,4096]{1,0:T(8,128)(2,1)} async-done(((bf16[1024,4096]{1,0:T(8,128)(2,1)}), bf16[256,4096]{1,0:T(8,128)(2,1)}) %reduce-scatter.2.cloned.1.call-update) | async-done | bytes 2097168 | tf_op jit(solution)/shard_map/reduce_scatter | solution.py:82
  (21 shorter events, 0.2 us)
Async XLA Ops:
  6.5 69.2 %all-gather.3.cloned.1.call-start = ((), (), s32[]{:S(2)}) async-start(), calls=%async_computation.2 | async-start | bytes 8650752 | tf_op jit(solution)/shard_map/all_gather | solution.py:59
  13.1 3.0 %copy-start = (bf16[4,256,8,128]{1,3,2,0:T(8,128)(2,1)}, bf16[4,256,8,128]{1,3,2,0:T(8,128)(2,1)S(1)}, u32[]{:S(2)}) copy-start(bf16[4,256,8,128]{1,3,2,0:T(8,128)(2,1)S(1)} %copy.73) | copy-start | bytes 6291460
  16.1 2.8 %copy-start.1 = (bf16[128,8,8,128]{3,2,1,0:T(8,128)(2,1)}, bf16[128,8,8,128]{3,2,1,0:T(8,128)(2,1)S(1)}, u32[]{:S(2)}) copy-start(bf16[128,8,8,128]{3,2,1,0:T(8,128)(2,1)S(1)} %copy.113) | copy-start | bytes 6291460
  18.9 195.7 %reduce-scatter.2.cloned.1.call-start = ((), (), s32[]{:S(2)}) async-start(), calls=%async_computation.1 | async-start | bytes 10485760 | tf_op jit(solution)/shard_map/reduce_scatter | solution.py:82
  19.0 2.5 %copy-start.2 = (f32[4,8,128,128]{3,2,1,0:T(8,128)S(1)}, f32[4,8,128,128]{3,2,1,0:T(8,128)}, u32[]{:S(2)}) copy-start(f32[4,8,128,128]{3,2,1,0:T(8,128)} %get-tuple-element.19) | copy-start | bytes 6291460
  21.3 1.0 copy-start.3
Sparse Core Ops, SparseCore 0:
  19.0 56.6 all-gather.2
  134.9 79.5 reduce-scatter.1
where the time goes:
time: 222 us; the launch traced here: 221 us
  waiting for transfers between devices  122 us (55%)
  matrix products  65.4 us (29%)
  local copies, waits for them, and re-layouts  17.9 us (8%)
  between operations  13.6 us (6%)
  other arithmetic  2.92 us (1%)
    reduce_scatter x1, waiting for transfers between devices, on_device(): lax.psum_scatter(lax.optimization_barrier(partial_sum.astype(jnp.bfloat16...  79.8 us
    all_gather x1, waiting for transfers between devices, on_device(): lax.all_gather(device_total[None].astype(jnp.bfloat16), 'ctx', axis=0, ti...  41.7 us
    dot_general x1, matrix products, on_device(): jnp.dot(normed, out_weight, preferred_element_type=jnp.float32)  14.7 us
    dot_general x1, matrix products, on_device(): jnp.einsum('chts,cshj->cthj', weights, value_stretches, preferred_element...  14.5 us
    dot_general x5, matrix products, on_device(): jnp.einsum('cthi,hij->cthj', query_stretches, bucket, preferred_element_t...  13.6 us
    unnamed x11, local copies, waits for them, and re-layouts  9.54 us
    dot_general x1, matrix products, on_device(): jnp.einsum('nl,nhij->lhij', picker, piece, precision=lax.Precision.HIGHEST)  8.12 us
    dot_general x2, matrix products, on_device(): jnp.einsum('cb,bhij->chij', picker, grouped, precision=lax.Precision.HIGH...  6.28 us
  transfers between devices with their start and end apart: 2, of which 2 were waited for; matrix products, arithmetic and copies ran while one was open for 6% of the time, Pallas kernels for 0%

commit v1 on v0

v1 whole, which is shorter than its diff:
```python
import jax
import jax.numpy as jnp
from jax import lax
from jax.experimental import pallas as pl
from jax.experimental.pallas import tpu as pltpu
from jax.sharding import PartitionSpec as P

C = 256
DH = 128
EPS = 1e-06
BF = jnp.bfloat16
F32 = jnp.float32


def state_kernel(k_ref, v_ref, total_ref, local_ref):
    for head in range(2):
        cols = slice(head * DH, (head + 1) * DH)
        states = []
        for stretch in range(4):
            rows = slice(stretch * C, (stretch + 1) * C)
            states.append(
                lax.dot_general(
                    k_ref[rows, cols],
                    v_ref[rows, cols],
                    (((0,), (0,)), ((), ())),
                    preferred_element_type=F32,
                )
            )
        first_two = states[0] + states[1]
        total_ref[head] = (first_two + states[2] + states[3]).astype(BF)
        local_ref[head, 0] = states[0].astype(BF)
        local_ref[head, 1] = states[2].astype(BF)
        local_ref[head, 2] = first_two.astype(BF)


def local_kernel(q_ref, k_ref, v_ref, g_ref, local_ref, out_ref):
    pair = pl.program_id(0)
    rows_ids = lax.broadcasted_iota(jnp.int32, (C, C), 0)
    cols_ids = lax.broadcasted_iota(jnp.int32, (C, C), 1)
    causal = rows_ids >= cols_ids
    for stretch in range(4):
        rows = slice(stretch * C, (stretch + 1) * C)
        for head in range(2):
            cols = slice(head * DH, (head + 1) * DH)
            q = q_ref[rows, cols]
            scores = lax.dot_general(
                q, k_ref[rows, cols], (((1,), (1,)), ((), ())), preferred_element_type=F32
            )
            weights = jnp.where(causal, scores, 0.0).astype(BF)
            gate = lambda level: g_ref[0, rows, head * 8 + level : head * 8 + level + 1]
            out = jnp.dot(weights, v_ref[rows, cols], preferred_element_type=F32) * gate(0)
            parts, states = [], []
            if stretch % 2 == 1:
                parts.append(q * gate(1).astype(BF))
                states.append(local_ref[head, stretch // 2])
            if stretch // 2 == 1:
                parts.append(q * gate(2).astype(BF))
                states.append(local_ref[head, 2])
            if parts:
                out = out + jnp.dot(
                    jnp.concatenate(parts, 1), jnp.concatenate(states, 0), preferred_element_type=F32
                )
            out_ref[rows, cols] = out


def far_kernel(q_ref, comb_ref, g_ref, far_ref, out_ref):
    levels = far_ref.shape[0]
    for stretch in range(4):
        rows = slice(stretch * C, (stretch + 1) * C)
        for head in range(2):
            cols = slice(head * DH, (head + 1) * DH)
            q = q_ref[rows, cols]
            parts = [
                q * g_ref[0, rows, head * 8 + 3 + j : head * 8 + 4 + j].astype(BF)
                for j in range(levels)
            ]
            states = jnp.concatenate([far_ref[j, head] for j in range(levels)], 0)
            out = comb_ref[rows, cols] + jnp.dot(
                jnp.concatenate(parts, 1), states, preferred_element_type=F32
            )
            mean = jnp.mean(out * out, axis=-1, keepdims=True)
            out_ref[rows, cols] = (out * lax.rsqrt(mean + EPS)).astype(BF)


def on_device(query_rows, key_rows, value_rows, level_gate, out_weight):
    tokens, width = query_rows.shape
    levels, heads, _ = level_gate.shape
    ctx_size = lax.axis_size("ctx")
    ctx_bits = ctx_size.bit_length() - 1
    pairs = heads // 2
    me = lax.axis_index("ctx")

    wide = pl.BlockSpec((tokens, 2 * DH), lambda p: (0, p))
    state_shape = lambda *lead: pl.BlockSpec((2, *lead, DH, DH), lambda p: (p,) + (0,) * (len(lead) + 2))
    total, local = pl.pallas_call(
        state_kernel,
        grid=(pairs,),
        in_specs=[wide, wide],
        out_specs=[state_shape(), state_shape(3)],
        out_shape=[
            jax.ShapeDtypeStruct((heads, DH, DH), BF),
            jax.ShapeDtypeStruct((heads, 3, DH, DH), BF),
        ],
        cost_estimate=pl.CostEstimate(flops=2 * tokens * width * DH, bytes_accessed=5 << 20, transcendentals=0),
        compiler_params=pltpu.CompilerParams(vmem_limit_bytes=32 << 20),
        name="states",
    )(key_rows, value_rows)

    far = []
    for bit in range(ctx_bits):
        step = 1 << bit
        got = lax.ppermute(total, "ctx", [(i, i ^ step) for i in range(ctx_size)])
        mine = (me // step) % 2 == 1
        far.append(jnp.where(mine, got, jnp.zeros_like(got)))
        total = (total.astype(F32) + got.astype(F32)).astype(BF)
    far = jnp.stack(far)

    gates = jnp.transpose(level_gate.reshape(levels, pairs, 2, tokens), (1, 3, 2, 0)).reshape(
        pairs, tokens, 2 * levels
    )
    gate_spec = pl.BlockSpec((1, tokens, 2 * levels), lambda p: (p, 0, 0))
    combined = pl.pallas_call(
        local_kernel,
        grid=(pairs,),
        in_specs=[wide, wide, wide, gate_spec, state_shape(3)],
        out_specs=wide,
        out_shape=jax.ShapeDtypeStruct((tokens, width), F32),
        cost_estimate=pl.CostEstimate(flops=12 * tokens * width * DH, bytes_accessed=12 << 20, transcendentals=0),
        compiler_params=pltpu.CompilerParams(vmem_limit_bytes=32 << 20),
        name="local",
    )(query_rows, key_rows, value_rows, gates, local)

    normed = pl.pallas_call(
        far_kernel,
        grid=(pairs,),
        in_specs=[
            wide,
            wide,
            gate_spec,
            pl.BlockSpec((ctx_bits, 2, DH, DH), lambda p: (0, p, 0, 0)),
        ],
        out_specs=wide,
        out_shape=jax.ShapeDtypeStruct((tokens, width), BF),
        cost_estimate=pl.CostEstimate(flops=10 * tokens * width * DH, bytes_accessed=9 << 20, transcendentals=0),
        compiler_params=pltpu.CompilerParams(vmem_limit_bytes=32 << 20),
        name="far_norm",
    )(query_rows, combined, gates, far)

    partial = jnp.dot(normed, out_weight, preferred_element_type=F32).astype(BF)
    return lax.psum_scatter(partial, "head", scatter_dimension=0, tiled=True)


def solution(mesh):
    in_specs = (
        P("ctx", "head"),
        P("ctx", "head"),
        P("ctx", "head"),
        P(None, "head", "ctx"),
        P("head", None),
    )
    out_specs = P(("ctx", "head"), None)
    return jax.shard_map(
        on_device, mesh=mesh, in_specs=in_specs, out_specs=out_specs, check_vma=False
    )
```

time: 222 us -> 167 us (0.75)
  matrix products: 65.4 us -> 10.8 us
  waiting for transfers between devices: 122 us -> 98.9 us
  Pallas kernels: 0 us -> 19.6 us
  starting transfers between devices: 0.04 us -> 10.8 us
  local copies, waits for them, and re-layouts: 17.9 us -> 11 us
    dot_general x13 -> x1, matrix products: 65.4 us -> 10.8 us  [on_device(): partial = jnp.dot(normed, out_weight, preferred_element_type=F32).astype(BF)]
    all_gather x1 -> x0, waiting for transfers between devices: 41.7 us -> none  [on_device(): lax.all_gather(device_total[None].astype(jnp.bfloat16), 'ctx', axis=0, ti...]
    pallas_call x0 -> x3, Pallas kernels: none -> 19.6 us  [the longest x1 10.4 us: on_device(): pl.pallas_call(far_kernel, grid=(pairs,), in_specs=[wide, wide, gate_spec...]
    ppermute x0 -> x5, waiting for transfers between devices: none -> 16.1 us  [on_device(): got = lax.ppermute(total, 'ctx', [(i, i ^ step) for i in range(ctx_size)])]
    ppermute x0 -> x5, starting transfers between devices: none -> 10.8 us  [on_device(): got = lax.ppermute(total, 'ctx', [(i, i ^ step) for i in range(ctx_size)])]
    reduce_scatter x1, waiting for transfers between devices: 79.8 us -> 82.8 us  [on_device(): return lax.psum_scatter(partial, 'head', scatter_dimension=0, tiled=True)]
    slice x2 -> x0, local copies, waits for them, and re-layouts: 2.83 us -> none  [the longest x1 2.82 us: on_device(): far_states = [gathered[level_bit] for level_bit in range(ctx_bits)]]
    convert_element_type x1 -> x0, local copies, waits for them, and re-layouts: 2.57 us -> none  [on_device(): normed = (combined * lax.rsqrt(jnp.mean(combined * combined, axis=-1, kee...]
  transfers between devices with their start and end apart: 2 -> 6, of which waited for: 2 -> 5; matrix products, arithmetic and copies ran while one was open for 6% -> 2% of each run, Pallas kernels for 0% -> 4%
where the time goes in v1:
time: 167 us; the launch traced here: 166 us
  waiting for transfers between devices  98.9 us (59%)
  Pallas kernels  19.6 us (12%)
  between operations  13.5 us (8%)
  local copies, waits for them, and re-layouts  11 us (7%)
  starting transfers between devices  10.8 us (6%)
  matrix products  10.8 us (6%)
    reduce_scatter x1, waiting for transfers between devices, on_device(): return lax.psum_scatter(partial, 'head', scatter_dimension=0, tiled=True)  82.8 us
    ppermute x5, waiting for transfers between devices, on_device(): got = lax.ppermute(total, 'ctx', [(i, i ^ step) for i in range(ctx_size)])  16.1 us
    dot_general x1, matrix products, on_device(): partial = jnp.dot(normed, out_weight, preferred_element_type=F32).astype(BF)  10.8 us
    ppermute x5, starting transfers between devices, on_device(): got = lax.ppermute(total, 'ctx', [(i, i ^ step) for i in range(ctx_size)])  10.8 us
    pallas_call x1, Pallas kernels, on_device(): pl.pallas_call(far_kernel, grid=(pairs,), in_specs=[wide, wide, gate_spec...  10.4 us
    unnamed x21, local copies, waits for them, and re-layouts  9.46 us
    pallas_call x1, Pallas kernels, on_device(): pl.pallas_call(local_kernel, grid=(pairs,), in_specs=[wide, wide, wide, g...  7.23 us
  transfers between devices with their start and end apart: 6, of which 5 were waited for; matrix products, arithmetic and copies ran while one was open for 2% of the time, Pallas kernels for 4%

profile of v1, /device:TPU:1, one launch (start us, length us, event | category | flops | bytes accessed | tf_op | source)
XLA Modules:
  0.0 166.4 jit_solution(13066615211746126597)
XLA Ops:
  6.5 1.6 copy-done
  8.1 1.6 copy-done.2
  9.7 2.0 %states.1 = (bf16[8,128,128]{2,1,0:T(8,128)(2,1)S(1)}, bf16[8,3,128,128]{3,2,1,0:T(8,128)(2,1)S(1)}) custom-call(bf16[1024,1024]{1,0:T(8,128)(2,1)S(1)} %copy-done, bf16[1024,1024]{1,0:T(8,128)(2,1)S(1)} %copy-done.2), custom_call_target="tpu_custom_call" | custom-call | flops 268435456 | bytes 5242880 | tf_op jit(solution)/shard_map/states/pallas_call | solution.py:95
  11.7 1.5 collective-permute-start
  13.2 1.2 collective-permute-done
  14.4 1.8 %collective-permute-start.1 = (bf16[8,128,128]{2,1,0:T(8,128)(2,1)S(1)}, bf16[8,128,128]{2,1,0:T(8,128)(2,1)S(1)}, u32[]{:S(2)}, u32[]{:S(2)}) collective-permute-start(bf16[8,128,128]{2,1,0:T(8,128)(2,1)S(1)} %add_convert_fusion.3), channel_id=1, source_target_pairs={{0,8},{4,12},{8,0},{12,4},{16,24},{20,28},{24,16},{28,20},{32,40},... | collective-permute-start | bytes 786440 | tf_op jit(solution)/shard_map/ppermute | solution.py:112
  16.2 6.3 %collective-permute-done.1 = bf16[8,128,128]{2,1,0:T(8,128)(2,1)S(1)} collective-permute-done((bf16[8,128,128]{2,1,0:T(8,128)(2,1)S(1)}, bf16[8,128,128]{2,1,0:T(8,128)(2,1)S(1)}, u32[]{:S(2)}, u32[]{:S(2)}) %collective-permute-start.1) | collective-permute-done | bytes 262176 | tf_op jit(solution)/shard_map/ppermute | solution.py:112
  22.7 0.6 copy-done.5
  23.3 3.1 %collective-permute-start.2 = (bf16[8,128,128]{2,1,0:T(8,128)(2,1)S(1)}, bf16[8,128,128]{2,1,0:T(8,128)(2,1)}, u32[]{:S(2)}, u32[]{:S(2)}) collective-permute-start(bf16[8,128,128]{2,1,0:T(8,128)(2,1)S(1)} %add_convert_fusion.2), channel_id=1, source_target_pairs={{0,16},{4,20},{8,24},{12,28},{16,0},{20,4},{24,8},{28,12},{32,48},... | collective-permute-start | bytes 786440 | tf_op jit(solution)/shard_map/ppermute | solution.py:112
  26.4 0.9 copy.7
  27.3 1.5 copy.8.g_ref
  28.8 1.6 copy-done.1
  30.4 1.6 copy-done.3
  32.0 1.6 copy-done.4
  33.6 7.2 %local.1.comb_ref = f32[1024,1024]{1,0:T(8,128)S(1)} custom-call(bf16[1024,1024]{1,0:T(8,128)(2,1)S(1)} %copy-done.4, bf16[1024,1024]{1,0:T(8,128)(2,1)S(1)} %copy-done.1, bf16[1024,1024]{1,0:T(8,128)(2,1)S(1)} %copy-done.3, f32[4,1024,16]{2,1,0:T(8,128)S(1)} %copy.8.g_ref, bf16[8,3,128,128]{3,2,1,0:T(8,128)(2,1)S(1)} %get-tuple-element.7.local_ref), custom_call_target="tpu_custom_call" | custom-call | flops 1610612736 | bytes 12582912 | tf_op jit(solution)/shard_map/local/pallas_call | solution.py:122
  40.9 1.0 add_convert_fusion.1
  41.9 1.4 collective-permute-start.3
  43.4 4.9 %collective-permute-done.3 = bf16[8,128,128]{2,1,0:T(8,128)(2,1)S(1)} collective-permute-done((bf16[8,128,128]{2,1,0:T(8,128)(2,1)S(1)}, bf16[8,128,128]{2,1,0:T(8,128)(2,1)S(1)}, u32[]{:S(2)}, u32[]{:S(2)}) %collective-permute-start.3) | collective-permute-done | bytes 262176 | tf_op jit(solution)/shard_map/ppermute | solution.py:112
  48.4 3.0 %collective-permute-start.4 = (bf16[8,128,128]{2,1,0:T(8,128)(2,1)S(1)}, bf16[8,128,128]{2,1,0:T(8,128)(2,1)S(1)}, u32[]{:S(2)}, u32[]{:S(2)}) collective-permute-start(bf16[8,128,128]{2,1,0:T(8,128)(2,1)S(1)} %add_convert_fusion), channel_id=1, source_target_pairs={{0,64},{4,68},{8,72},{12,76},{16,80},{20,84},{24,88},{28,92},{32,9... | collective-permute-start | bytes 786440 | tf_op jit(solution)/shard_map/ppermute | solution.py:112
  51.4 0.1 bitcast_dynamic-update-slice_fusion.2
  51.5 3.7 %collective-permute-done.4 = bf16[8,128,128]{2,1,0:T(8,128)(2,1)S(1)} collective-permute-done((bf16[8,128,128]{2,1,0:T(8,128)(2,1)S(1)}, bf16[8,128,128]{2,1,0:T(8,128)(2,1)S(1)}, u32[]{:S(2)}, u32[]{:S(2)}) %collective-permute-start.4) | collective-permute-done | bytes 262176 | tf_op jit(solution)/shard_map/ppermute | solution.py:112
  55.4 10.4 %far_norm.1 = bf16[1024,1024]{1,0:T(8,128)(2,1)S(1)} custom-call(bf16[1024,1024]{1,0:T(8,128)(2,1)S(1)} %copy-done.4, f32[1024,1024]{1,0:T(8,128)S(1)} %local.1.comb_ref, f32[4,1024,16]{2,1,0:T(8,128)S(1)} %copy.8.g_ref, bf16[5,8,128,128]{3,2,1,0:T(8,128)(2,1)S(1)} %bitcast_dynamic-update-slice_fusion.far_ref), custom_call_target="tpu_custom_call" | custom-call | flops 1342177280 | bytes 9437184 | tf_op jit(solution)/shard_map/far_norm/pallas_call | solution.py:133
  65.9 10.8 %convolution_convert_fusion = bf16[1024,4096]{1,0:T(8,128)(2,1)} fusion(bf16[1024,1024]{1,0:T(8,128)(2,1)S(1)} %far_norm.1, bf16[1024,4096]{1,0:T(8,128)(2,1)S(1)} %bitcast.19), kind=kOutput, calls=%fused_computation | convolution fusion | flops 8594128896 | bytes 18874368 | tf_op jit(solution)/shard_map/dot_general | solution.py:149
  76.7 82.8 %reduce-scatter.2.cloned.1.call-done = bf16[256,4096]{1,0:T(8,128)(2,1)} async-done(((bf16[1024,4096]{1,0:T(8,128)(2,1)}), bf16[256,4096]{1,0:T(8,128)(2,1)}) %reduce-scatter.2.cloned.1.call-update) | async-done | bytes 2097168 | tf_op jit(solution)/shard_map/reduce_scatter | solution.py:150
  (25 shorter events, 0.6 us)
Async XLA Ops:
  6.5 153.0 %reduce-scatter.2.cloned.1.call-start = ((), (), s32[]{:S(2)}) async-start(), calls=%async_computation.1 | async-start | bytes 10485760 | tf_op jit(solution)/shard_map/reduce_scatter | solution.py:150
  6.5 1.6 copy-start
  8.1 1.6 copy-start.2
  9.7 16.7 %copy-start.7 = (f32[8,8,1024]{2,1,0:T(8,128)S(1)}, f32[8,8,1024]{2,1,0:T(8,128)}, u32[]{:S(2)}) copy-start(f32[8,8,1024]{2,1,0:T(8,128)} %param.8) | copy-start | bytes 786436
  11.7 2.7 %collective-permute-start = (bf16[8,128,128]{2,1,0:T(8,128)(2,1)S(1)}, bf16[8,128,128]{2,1,0:T(8,128)(2,1)S(1)}, u32[]{:S(2)}, u32[]{:S(2)}) collective-permute-start(bf16[8,128,128]{2,1,0:T(8,128)(2,1)S(1)} %get-tuple-element.8), channel_id=1, source_target_pairs={{0,4},{4,0},{8,12},{12,8},{16,20},{20,16},{24,28},{28,24},{32,36},... | collective-permute-start | bytes 786440 | tf_op jit(solution)/shard_map/ppermute | solution.py:112
  14.4 8.1 %collective-permute-start.1 = (bf16[8,128,128]{2,1,0:T(8,128)(2,1)S(1)}, bf16[8,128,128]{2,1,0:T(8,128)(2,1)S(1)}, u32[]{:S(2)}, u32[]{:S(2)}) collective-permute-start(bf16[8,128,128]{2,1,0:T(8,128)(2,1)S(1)} %add_convert_fusion.3), channel_id=1, source_target_pairs={{0,8},{4,12},{8,0},{12,4},{16,24},{20,28},{24,16},{28,20},{32,40},... | collective-permute-start | bytes 786440 | tf_op jit(solution)/shard_map/ppermute | solution.py:112
  22.6 0.7 copy-start.5
  23.3 17.6 %collective-permute-start.2 = (bf16[8,128,128]{2,1,0:T(8,128)(2,1)S(1)}, bf16[8,128,128]{2,1,0:T(8,128)(2,1)}, u32[]{:S(2)}, u32[]{:S(2)}) collective-permute-start(bf16[8,128,128]{2,1,0:T(8,128)(2,1)S(1)} %add_convert_fusion.2), channel_id=1, source_target_pairs={{0,16},{4,20},{8,24},{12,28},{16,0},{20,4},{24,8},{28,12},{32,48},... | collective-permute-start | bytes 786440 | tf_op jit(solution)/shard_map/ppermute | solution.py:112
  28.8 1.6 copy-start.1
  30.4 1.6 copy-start.3
  32.0 1.6 copy-start.4
  33.6 9.7 %copy-start.6 = (bf16[8,128,128]{2,1,0:T(8,128)(2,1)S(1)}, bf16[8,128,128]{2,1,0:T(8,128)(2,1)}, u32[]{:S(2)}) copy-start(bf16[8,128,128]{2,1,0:T(8,128)(2,1)} %copy-done.5) | copy-start | bytes 786436
  41.9 6.4 %collective-permute-start.3 = (bf16[8,128,128]{2,1,0:T(8,128)(2,1)S(1)}, bf16[8,128,128]{2,1,0:T(8,128)(2,1)S(1)}, u32[]{:S(2)}, u32[]{:S(2)}) collective-permute-start(bf16[8,128,128]{2,1,0:T(8,128)(2,1)S(1)} %add_convert_fusion.1), channel_id=1, source_target_pairs={{0,32},{4,36},{8,40},{12,44},{16,48},{20,52},{24,56},{28,60},{32,0... | collective-permute-start | bytes 786440 | tf_op jit(solution)/shard_map/ppermute | solution.py:112
  43.3 22.6 %slice-start = ((s8[8388608]{0:T(1024)(128)(4,1)}), s8[4194304]{0:T(1024)(128)(4,1)S(1)}, s32[]{:S(2)}) async-start(s8[8388608]{0:T(1024)(128)(4,1)} %bitcast.18), calls=%async_computation.2 | async-start | bytes 8388608
  48.4 6.9 %collective-permute-start.4 = (bf16[8,128,128]{2,1,0:T(8,128)(2,1)S(1)}, bf16[8,128,128]{2,1,0:T(8,128)(2,1)S(1)}, u32[]{:S(2)}, u32[]{:S(2)}) collective-permute-start(bf16[8,128,128]{2,1,0:T(8,128)(2,1)S(1)} %add_convert_fusion), channel_id=1, source_target_pairs={{0,64},{4,68},{8,72},{12,76},{16,80},{20,84},{24,88},{28,92},{32,9... | collective-permute-start | bytes 786440 | tf_op jit(solution)/shard_map/ppermute | solution.py:112
  55.4 10.5 %slice-start.1 = ((s8[8388608]{0:T(1024)(128)(4,1)}), s8[4194304]{0:T(1024)(128)(4,1)S(1)}, s32[]{:S(2)}) async-start(s8[8388608]{0:T(1024)(128)(4,1)} %bitcast.18), calls=%async_computation.3 | async-start | bytes 8388608
Sparse Core Ops, SparseCore 0:
  76.8 82.6 reduce-scatter.1

commit v2 on v1

v2 whole, which is shorter than its diff:
```python
import jax
import jax.numpy as jnp
from jax import lax
from jax.experimental import pallas as pl
from jax.experimental.pallas import tpu as pltpu
from jax.sharding import PartitionSpec as P

C = 256
DH = 128
EPS = 1e-06
BF = jnp.bfloat16
F32 = jnp.float32
VMEM_LIMIT = 56 << 20
CHUNKS = 4


def dot_t(a, b):
    return lax.dot_general(a, b, (((1,), (1,)), ((), ())), preferred_element_type=F32)


def dot_tt(a, b):
    return lax.dot_general(a, b, (((0,), (0,)), ((), ())), preferred_element_type=F32)


def params():
    return pltpu.CompilerParams(vmem_limit_bytes=VMEM_LIMIT)


def cost(flops, nbytes):
    return pl.CostEstimate(flops=flops, bytes_accessed=nbytes, transcendentals=0)


def state_kernel(k_ref, v_ref, total_ref, local_ref):
    for head in range(2):
        cols = slice(head * DH, (head + 1) * DH)
        states = []
        for stretch in range(4):
            rows = slice(stretch * C, (stretch + 1) * C)
            states.append(dot_tt(v_ref[rows, cols], k_ref[rows, cols]))
        first_two = states[0] + states[1]
        total_ref[head] = (first_two + states[2] + states[3]).astype(BF)
        local_ref[head, 0] = states[0].astype(BF)
        local_ref[head, 1] = states[2].astype(BF)
        local_ref[head, 2] = first_two.astype(BF)


def local_kernel(q_ref, k_ref, v_ref, g_ref, local_ref, out_ref):
    pair = pl.program_id(0)
    causal = lax.broadcasted_iota(jnp.int32, (C, C), 0) <= lax.broadcasted_iota(
        jnp.int32, (C, C), 1
    )
    for stretch in range(4):
        rows = slice(stretch * C, (stretch + 1) * C)
        for head in range(2):
            cols = slice(head * DH, (head + 1) * DH)
            q = q_ref[rows, cols]
            gate = lambda level: g_ref[level, pl.ds(2 * pair + head, 1), rows]
            weights = jnp.where(causal, dot_t(k_ref[rows, cols], q), 0.0).astype(BF)
            out = dot_tt(v_ref[rows, cols], weights) * gate(0)
            if stretch % 2 == 1:
                out = out + dot_t(local_ref[head, stretch // 2], q) * gate(1)
            if stretch // 2 == 1:
                out = out + dot_t(local_ref[head, 2], q) * gate(2)
            out_ref[cols, rows] = out


def far_kernel(s_ref, q_ref, comb_ref, g_ref, sib_ref, zo_ref, zs_ref, yo_ref, ys_ref, out_ref):
    core = s_ref[0]
    masks = [s_ref[1 + j].astype(F32) for j in range(5)]
    for slot in range(8):
        own = slot < 4
        inner = slot % 4
        head = (core if own else 1 - core) * 4 + inner
        z_ref, y_ref = (zo_ref, yo_ref) if own else (zs_ref, ys_ref)
        offset = pl.multiple_of(head * DH, DH)
        q = q_ref[:, pl.ds(offset, DH)]
        out = comb_ref[pl.ds(offset, DH), :]
        states = [sib_ref[head], z_ref[0, inner], z_ref[1, inner], y_ref[0, inner], y_ref[1, inner]]
        for j in range(5):
            out = out + dot_t(states[j], q) * (g_ref[3 + j, pl.ds(head, 1), :] * masks[j])
        mean = jnp.mean(out * out, axis=0, keepdims=True)
        out_ref[0, :, pl.ds(offset, DH)] = jnp.transpose(out * lax.rsqrt(mean + EPS)).astype(BF)


def proj_kernel(s_ref, own_ref, got_ref, w_ref, a_ref, b_ref, c_ref, d_ref, out_ref):
    acc = jnp.dot(own_ref[0], w_ref[...], preferred_element_type=F32)
    for piece, ref in enumerate((a_ref, b_ref, c_ref, d_ref)):
        cols = pl.ds(pl.multiple_of(s_ref[piece] * 256, 256), 256)
        acc = acc + jnp.dot(got_ref[0, :, cols], ref[...], preferred_element_type=F32)
    out_ref[...] = acc.astype(out_ref.dtype)


def on_device(query_rows, key_rows, value_rows, level_gate, out_weight):
    tokens, width = query_rows.shape
    levels, heads, _ = level_gate.shape
    model = out_weight.shape[1]
    pairs = heads // 2
    ctx_size = lax.axis_size("ctx")
    me = lax.axis_index("ctx")
    x = lax.axis_index("head")
    bit = lambda j: lax.bitwise_and(lax.shift_right_logical(me, j), 1)
    core = bit(0)

    def ctx_swap(array, step):
        return lax.ppermute(array, "ctx", [(i, i ^ step) for i in range(ctx_size)])

    def near(array):
        return lax.ppermute(array, "head", [(i, i ^ 1) for i in range(4)])

    def across(array):
        return lax.ppermute(array, "head", [(i, 3 - i) for i in range(4)])

    chunk = model // CHUNKS
    pieces, orders = [], []
    for i in range(CHUNKS):
        step_bit = 1 if i % 2 == 0 else 3
        quarter = core * 2 + bit(step_bit)
        other = core * 2 + 1 - bit(step_bit)
        mine = near(lax.dynamic_slice(out_weight, (quarter * 256, i * chunk), (256, chunk)))
        next_one = ctx_swap(mine, 1 << step_bit)
        pieces.append((mine, next_one, ctx_swap(mine, 1), ctx_swap(next_one, 1)))
        flip = lambda part: lax.bitwise_xor(part, 2)
        orders.append(jnp.stack([quarter, other, flip(quarter), flip(other)]).astype(jnp.int32))

    wide = pl.BlockSpec((tokens, 2 * DH), lambda p: (0, p))
    total, local = pl.pallas_call(
        state_kernel,
        grid=(pairs,),
        in_specs=[wide, wide],
        out_specs=[
            pl.BlockSpec((2, DH, DH), lambda p: (p, 0, 0)),
            pl.BlockSpec((2, 3, DH, DH), lambda p: (p, 0, 0, 0)),
        ],
        out_shape=[
            jax.ShapeDtypeStruct((heads, DH, DH), BF),
            jax.ShapeDtypeStruct((heads, 3, DH, DH), BF),
        ],
        cost_estimate=cost(2 * tokens * width * DH, 5 << 20),
        compiler_params=params(),
        name="states",
    )(key_rows, value_rows)

    half = heads // 2
    pick = lambda array: lax.dynamic_slice_in_dim(array, core * half, half, 0)
    add = lambda *arrays: sum(a.astype(F32) for a in arrays)
    sibling = ctx_swap(total, 1)
    chip = add(pick(total), pick(sibling)).astype(BF)
    z1, z2, z3 = (ctx_swap(chip, step) for step in (2, 4, 6))
    z_own = jnp.stack([z1, add(z2, z3).astype(BF)])
    row = add(chip, z1, z2, z3).astype(BF)
    y1, y2, y3 = (ctx_swap(row, step) for step in (8, 16, 24))
    z_sib = ctx_swap(z_own, 1)
    y_own = jnp.stack([y1, add(y2, y3).astype(BF)])
    y_sib = ctx_swap(y_own, 1)

    combined = pl.pallas_call(
        local_kernel,
        grid=(pairs,),
        in_specs=[
            wide,
            wide,
            wide,
            pl.BlockSpec((levels, heads, tokens), lambda p: (0, 0, 0)),
            pl.BlockSpec((2, 3, DH, DH), lambda p: (p, 0, 0, 0)),
        ],
        out_specs=pl.BlockSpec((2 * DH, tokens), lambda p: (p, 0)),
        out_shape=jax.ShapeDtypeStruct((width, tokens), F32),
        cost_estimate=cost(12 * tokens * width * DH, 12 << 20),
        compiler_params=params(),
        name="local",
    )(query_rows, key_rows, value_rows, level_gate, local)

    def far_norm(blocks, name):
        count = len(blocks)
        scalars = jnp.stack([core] + [bit(j) for j in range(5)] + list(blocks)).astype(jnp.int32)
        full = lambda *shape: pl.BlockSpec(shape, lambda i, s: (0,) * len(shape))
        return pl.pallas_call(
            far_kernel,
            grid_spec=pltpu.PrefetchScalarGridSpec(
                num_scalar_prefetch=1,
                grid=(count,),
                in_specs=[
                    pl.BlockSpec((C, width), lambda i, s: (s[6 + i], 0)),
                    pl.BlockSpec((width, C), lambda i, s: (0, s[6 + i])),
                    pl.BlockSpec((levels, heads, C), lambda i, s: (0, 0, s[6 + i])),
                    full(heads, DH, DH),
                    full(2, half, DH, DH),
                    full(2, half, DH, DH),
                    full(2, half, DH, DH),
                    full(2, half, DH, DH),
                ],
                out_specs=pl.BlockSpec((1, C, width), lambda i, s: (i, 0, 0)),
            ),
            out_shape=jax.ShapeDtypeStruct((count, C, width), BF),
            cost_estimate=cost(10 * count * C * width * DH, count * (2 << 20)),
            compiler_params=params(),
            name=name,
        )(scalars, query_rows, combined, level_gate, sibling, z_own, z_sib, y_own, y_sib)

    near_x = lax.bitwise_xor(x, 1)
    across_x = 3 - x
    far_x = lax.bitwise_xor(x, 2)
    first = far_norm([far_x], "far_first")
    got_across = near(first)
    rest = far_norm([across_x, near_x, x], "far_rest")
    got_own = near(rest[1:2])

    tile = 256
    tiles = chunk // tile

    def project(own_index, got, i, dtype, name):
        piece = pl.BlockSpec((256, tile), lambda n, s: (0, n))
        return pl.pallas_call(
            proj_kernel,
            grid_spec=pltpu.PrefetchScalarGridSpec(
                num_scalar_prefetch=1,
                grid=(tiles,),
                in_specs=[
                    pl.BlockSpec((1, C, width), lambda n, s: (own_index, 0, 0)),
                    pl.BlockSpec((1, C, width), lambda n, s: (0, 0, 0)),
                    pl.BlockSpec((width, tile), lambda n, s: (0, i * tiles + n)),
                    piece,
                    piece,
                    piece,
                    piece,
                ],
                out_specs=pl.BlockSpec((C, tile), lambda n, s: (0, n)),
            ),
            out_shape=jax.ShapeDtypeStruct((C, chunk), dtype),
            cost_estimate=cost(4 * C * width * chunk, 5 << 20),
            compiler_params=params(),
            name=name,
        )(orders[i], rest, got, out_weight, *pieces[i])

    received = []
    for i in range(CHUNKS):
        received.append(across(project(0, got_across, i, BF, "proj_across%d" % i)))
    outs = []
    for i in range(CHUNKS):
        own = project(2, got_own, i, F32, "proj_own%d" % i)
        outs.append((own + received[i].astype(F32)).astype(BF))
    return jnp.concatenate(outs, 1)


def solution(mesh):
    in_specs = (
        P("ctx", "head"),
        P("ctx", "head"),
        P("ctx", "head"),
        P(None, "head", "ctx"),
        P("head", None),
    )
    out_specs = P(("ctx", "head"), None)
    return jax.shard_map(
        on_device, mesh=mesh, in_specs=in_specs, out_specs=out_specs, check_vma=False
    )
```

time: 167 us -> 162 us (0.970)
  waiting for transfers between devices: 98.9 us -> 39 us
  Pallas kernels: 19.6 us -> 73 us
  starting transfers between devices: 10.8 us -> 36.8 us
  between operations: 13.5 us -> 0.26 us
  matrix products: 10.8 us -> 0 us
  local copies, waits for them, and re-layouts: 11 us -> 7.41 us
  other arithmetic: 1.63 us -> 4.5 us
    reduce_scatter x1 -> x0, waiting for transfers between devices: 82.8 us -> none  [on_device(): return lax.psum_scatter(partial, 'head', scatter_dimension=0, tiled=True)]
    pallas_call x2 -> x11, Pallas kernels: 17.7 us -> 68.5 us  [the longest x8 47.9 us: project(): pl.pallas_call(proj_kernel, grid_spec=pltpu.PrefetchScalarGridSpec(num_sc...]
    ppermute x5 -> x31, starting transfers between devices: 10.8 us -> 36.8 us  [the longest x21 24.8 us: ctx_swap(): return lax.ppermute(array, 'ctx', [(i, i ^ step) for i in range(ctx_size)])]
    ppermute x5 -> x31, waiting for transfers between devices: 16.1 us -> 39 us  [the longest x6 18.8 us: near(): return lax.ppermute(array, 'head', [(i, i ^ 1) for i in range(4)])]
    dot_general x1 -> x0, matrix products: 10.8 us -> none  [on_device(): partial = jnp.dot(normed, out_weight, preferred_element_type=F32).astype(BF)]
    unnamed x21 -> x40, local copies, waits for them, and re-layouts: 9.46 us -> 2.55 us
    pallas_call x1, Pallas kernels: 1.97 us -> 4.52 us  [on_device(): pl.pallas_call(state_kernel, grid=(pairs,), in_specs=[wide, wide], out_sp...]
    slice x0 -> x1, local copies, waits for them, and re-layouts: none -> 1.88 us  [on_device(): got_own = near(rest[1:2])]
  transfers between devices with their start and end apart: 6 -> 31, of which waited for: 5 -> 10; matrix products, arithmetic and copies ran while one was open for 2% -> 4% of each run, Pallas kernels for 4% -> 43%
where the time goes in v2:
time: 162 us; the launch traced here: 161 us
  Pallas kernels  73 us (45%)
  waiting for transfers between devices  39 us (24%)
  starting transfers between devices  36.8 us (23%)
  local copies, waits for them, and re-layouts  7.41 us (5%)
  other arithmetic  4.5 us (3%)
    pallas_call x8, Pallas kernels, project(): pl.pallas_call(proj_kernel, grid_spec=pltpu.PrefetchScalarGridSpec(num_sc...  47.9 us
    ppermute x21, starting transfers between devices, ctx_swap(): return lax.ppermute(array, 'ctx', [(i, i ^ step) for i in range(ctx_size)])  24.8 us
    ppermute x6, waiting for transfers between devices, near(): return lax.ppermute(array, 'head', [(i, i ^ 1) for i in range(4)])  18.8 us
    ppermute x21, waiting for transfers between devices, ctx_swap(): return lax.ppermute(array, 'ctx', [(i, i ^ step) for i in range(ctx_size)])  15.3 us
    pallas_call x2, Pallas kernels, far_norm(): pl.pallas_call(far_kernel, grid_spec=pltpu.PrefetchScalarGridSpec(num_sca...  11.6 us
    pallas_call x1, Pallas kernels, on_device(): pl.pallas_call(local_kernel, grid=(pairs,), in_specs=[wide, wide, wide, p...  8.97 us
    ppermute x6, starting transfers between devices, near(): return lax.ppermute(array, 'head', [(i, i ^ 1) for i in range(4)])  6.43 us
    ppermute x4, starting transfers between devices, across(): return lax.ppermute(array, 'head', [(i, 3 - i) for i in range(4)])  5.51 us
  transfers between devices with their start and end apart: 31, of which 10 were waited for; matrix products, arithmetic and copies ran while one was open for 4% of the time, Pallas kernels for 43%

profile of v2, /device:TPU:1, one launch (start us, length us, event | category | flops | bytes accessed | tf_op | source)
XLA Modules:
  0.0 160.9 jit_solution(4692326639614611320)
XLA Ops:
  0.0 4.5 %states.1 = (bf16[8,128,128]{2,1,0:T(8,128)(2,1)}, bf16[8,3,128,128]{3,2,1,0:T(8,128)(2,1)}) custom-call(bf16[1024,1024]{1,0:T(8,128)(2,1)} %k_ref.3, bf16[1024,1024]{1,0:T(8,128)(2,1)} %v_ref.3), custom_call_target="tpu_custom_call" | custom-call | flops 268435456 | bytes 5242880 | tf_op jit(solution)/shard_map/states/pallas_call | solution.py:126
  10.2 3.3 %collective-permute-start.2 = (bf16[4,128,128]{2,1,0:T(8,128)(2,1)S(1)}, bf16[4,128,128]{2,1,0:T(8,128)(2,1)S(1)}, u32[]{:S(2)}, u32[]{:S(2)}) collective-permute-start(bf16[4,128,128]{2,1,0:T(8,128)(2,1)S(1)} %add_convert_fusion.5), channel_id=1, source_target_pairs={{0,16},{4,20},{8,24},{12,28},{16,0},{20,4},{24,8},{28,12},{32,48},... | collective-permute-start | bytes 393224 | tf_op jit(solution)/shard_map/ppermute | solution.py:105
  16.5 3.1 %collective-permute-done.2 = bf16[4,128,128]{2,1,0:T(8,128)(2,1)S(1)} collective-permute-done((bf16[4,128,128]{2,1,0:T(8,128)(2,1)S(1)}, bf16[4,128,128]{2,1,0:T(8,128)(2,1)S(1)}, u32[]{:S(2)}, u32[]{:S(2)}) %collective-permute-start.2) | collective-permute-done | bytes 131104 | tf_op jit(solution)/shard_map/ppermute | solution.py:105
  19.6 2.5 %collective-permute-done.3 = bf16[4,128,128]{2,1,0:T(8,128)(2,1)S(1)} collective-permute-done((bf16[4,128,128]{2,1,0:T(8,128)(2,1)S(1)}, bf16[4,128,128]{2,1,0:T(8,128)(2,1)S(1)}, u32[]{:S(2)}, u32[]{:S(2)}) %collective-permute-start.3) | collective-permute-done | bytes 131104 | tf_op jit(solution)/shard_map/ppermute | solution.py:105
  22.1 3.0 %collective-permute-start.6 = (bf16[4,128,128]{2,1,0:T(8,128)(2,1)S(1)}, bf16[4,128,128]{2,1,0:T(8,128)(2,1)S(1)}, u32[]{:S(2)}, u32[]{:S(2)}) collective-permute-start(bf16[4,128,128]{2,1,0:T(8,128)(2,1)S(1)} %get-tuple-element.13), channel_id=1, source_target_pairs={{0,64},{4,68},{8,72},{12,76},{16,80},{20,84},{24,88},{28,92},{32,9... | collective-permute-start | bytes 393224 | tf_op jit(solution)/shard_map/ppermute | solution.py:105
  27.8 2.4 %collective-permute-start.7 = (bf16[4,128,128]{2,1,0:T(8,128)(2,1)S(1)}, bf16[4,128,128]{2,1,0:T(8,128)(2,1)S(1)}, u32[]{:S(2)}, u32[]{:S(2)}) collective-permute-start(bf16[4,128,128]{2,1,0:T(8,128)(2,1)S(1)} %get-tuple-element.13), channel_id=1, source_target_pairs={{0,96},{4,100},{8,104},{12,108},{16,112},{20,116},{24,120},{28,124... | collective-permute-start | bytes 393224 | tf_op jit(solution)/shard_map/ppermute | solution.py:105
  30.3 2.6 %collective-permute-done.7 = bf16[4,128,128]{2,1,0:T(8,128)(2,1)S(1)} collective-permute-done((bf16[4,128,128]{2,1,0:T(8,128)(2,1)S(1)}, bf16[4,128,128]{2,1,0:T(8,128)(2,1)S(1)}, u32[]{:S(2)}, u32[]{:S(2)}) %collective-permute-start.7) | collective-permute-done | bytes 131104 | tf_op jit(solution)/shard_map/ppermute | solution.py:105
  33.0 4.0 %collective-permute-done.5 = bf16[4,128,128]{2,1,0:T(8,128)(2,1)S(1)} collective-permute-done((bf16[4,128,128]{2,1,0:T(8,128)(2,1)S(1)}, bf16[4,128,128]{2,1,0:T(8,128)(2,1)S(1)}, u32[]{:S(2)}, u32[]{:S(2)}) %collective-permute-start.5) | collective-permute-done | bytes 131104 | tf_op jit(solution)/shard_map/ppermute | solution.py:105
  37.0 4.1 %collective-permute-start.4 = (bf16[2,4,128,128]{3,2,1,0:T(8,128)(2,1)S(1)}, bf16[2,4,128,128]{3,2,1,0:T(8,128)(2,1)S(1)}, u32[]{:S(2)}, u32[]{:S(2)}) collective-permute-start(bf16[2,4,128,128]{3,2,1,0:T(8,128)(2,1)S(1)} %pad_maximum_fusion.1.zo_ref), channel_id=1, source_target_pairs={{0,4},{4,0},{8,12},{12,8},{16,20},{20,16},{24,28},{28,24},{32,36},... | collective-permute-start | bytes 786440 | tf_op jit(solution)/shard_map/ppermute | solution.py:105
  42.2 8.2 %collective-permute-done.21.a_ref = bf16[256,1024]{1,0:T(8,128)(2,1)S(1)} collective-permute-done((bf16[256,1024]{1,0:T(8,128)(2,1)S(1)}, bf16[256,1024]{1,0:T(8,128)(2,1)S(1)}, u32[]{:S(2)}, u32[]{:S(2)}) %collective-permute-start.21) | collective-permute-done | bytes 524320 | tf_op jit(solution)/shard_map/ppermute | solution.py:108
  51.6 10.2 %collective-permute-done.26.a_ref = bf16[256,1024]{1,0:T(8,128)(2,1)S(1)} collective-permute-done((bf16[256,1024]{1,0:T(8,128)(2,1)S(1)}, bf16[256,1024]{1,0:T(8,128)(2,1)S(1)}, u32[]{:S(2)}, u32[]{:S(2)}) %collective-permute-start.26) | collective-permute-done | bytes 524320 | tf_op jit(solution)/shard_map/ppermute | solution.py:108
  67.4 9.0 %local.1.comb_ref = f32[1024,1024]{1,0:T(8,128)} custom-call(bf16[1024,1024]{1,0:T(8,128)(2,1)} %q_ref.5, bf16[1024,1024]{1,0:T(8,128)(2,1)} %k_ref.3, bf16[1024,1024]{1,0:T(8,128)(2,1)} %v_ref.3, f32[8,8,1024]{2,1,0:T(8,128)} %g_ref.5, bf16[8,3,128,128]{3,2,1,0:T(8,128)(2,1)} %get-tuple-element.7.local_ref), custom_call_target="tpu_custom_call" | custom-call | flops 1610612736 | bytes 12582912 | tf_op jit(solution)/shard_map/local/pallas_call | solution.py:156
  77.0 4.4 %far_first.1 = bf16[1,256,1024]{2,1,0:T(8,128)(2,1)} custom-call(s32[7]{0:T(128)} %stack.119.s_ref, bf16[1024,1024]{1,0:T(8,128)(2,1)} %q_ref.5, f32[1024,1024]{1,0:T(8,128)} %local.1.comb_ref, f32[8,8,1024]{2,1,0:T(8,128)} %g_ref.5, bf16[8,128,128]{2,1,0:T(8,128)(2,1)} %copy-done.16, bf16[2,4,128,128]{3,2,1,0:T(8,128)(2,1)} %copy-done.6, ...), custom_call_target="tpu_custom_call" | custom-call | flops 335544320 | bytes 2097152 | tf_op jit(solution)/shard_map/far_first/pallas_call | solution.py:177
  84.9 7.2 %far_rest.1.own_ref = bf16[3,256,1024]{2,1,0:T(8,128)(2,1)} custom-call(s32[9]{0:T(128)} %stack.111.s_ref, bf16[1024,1024]{1,0:T(8,128)(2,1)} %q_ref.5, f32[1024,1024]{1,0:T(8,128)} %local.1.comb_ref, f32[8,8,1024]{2,1,0:T(8,128)} %g_ref.5, bf16[8,128,128]{2,1,0:T(8,128)(2,1)} %copy-done.16, bf16[2,4,128,128]{3,2,1,0:T(8,128)(2,1)} %copy-done.6, ...), custom_call_target="tpu_custom_call" | custom-call | flops 1006632960 | bytes 6291456 | tf_op jit(solution)/shard_map/far_rest/pallas_call | solution.py:177
  98.8 6.1 %proj_across0.1 = bf16[256,1024]{1,0:T(8,128)(2,1)} custom-call(s32[4]{0:T(128)} %pad_add_fusion.s_ref, bf16[3,256,1024]{2,1,0:T(8,128)(2,1)} %far_rest.1.own_ref, bf16[1,256,1024]{2,1,0:T(8,128)(2,1)} %copy-done, bf16[1024,4096]{1,0:T(8,128)(2,1)} %w_ref.15, bf16[256,1024]{1,0:T(8,128)(2,1)} %copy-done.8, bf16[256,1024]{1,0:T(8,128)(2,1)} %copy-done.12, ...), custom_call_target="tpu_custom_call" | custom-call | flops 1073741824 | bytes 5242880 | tf_op jit(solution)/shard_map/proj_across0/pallas_call | solution.py:213
  104.9 6.0 %proj_across1.1 = bf16[256,1024]{1,0:T(8,128)(2,1)} custom-call(s32[4]{0:T(128)} %pad_add_fusion.1.s_ref, bf16[3,256,1024]{2,1,0:T(8,128)(2,1)} %far_rest.1.own_ref, bf16[1,256,1024]{2,1,0:T(8,128)(2,1)} %copy-done, bf16[1024,4096]{1,0:T(8,128)(2,1)} %w_ref.15, bf16[256,1024]{1,0:T(8,128)(2,1)} %copy-done.11, ...), custom_call_target="tpu_custom_call" | custom-call | flops 1073741824 | bytes 5242880 | tf_op jit(solution)/shard_map/proj_across1/pallas_call | solution.py:213
  110.9 1.9 %collective-permute-start.15 = (bf16[256,1024]{1,0:T(8,128)(2,1)S(1)}, bf16[256,1024]{1,0:T(8,128)(2,1)S(1)}, u32[]{:S(2)}, u32[]{:S(2)}) collective-permute-start(bf16[256,1024]{1,0:T(8,128)(2,1)S(1)} %copy-done.19), channel_id=1, source_target_pairs={{0,3},{1,2},{2,1},{3,0},{4,7},{5,6},{6,5},{7,4},{8,11},{9,10},{10,... | collective-permute-start | bytes 1572872 | tf_op jit(solution)/shard_map/ppermute | solution.py:111
  113.7 5.8 %proj_across2.1 = bf16[256,1024]{1,0:T(8,128)(2,1)} custom-call(s32[4]{0:T(128)} %pad_add_fusion.s_ref, bf16[3,256,1024]{2,1,0:T(8,128)(2,1)} %far_rest.1.own_ref, bf16[1,256,1024]{2,1,0:T(8,128)(2,1)} %copy-done, bf16[1024,4096]{1,0:T(8,128)(2,1)} %w_ref.15, bf16[256,1024]{1,0:T(8,128)(2,1)} %copy-done.10, bf16[256,1024]{1,0:T(8,128)(2,1)} %collective-permute-done.22.b_ref, ...), custom_call_target="tpu_custom_call" | custom-call | flops 1073741824 | bytes 5242880 | tf_op jit(solution)/shard_map/proj_across2/pallas_call | solution.py:213
  121.4 5.9 %proj_across3.1 = bf16[256,1024]{1,0:T(8,128)(2,1)} custom-call(s32[4]{0:T(128)} %pad_add_fusion.1.s_ref, bf16[3,256,1024]{2,1,0:T(8,128)(2,1)} %far_rest.1.own_ref, bf16[1,256,1024]{2,1,0:T(8,128)(2,1)} %copy-done, bf16[1024,4096]{1,0:T(8,128)(2,1)} %w_ref.15, bf16[256,1024]{1,0:T(8,128)(2,1)} %copy-done.9, ...), custom_call_target="tpu_custom_call" | custom-call | flops 1073741824 | bytes 5242880 | tf_op jit(solution)/shard_map/proj_across3/pallas_call | solution.py:213
  129.0 6.0 %proj_own0.1 = f32[256,1024]{1,0:T(8,128)} custom-call(s32[4]{0:T(128)} %pad_add_fusion.s_ref, bf16[3,256,1024]{2,1,0:T(8,128)(2,1)} %far_rest.1.own_ref, bf16[1,256,1024]{2,1,0:T(8,128)(2,1)} %copy-done.1, bf16[1024,4096]{1,0:T(8,128)(2,1)} %w_ref.15, bf16[256,1024]{1,0:T(8,128)(2,1)} %copy-done.8, bf16[256,1024]{1,0:T(8,128)(2,1)} %copy-done.12, ...), custom_call_target="tpu_custom_call" | custom-call | flops 1073741824 | bytes 5242880 | tf_op jit(solution)/shard_map/proj_own0/pallas_call | solution.py:213
  135.0 6.0 %proj_own1.1 = f32[256,1024]{1,0:T(8,128)} custom-call(s32[4]{0:T(128)} %pad_add_fusion.1.s_ref, bf16[3,256,1024]{2,1,0:T(8,128)(2,1)} %far_rest.1.own_ref, bf16[1,256,1024]{2,1,0:T(8,128)(2,1)} %copy-done.1, bf16[1024,4096]{1,0:T(8,128)(2,1)} %w_ref.15, bf16[256,1024]{1,0:T(8,128)(2,1)} %copy-done.11, bf16[256,1024]{1,0:T(8,128)(2,1)} %collective-permute-done.17.b_ref, ...), custom_call_target="tpu_custom_call" | custom-call | flops 1073741824 | bytes 5242880 | tf_op jit(solution)/shard_map/proj_own1/pallas_call | solution.py:213
  140.9 6.0 %proj_own2.1 = f32[256,1024]{1,0:T(8,128)} custom-call(s32[4]{0:T(128)} %pad_add_fusion.s_ref, bf16[3,256,1024]{2,1,0:T(8,128)(2,1)} %far_rest.1.own_ref, bf16[1,256,1024]{2,1,0:T(8,128)(2,1)} %copy-done.1, bf16[1024,4096]{1,0:T(8,128)(2,1)} %w_ref.15, bf16[256,1024]{1,0:T(8,128)(2,1)} %copy-done.10, bf16[256,1024]{1,0:T(8,128)(2,1)} %collective-permute-done.22.b_ref, ...), custom_call_target="tpu_custom_call" | custom-call | flops 1073741824 | bytes 5242880 | tf_op jit(solution)/shard_map/proj_own2/pallas_call | solution.py:213
  146.9 6.1 %proj_own3.1 = f32[256,1024]{1,0:T(8,128)} custom-call(s32[4]{0:T(128)} %pad_add_fusion.1.s_ref, bf16[3,256,1024]{2,1,0:T(8,128)(2,1)} %far_rest.1.own_ref, bf16[1,256,1024]{2,1,0:T(8,128)(2,1)} %copy-done.1, bf16[1024,4096]{1,0:T(8,128)(2,1)} %w_ref.15, bf16[256,1024]{1,0:T(8,128)(2,1)} %copy-done.9, bf16[256,1024]{1,0:T(8,128)(2,1)} %collective-permute-done.27.b_ref, ...), custom_call_target="tpu_custom_call" | custom-call | flops 1073741824 | bytes 5242880 | tf_op jit(solution)/shard_map/proj_own3/pallas_call | solution.py:213
  154.4 4.9 %collective-permute-done.30 = bf16[256,1024]{1,0:T(8,128)(2,1)S(1)} collective-permute-done((bf16[256,1024]{1,0:T(8,128)(2,1)}, bf16[256,1024]{1,0:T(8,128)(2,1)S(1)}, u32[]{:S(2)}, u32[]{:S(2)}) %collective-permute-start.30) | collective-permute-done | bytes 524320 | tf_op jit(solution)/shard_map/ppermute | solution.py:111
  (106 shorter events, 37.6 us)
Async XLA Ops:
  10.2 9.4 %collective-permute-start.2 = (bf16[4,128,128]{2,1,0:T(8,128)(2,1)S(1)}, bf16[4,128,128]{2,1,0:T(8,128)(2,1)S(1)}, u32[]{:S(2)}, u32[]{:S(2)}) collective-permute-start(bf16[4,128,128]{2,1,0:T(8,128)(2,1)S(1)} %add_convert_fusion.5), channel_id=1, source_target_pairs={{0,16},{4,20},{8,24},{12,28},{16,0},{20,4},{24,8},{28,12},{32,48},... | collective-permute-start | bytes 393224 | tf_op jit(solution)/shard_map/ppermute | solution.py:105
  15.2 25.9 %collective-permute-start.10 = (bf16[256,1024]{1,0:T(8,128)(2,1)S(1)}, bf16[256,1024]{1,0:T(8,128)(2,1)S(1)}, u32[]{:S(2)}, u32[]{:S(2)}) collective-permute-start(bf16[256,1024]{1,0:T(8,128)(2,1)S(1)} %get-tuple-element.9), channel_id=1, source_target_pairs={{0,1},{1,0},{2,3},{3,2},{4,5},{5,4},{6,7},{7,6},{8,9},{9,8},{10,11... | collective-permute-start | bytes 1572872 | tf_op jit(solution)/shard_map/ppermute | solution.py:108
  25.1 16.0 %collective-permute-start.16 = (bf16[256,1024]{1,0:T(8,128)(2,1)S(1)}, bf16[256,1024]{1,0:T(8,128)(2,1)S(1)}, u32[]{:S(2)}, u32[]{:S(2)}) collective-permute-start(bf16[256,1024]{1,0:T(8,128)(2,1)S(1)} %get-tuple-element.12), channel_id=1, source_target_pairs={{0,1},{1,0},{2,3},{3,2},{4,5},{5,4},{6,7},{7,6},{8,9},{9,8},{10,11... | collective-permute-start | bytes 1572872 | tf_op jit(solution)/shard_map/ppermute | solution.py:108
  26.3 24.0 %collective-permute-start.21 = (bf16[256,1024]{1,0:T(8,128)(2,1)S(1)}, bf16[256,1024]{1,0:T(8,128)(2,1)S(1)}, u32[]{:S(2)}, u32[]{:S(2)}) collective-permute-start(bf16[256,1024]{1,0:T(8,128)(2,1)S(1)} %get-tuple-element.11), channel_id=1, source_target_pairs={{0,1},{1,0},{2,3},{3,2},{4,5},{5,4},{6,7},{7,6},{8,9},{9,8},{10,11... | collective-permute-start | bytes 1572872 | tf_op jit(solution)/shard_map/ppermute | solution.py:108
  26.6 35.1 %collective-permute-start.26 = (bf16[256,1024]{1,0:T(8,128)(2,1)S(1)}, bf16[256,1024]{1,0:T(8,128)(2,1)S(1)}, u32[]{:S(2)}, u32[]{:S(2)}) collective-permute-start(bf16[256,1024]{1,0:T(8,128)(2,1)S(1)} %get-tuple-element.10), channel_id=1, source_target_pairs={{0,1},{1,0},{2,3},{3,2},{4,5},{5,4},{6,7},{7,6},{8,9},{9,8},{10,11... | collective-permute-start | bytes 1572872 | tf_op jit(solution)/shard_map/ppermute | solution.py:108
  37.0 26.4 %collective-permute-start.4 = (bf16[2,4,128,128]{3,2,1,0:T(8,128)(2,1)S(1)}, bf16[2,4,128,128]{3,2,1,0:T(8,128)(2,1)S(1)}, u32[]{:S(2)}, u32[]{:S(2)}) collective-permute-start(bf16[2,4,128,128]{3,2,1,0:T(8,128)(2,1)S(1)} %pad_maximum_fusion.1.zo_ref), channel_id=1, source_target_pairs={{0,4},{4,0},{8,12},{12,8},{16,20},{20,16},{24,28},{28,24},{32,36},... | collective-permute-start | bytes 786440 | tf_op jit(solution)/shard_map/ppermute | solution.py:105
  41.1 24.2 %collective-permute-start.11 = (bf16[256,1024]{1,0:T(8,128)(2,1)S(1)}, bf16[256,1024]{1,0:T(8,128)(2,1)S(1)}, u32[]{:S(2)}, u32[]{:S(2)}) collective-permute-start(bf16[256,1024]{1,0:T(8,128)(2,1)S(1)} %collective-permute-done.10.a_ref), channel_id=1, source_target_pairs={{0,8},{4,12},{8,0},{12,4},{16,24},{20,28},{24,16},{28,20},{32,40},... | collective-permute-start | bytes 1572872 | tf_op jit(solution)/shard_map/ppermute | solution.py:105
  41.2 40.2 %collective-permute-start.12 = (bf16[256,1024]{1,0:T(8,128)(2,1)S(1)}, bf16[256,1024]{1,0:T(8,128)(2,1)}, u32[]{:S(2)}, u32[]{:S(2)}) collective-permute-start(bf16[256,1024]{1,0:T(8,128)(2,1)S(1)} %collective-permute-done.10.a_ref), channel_id=1, source_target_pairs={{0,4},{4,0},{8,12},{12,8},{16,20},{20,16},{24,28},{28,24},{32,36},... | collective-permute-start | bytes 1572872 | tf_op jit(solution)/shard_map/ppermute | solution.py:105
  50.4 32.2 %collective-permute-start.17 = (bf16[256,1024]{1,0:T(8,128)(2,1)S(1)}, bf16[256,1024]{1,0:T(8,128)(2,1)}, u32[]{:S(2)}, u32[]{:S(2)}) collective-permute-start(bf16[256,1024]{1,0:T(8,128)(2,1)S(1)} %collective-permute-done.16.a_ref), channel_id=1, source_target_pairs={{0,32},{4,36},{8,40},{12,44},{16,48},{20,52},{24,56},{28,60},{32,0... | collective-permute-start | bytes 1572872 | tf_op jit(solution)/shard_map/ppermute | solution.py:105
  61.7 21.8 %collective-permute-start.18 = (bf16[256,1024]{1,0:T(8,128)(2,1)S(1)}, bf16[256,1024]{1,0:T(8,128)(2,1)}, u32[]{:S(2)}, u32[]{:S(2)}) collective-permute-start(bf16[256,1024]{1,0:T(8,128)(2,1)S(1)} %collective-permute-done.16.a_ref), channel_id=1, source_target_pairs={{0,4},{4,0},{8,12},{12,8},{16,20},{20,16},{24,28},{28,24},{32,36},... | collective-permute-start | bytes 1572872 | tf_op jit(solution)/shard_map/ppermute | solution.py:105
  65.3 18.4 %collective-permute-start.22 = (bf16[256,1024]{1,0:T(8,128)(2,1)S(1)}, bf16[256,1024]{1,0:T(8,128)(2,1)}, u32[]{:S(2)}, u32[]{:S(2)}) collective-permute-start(bf16[256,1024]{1,0:T(8,128)(2,1)S(1)} %collective-permute-done.21.a_ref), channel_id=1, source_target_pairs={{0,8},{4,12},{8,0},{12,4},{16,24},{20,28},{24,16},{28,20},{32,40},... | collective-permute-start | bytes 1572872 | tf_op jit(solution)/shard_map/ppermute | solution.py:105
  66.1 18.0 %collective-permute-start.27 = (bf16[256,1024]{1,0:T(8,128)(2,1)S(1)}, bf16[256,1024]{1,0:T(8,128)(2,1)}, u32[]{:S(2)}, u32[]{:S(2)}) collective-permute-start(bf16[256,1024]{1,0:T(8,128)(2,1)S(1)} %collective-permute-done.26.a_ref), channel_id=1, source_target_pairs={{0,32},{4,36},{8,40},{12,44},{16,48},{20,52},{24,56},{28,60},{32,0... | collective-permute-start | bytes 1572872 | tf_op jit(solution)/shard_map/ppermute | solution.py:105
  81.4 13.0 %collective-permute-start.14 = (bf16[1,256,1024]{2,1,0:T(8,128)(2,1)}, bf16[1,256,1024]{2,1,0:T(8,128)(2,1)S(1)}, u32[]{:S(2)}, u32[]{:S(2)}) collective-permute-start(bf16[1,256,1024]{2,1,0:T(8,128)(2,1)} %far_first.1), channel_id=1, source_target_pairs={{0,1},{1,0},{2,3},{3,2},{4,5},{5,4},{6,7},{7,6},{8,9},{9,8},{10,11... | collective-permute-start | bytes 1572872 | tf_op jit(solution)/shard_map/ppermute | solution.py:108
  82.6 13.3 %collective-permute-start.13 = (bf16[256,1024]{1,0:T(8,128)(2,1)S(1)}, bf16[256,1024]{1,0:T(8,128)(2,1)S(1)}, u32[]{:S(2)}, u32[]{:S(2)}) collective-permute-start(bf16[256,1024]{1,0:T(8,128)(2,1)S(1)} %copy-done.13), channel_id=1, source_target_pairs={{0,4},{4,0},{8,12},{12,8},{16,20},{20,16},{24,28},{28,24},{32,36},... | collective-permute-start | bytes 1572872 | tf_op jit(solution)/shard_map/ppermute | solution.py:105
  83.6 13.6 %collective-permute-start.19 = (bf16[256,1024]{1,0:T(8,128)(2,1)}, bf16[256,1024]{1,0:T(8,128)(2,1)S(1)}, u32[]{:S(2)}, u32[]{:S(2)}) collective-permute-start(bf16[256,1024]{1,0:T(8,128)(2,1)} %collective-permute-done.17.b_ref), channel_id=1, source_target_pairs={{0,4},{4,0},{8,12},{12,8},{16,20},{20,16},{24,28},{28,24},{32,36},... | collective-permute-start | bytes 1572872 | tf_op jit(solution)/shard_map/ppermute | solution.py:105
  83.7 27.2 %collective-permute-start.23 = (bf16[256,1024]{1,0:T(8,128)(2,1)S(1)}, bf16[256,1024]{1,0:T(8,128)(2,1)}, u32[]{:S(2)}, u32[]{:S(2)}) collective-permute-start(bf16[256,1024]{1,0:T(8,128)(2,1)S(1)} %collective-permute-done.21.a_ref), channel_id=1, source_target_pairs={{0,4},{4,0},{8,12},{12,8},{16,20},{20,16},{24,28},{28,24},{32,36},... | collective-permute-start | bytes 1572872 | tf_op jit(solution)/shard_map/ppermute | solution.py:105
  84.1 28.7 %collective-permute-start.24 = (bf16[256,1024]{1,0:T(8,128)(2,1)}, bf16[256,1024]{1,0:T(8,128)(2,1)}, u32[]{:S(2)}, u32[]{:S(2)}) collective-permute-start(bf16[256,1024]{1,0:T(8,128)(2,1)} %collective-permute-done.22.b_ref), channel_id=1, source_target_pairs={{0,4},{4,0},{8,12},{12,8},{16,20},{20,16},{24,28},{28,24},{32,36},... | collective-permute-start | bytes 1572872 | tf_op jit(solution)/shard_map/ppermute | solution.py:105
  94.4 25.1 %collective-permute-start.28 = (bf16[256,1024]{1,0:T(8,128)(2,1)S(1)}, bf16[256,1024]{1,0:T(8,128)(2,1)}, u32[]{:S(2)}, u32[]{:S(2)}) collective-permute-start(bf16[256,1024]{1,0:T(8,128)(2,1)S(1)} %collective-permute-done.26.a_ref), channel_id=1, source_target_pairs={{0,4},{4,0},{8,12},{12,8},{16,20},{20,16},{24,28},{28,24},{32,36},... | collective-permute-start | bytes 1572872 | tf_op jit(solution)/shard_map/ppermute | solution.py:105
  96.0 32.2 %collective-permute-start.9 = (bf16[1,256,1024]{2,1,0:T(8,128)(2,1)}, bf16[1,256,1024]{2,1,0:T(8,128)(2,1)S(1)}, u32[]{:S(2)}, u32[]{:S(2)}) collective-permute-start(bf16[1,256,1024]{2,1,0:T(8,128)(2,1)} %slice.4), channel_id=1, source_target_pairs={{0,1},{1,0},{2,3},{3,2},{4,5},{5,4},{6,7},{7,6},{8,9},{9,8},{10,11... | collective-permute-start | bytes 1572872 | tf_op jit(solution)/shard_map/ppermute | solution.py:108
  97.2 24.2 %collective-permute-start.29 = (bf16[256,1024]{1,0:T(8,128)(2,1)}, bf16[256,1024]{1,0:T(8,128)(2,1)}, u32[]{:S(2)}, u32[]{:S(2)}) collective-permute-start(bf16[256,1024]{1,0:T(8,128)(2,1)} %collective-permute-done.27.b_ref), channel_id=1, source_target_pairs={{0,4},{4,0},{8,12},{12,8},{16,20},{20,16},{24,28},{28,24},{32,36},... | collective-permute-start | bytes 1572872 | tf_op jit(solution)/shard_map/ppermute | solution.py:105
  110.9 42.2 %collective-permute-start.15 = (bf16[256,1024]{1,0:T(8,128)(2,1)S(1)}, bf16[256,1024]{1,0:T(8,128)(2,1)S(1)}, u32[]{:S(2)}, u32[]{:S(2)}) collective-permute-start(bf16[256,1024]{1,0:T(8,128)(2,1)S(1)} %copy-done.19), channel_id=1, source_target_pairs={{0,3},{1,2},{2,1},{3,0},{4,7},{5,6},{6,5},{7,4},{8,11},{9,10},{10,... | collective-permute-start | bytes 1572872 | tf_op jit(solution)/shard_map/ppermute | solution.py:111
  112.8 40.4 %collective-permute-start.20 = (bf16[256,1024]{1,0:T(8,128)(2,1)}, bf16[256,1024]{1,0:T(8,128)(2,1)S(1)}, u32[]{:S(2)}, u32[]{:S(2)}) collective-permute-start(bf16[256,1024]{1,0:T(8,128)(2,1)} %proj_across1.1), channel_id=1, source_target_pairs={{0,3},{1,2},{2,1},{3,0},{4,7},{5,6},{6,5},{7,4},{8,11},{9,10},{10,... | collective-permute-start | bytes 1572872 | tf_op jit(solution)/shard_map/ppermute | solution.py:111
  119.5 33.9 %collective-permute-start.25 = (bf16[256,1024]{1,0:T(8,128)(2,1)}, bf16[256,1024]{1,0:T(8,128)(2,1)S(1)}, u32[]{:S(2)}, u32[]{:S(2)}) collective-permute-start(bf16[256,1024]{1,0:T(8,128)(2,1)} %proj_across2.1), channel_id=1, source_target_pairs={{0,3},{1,2},{2,1},{3,0},{4,7},{5,6},{6,5},{7,4},{8,11},{9,10},{10,... | collective-permute-start | bytes 1572872 | tf_op jit(solution)/shard_map/ppermute | solution.py:111
  127.3 32.0 %collective-permute-start.30 = (bf16[256,1024]{1,0:T(8,128)(2,1)}, bf16[256,1024]{1,0:T(8,128)(2,1)S(1)}, u32[]{:S(2)}, u32[]{:S(2)}) collective-permute-start(bf16[256,1024]{1,0:T(8,128)(2,1)} %proj_across3.1), channel_id=1, source_target_pairs={{0,3},{1,2},{2,1},{3,0},{4,7},{5,6},{6,5},{7,4},{8,11},{9,10},{10,... | collective-permute-start | bytes 1572872 | tf_op jit(solution)/shard_map/ppermute | solution.py:111
  (27 other events, 371.6 us)

commit v3 on v2

v3 whole, which is shorter than its diff:
```python
import functools

import jax
import jax.numpy as jnp
from jax import lax
from jax.experimental import pallas as pl
from jax.experimental.pallas import tpu as pltpu
from jax.sharding import PartitionSpec as P

C = 256
DH = 128
EPS = 1e-06
BF = jnp.bfloat16
F32 = jnp.float32
VMEM_LIMIT = 36 << 20
CHUNKS = 4
STEP_BITS = (1, 3, 1, 3)


def dot_t(a, b):
    return lax.dot_general(a, b, (((1,), (1,)), ((), ())), preferred_element_type=F32)


def dot_tt(a, b):
    return lax.dot_general(a, b, (((0,), (0,)), ((), ())), preferred_element_type=F32)


def params():
    return pltpu.CompilerParams(vmem_limit_bytes=VMEM_LIMIT)


def cost(flops, nbytes):
    return pl.CostEstimate(flops=flops >> 12, bytes_accessed=nbytes >> 12, transcendentals=0)


def start_all(copies):
    for copy in copies:
        copy.start()
    return copies


def start_all(copies):
    for copy in copies:
        copy.start()
    return copies


def wait_all(copies):
    for copy in copies:
        copy.wait()


def slice_copies(chunks, s_ref, w_hbm, outs, sems, first):
    copies = []
    for n, (chunk, out) in enumerate(zip(chunks, outs)):
        rows, cols = out.shape
        start = (s_ref[0] * 2 + s_ref[1 + STEP_BITS[chunk]]) * rows
        src = w_hbm.at[pl.ds(pl.multiple_of(start, rows), rows), chunk * cols : (chunk + 1) * cols]
        copies.append(pltpu.make_async_copy(src, out, sems.at[first + n]))
    return copies


def state_kernel(
    s_ref, k_hbm, v_hbm, w_hbm, total_ref, local_ref, w0_hbm, w1_hbm, k_buf, v_buf, acc, sems
):
    heads = total_ref.shape[0]
    copies = []
    for stretch in range(4):
        rows = slice(stretch * C, (stretch + 1) * C)
        copies.append(
            start_all(
                [
                    pltpu.make_async_copy(src.at[rows], dst.at[rows], sems.at[2 * stretch + n])
                    for n, (src, dst) in enumerate(((k_hbm, k_buf), (v_hbm, v_buf)))
                ]
            )
        )
    slices = start_all(slice_copies((0, 1), s_ref, w_hbm, (w0_hbm, w1_hbm), sems, 8))
    for stretch in range(4):
        rows = slice(stretch * C, (stretch + 1) * C)
        wait_all(copies[stretch])
        for head in range(heads):
            cols = slice(head * DH, (head + 1) * DH)
            state = dot_tt(v_buf[rows, cols], k_buf[rows, cols])
            if stretch == 0:
                acc[head] = state
                local_ref[head, 0] = state.astype(BF)
            elif stretch == 1:
                state = acc[head] + state
                acc[head] = state
                local_ref[head, 2] = state.astype(BF)
            elif stretch == 2:
                acc[head] = acc[head] + state
                local_ref[head, 1] = state.astype(BF)
            else:
                total_ref[head] = (acc[head] + state).astype(BF)
    wait_all(slices)


def local_kernel(
    s_ref, q_hbm, k_hbm, v_hbm, w_hbm, g_ref, local_ref, token_ref, out_hbm, w2_ref, w3_ref,
    q_buf, k_buf, v_buf, out_buf, sems
):
    copies = []
    for stretch in range(4):
        rows = slice(stretch * C, (stretch + 1) * C)
        copies.append(
            start_all(
                [
                    pltpu.make_async_copy(src.at[rows], dst.at[rows], sems.at[3 * stretch + n])
                    for n, (src, dst) in enumerate(
                        ((q_hbm, q_buf), (k_hbm, k_buf), (v_hbm, v_buf))
                    )
                ]
            )
        )
    slices = start_all(slice_copies((2, 3), s_ref, w_hbm, (w2_ref, w3_ref), sems, 16))
    causal = lax.broadcasted_iota(jnp.int32, (C, C), 0) <= lax.broadcasted_iota(
        jnp.int32, (C, C), 1
    )
    stores = []
    for stretch in range(4):
        rows = slice(stretch * C, (stretch + 1) * C)
        wait_all(copies[stretch])
        for head in range(local_ref.shape[0]):
            cols = slice(head * DH, (head + 1) * DH)
            gate = lambda level: g_ref[level, head : head + 1, rows]
            q = q_buf[rows, cols]
            weights = jnp.where(causal, dot_t(k_buf[rows, cols], q), 0.0).astype(BF)
            out = dot_tt(v_buf[rows, cols], weights) * gate(0)
            if stretch % 2 == 1:
                out = out + dot_t(local_ref[head, stretch // 2], q) * gate(1)
            if stretch // 2 == 1:
                out = out + dot_t(local_ref[head, 2], q) * gate(2)
            out_buf[stretch, cols, :] = out
        store = pltpu.make_async_copy(
            out_buf.at[stretch], out_hbm.at[stretch], sems.at[12 + stretch]
        )
        store.start()
        stores.append(store)
    wait_all(stores)
    wait_all(slices)


def far_block(s_ref, q_ref, comb_ref, g_ref, core_ref, zo_ref, yo_ref, zs_ref, ys_ref, out_ref):
    masks = [s_ref[1 + j].astype(F32) for j in range(5)]
    half = zo_ref.shape[1]
    for slot in range(2 * half):
        own = slot < half
        inner = slot % half
        head = (s_ref[0] if own else 1 - s_ref[0]) * half + inner
        z_ref, y_ref = (zo_ref, yo_ref) if own else (zs_ref, ys_ref)
        offset = pl.multiple_of(head * DH, DH)
        states = jnp.concatenate(
            [core_ref[head], z_ref[0, inner], z_ref[1, inner], y_ref[0, inner], y_ref[1, inner]], 0
        )
        read = dot_t(states, q_ref[:, pl.ds(offset, DH)])
        out = comb_ref[0, pl.ds(offset, DH), :]
        for j in range(5):
            out = out + read[j * DH : (j + 1) * DH] * (g_ref[3 + j, pl.ds(head, 1), :] * masks[j])
        mean = jnp.mean(out * out, axis=0, keepdims=True)
        out_ref[:, slot * DH : (slot + 1) * DH] = jnp.transpose(
            (out * lax.rsqrt(mean + EPS)).astype(BF)
        )


def far_first_kernel(s_ref, token_ref, *refs):
    far_block(s_ref, *refs)


def far_rest_kernel(s_ref, token_ref, *refs):
    *inputs, near_ref, keep_ref, buf = refs
    far_block(s_ref, *inputs, buf)

    @pl.when(pl.program_id(0) == 0)
    def _():
        near_ref[...] = buf[...]

    @pl.when(pl.program_id(0) > 0)
    def _():
        keep_ref[0] = buf[...]


def gate_kernel(data_ref, token_ref, out_ref):
    pass


def weight_copies(chunk, s_ref, w_hbm, pieces, dst, size, cols, sems, first):
    rows = dst.shape[0]
    half, quarter = rows // 4, rows // 8
    core, low = s_ref[0], s_ref[1 + STEP_BITS[chunk]]
    copies = []

    def add(src, row, count):
        copies.append(
            pltpu.make_async_copy(
                src, dst.at[pl.ds(row, count), cols], sems.at[first + len(copies)]
            )
        )

    own_cols = slice(chunk * size + cols.start, chunk * size + cols.stop)
    for part, which in enumerate((core, 1 - core)):
        add(w_hbm.at[pl.ds(pl.multiple_of(which * half, half), half), own_cols], part * half, half)
    for part, ref in enumerate(pieces):
        place = low if part % 2 == 0 else 1 - low
        start = pl.multiple_of((2 + part // 2) * half + place * quarter, quarter)
        add(ref.at[:, cols], start, quarter)
    return copies


def across_kernel(chunk, s_ref, token_ref, keep, got, w_hbm, *refs):
    pieces, out_ref, lhs, w, sems = refs[:4], *refs[4:]
    width = lhs.shape[1] // 2
    size = out_ref.shape[1]
    tile = size // 2
    left = start_all(
        [
            pltpu.make_async_copy(keep.at[0], lhs.at[:, :width], sems.at[0]),
            pltpu.make_async_copy(got, lhs.at[:, width:], sems.at[1]),
        ]
    )
    right = [
        start_all(
            weight_copies(
                chunk, s_ref, w_hbm, pieces, w, size, slice(n * tile, (n + 1) * tile), sems, 2 + 6 * n
            )
        )
        for n in range(2)
    ]
    wait_all(left)
    for n, group in enumerate(right):
        cols = slice(n * tile, (n + 1) * tile)
        wait_all(group)
        out_ref[:, cols] = jnp.dot(lhs[...], w[:, cols], preferred_element_type=F32).astype(
            out_ref.dtype
        )


def own_kernel(s_ref, token_ref, keep, got, w_hbm, *refs):
    count = CHUNKS
    pieces = [refs[4 * i : 4 * i + 4] for i in range(count)]
    received = refs[4 * count : 5 * count - 1]
    out_hbm, last_ref, lhs, w, out_buf, sems = refs[5 * count - 1 :]
    width = lhs.shape[1] // 2
    size = w.shape[2]
    left = start_all(
        [
            pltpu.make_async_copy(keep.at[1], lhs.at[:, :width], sems.at[0]),
            pltpu.make_async_copy(got, lhs.at[:, width:], sems.at[1]),
        ]
    )
    right = [
        start_all(
            weight_copies(
                i, s_ref, w_hbm, pieces[i], w.at[i], size, slice(0, size), sems, 2 + 6 * i
            )
        )
        for i in range(count)
    ]
    wait_all(left)
    stores = []
    for i in range(count):
        cols = slice(i * size, (i + 1) * size)
        wait_all(right[i])
        own = jnp.dot(lhs[...], w[i], preferred_element_type=F32)
        if i == count - 1:
            last_ref[...] = own
            break
        out_buf[:, cols] = (own + received[i][...].astype(F32)).astype(BF)
        store = pltpu.make_async_copy(
            out_buf.at[:, cols], out_hbm.at[:, cols], sems.at[2 + 6 * count + i]
        )
        store.start()
        stores.append(store)
    wait_all(stores)


def finish_kernel(base_ref, own_ref, got_ref, out_hbm, buf, sem):
    buf[...] = (own_ref[...] + got_ref[...].astype(F32)).astype(BF)
    size = buf.shape[1]
    copy = pltpu.make_async_copy(buf, out_hbm.at[:, (CHUNKS - 1) * size : CHUNKS * size], sem.at[0])
    copy.start()
    copy.wait()


def on_device(query_rows, key_rows, value_rows, level_gate, out_weight):
    tokens, width = query_rows.shape
    levels, heads, _ = level_gate.shape
    model = out_weight.shape[1]
    stretches = tokens // C
    half = heads // 2
    chunk = model // CHUNKS
    ctx_size = lax.axis_size("ctx")
    me = lax.axis_index("ctx")
    x = lax.axis_index("head")
    bit = lambda j: lax.bitwise_and(lax.shift_right_logical(me, j), 1)
    core = bit(0)
    any_spec = pl.BlockSpec(memory_space=pl.ANY)
    vmem_spec = pl.BlockSpec(memory_space=pltpu.VMEM)
    smem_spec = pl.BlockSpec(memory_space=pltpu.SMEM)
    dma = pltpu.SemaphoreType.DMA
    near_x, across_x, far_x = lax.bitwise_xor(x, 1), 3 - x, lax.bitwise_xor(x, 2)
    scalars = jnp.stack([core] + [bit(j) for j in range(5)] + [far_x, near_x, across_x, x])
    scalars = scalars.astype(jnp.int32)
    hbm = lambda array: pltpu.with_memory_space_constraint(array, pltpu.HBM)
    query_rows, key_rows, value_rows, out_weight = map(
        hbm, (query_rows, key_rows, value_rows, out_weight)
    )

    def ctx_swap(array, step):
        return lax.ppermute(array, "ctx", [(i, i ^ step) for i in range(ctx_size)])

    def near(array):
        return lax.ppermute(array, "head", [(i, i ^ 1) for i in range(4)])

    def across(array):
        return lax.ppermute(array, "head", [(i, 3 - i) for i in range(4)])

    def after(array, token):
        return pl.pallas_call(
            gate_kernel,
            in_specs=[any_spec, any_spec],
            out_specs=any_spec,
            out_shape=jax.ShapeDtypeStruct(array.shape, array.dtype),
            input_output_aliases={0: 0},
            name="after",
        )(array, token)

    piece_shape = jax.ShapeDtypeStruct((width // 4, chunk), BF)
    total, local, slice0, slice1 = pl.pallas_call(
        state_kernel,
        in_specs=[smem_spec, any_spec, any_spec, any_spec],
        out_specs=[vmem_spec] * 4,
        out_shape=[
            jax.ShapeDtypeStruct((heads, DH, DH), BF),
            jax.ShapeDtypeStruct((heads, 3, DH, DH), BF),
            piece_shape,
            piece_shape,
        ],
        scratch_shapes=[
            pltpu.VMEM((tokens, width), BF),
            pltpu.VMEM((tokens, width), BF),
            pltpu.VMEM((heads, DH, DH), F32),
            dma((10,)),
        ],
        cost_estimate=cost(2 * tokens * width * DH, 7 << 20),
        compiler_params=params(),
        name="states",
    )(scalars, key_rows, value_rows, out_weight)

    pick = lambda array: lax.dynamic_slice_in_dim(array, core * half, half, 0)
    add = lambda *arrays: sum(a.astype(F32) for a in arrays)
    sibling = ctx_swap(total, 1)
    fetched = [near(slice0)]
    chip = add(pick(total), pick(sibling)).astype(BF)
    z1, z2, z3 = (ctx_swap(chip, step) for step in (2, 4, 6))
    fetched.append(near(after(slice1, chip)))

    combined, slice2, slice3 = pl.pallas_call(
        local_kernel,
        in_specs=[smem_spec] + [any_spec] * 4 + [vmem_spec] * 2 + [any_spec],
        out_specs=[any_spec, vmem_spec, vmem_spec],
        out_shape=[pltpu.HBM((stretches, width, C), F32), piece_shape, piece_shape],
        scratch_shapes=[
            pltpu.VMEM((tokens, width), BF),
            pltpu.VMEM((tokens, width), BF),
            pltpu.VMEM((tokens, width), BF),
            pltpu.VMEM((stretches, width, C), F32),
            dma((18,)),
        ],
        cost_estimate=cost(12 * tokens * width * DH, 12 << 20),
        compiler_params=params(),
        name="local",
    )(scalars, query_rows, key_rows, value_rows, out_weight, level_gate, local, chip)
    z3 = after(z3, combined)
    z_own = jnp.stack([z1, add(z2, z3).astype(BF)])
    row = add(chip, z1, z2, z3).astype(BF)
    y1, y2, y3 = (ctx_swap(row, step) for step in (8, 16, 24))
    z_sib = ctx_swap(z_own, 1)

    def gather(i, first_token, second_token):
        mine = after(fetched[i], first_token)
        other = after(ctx_swap(mine, 1 << STEP_BITS[i]), second_token)
        return (mine, other, ctx_swap(mine, 1), ctx_swap(other, 1))

    y_own = jnp.stack([y1, add(y2, y3).astype(BF)])
    y_sib = ctx_swap(y_own, 1)
    fetched.append(near(after(slice2, z_own)))
    pieces = [gather(0, z_own, y_own)]

    def far_norm(first, token):
        count = 1 if first else 3
        base = 6 if first else 7
        block = (C, width)
        return pl.pallas_call(
            far_first_kernel if first else far_rest_kernel,
            grid_spec=pltpu.PrefetchScalarGridSpec(
                num_scalar_prefetch=1,
                grid=(count,),
                in_specs=[
                    any_spec,
                    pl.BlockSpec((C, width), lambda i, s: (s[base + i], 0)),
                    pl.BlockSpec((1, width, C), lambda i, s: (s[base + i], 0, 0)),
                    pl.BlockSpec((levels, heads, C), lambda i, s: (0, 0, s[base + i])),
                ]
                + [vmem_spec] * 5,
                out_specs=[pl.BlockSpec(block, lambda i, s: (0, 0))]
                + (
                    []
                    if first
                    else [pl.BlockSpec((1, *block), lambda i, s: (jnp.maximum(i - 1, 0), 0, 0))]
                ),
                scratch_shapes=[] if first else [pltpu.VMEM(block, BF)],
            ),
            out_shape=[pltpu.HBM(block, BF)] + ([] if first else [pltpu.HBM((2, *block), BF)]),
            cost_estimate=cost(10 * count * C * width * DH, count * (2 << 20)),
            compiler_params=params(),
            name="far_first" if first else "far_rest",
        )(
            scalars, token, query_rows, combined, level_gate, sibling, z_own, y_own, z_sib, y_sib
        )

    (first,) = far_norm(True, pieces[0][3])
    got_across = near(first)
    near_rows, keep = far_norm(False, first)

    def project(i, tokens):
        def kernel(s_ref, *refs):
            across_kernel(i, s_ref, *refs[len(tokens) - 1 :])

        return pl.pallas_call(
            kernel,
            in_specs=[smem_spec] + [any_spec] * (7 + len(tokens)),
            out_specs=vmem_spec,
            out_shape=jax.ShapeDtypeStruct((C, chunk), BF),
            scratch_shapes=[
                pltpu.VMEM((C, 2 * width), BF),
                pltpu.VMEM((2 * width, chunk), BF),
                dma((14,)),
            ],
            cost_estimate=cost(4 * C * width * chunk, 5 << 20),
            compiler_params=params(),
            name="across%d" % i,
        )(scalars, *tokens, keep, got_across, out_weight, *pieces[i])

    partials = [project(0, [keep])]
    received = [across(partials[0])]
    pieces.append(gather(1, y_own, keep))
    fetched.append(near(after(slice3, partials[0])))
    pieces.append(gather(2, keep, partials[0]))
    partials.append(project(1, [partials[0]]))
    received.append(across(partials[1]))
    got_own = near(after(near_rows, partials[1]))
    partials.append(project(2, [partials[1], received[0]]))
    received.append(across(partials[2]))
    pieces.append(gather(3, partials[1], partials[2]))
    partials.append(project(3, [partials[2], received[1]]))
    received.append(across(partials[3]))
    token = partials[3]
    out, last = pl.pallas_call(
        own_kernel,
        in_specs=[smem_spec] + [any_spec] * (4 + 4 * CHUNKS) + [vmem_spec] * (CHUNKS - 1),
        out_specs=[any_spec, vmem_spec],
        out_shape=[pltpu.HBM((C, model), BF), jax.ShapeDtypeStruct((C, chunk), F32)],
        scratch_shapes=[
            pltpu.VMEM((C, 2 * width), BF),
            pltpu.VMEM((CHUNKS, 2 * width, chunk), BF),
            pltpu.VMEM((C, (CHUNKS - 1) * chunk), BF),
            dma((2 + 7 * CHUNKS,)),
        ],
        cost_estimate=cost(4 * C * width * model, 20 << 20),
        compiler_params=params(),
        name="own",
    )(
        scalars,
        token,
        keep,
        got_own,
        out_weight,
        *[piece for group in pieces for piece in group],
        *received[:-1],
    )
    return pl.pallas_call(
        finish_kernel,
        in_specs=[any_spec, vmem_spec, vmem_spec],
        out_specs=any_spec,
        out_shape=pltpu.HBM((C, model), BF),
        scratch_shapes=[pltpu.VMEM((C, chunk), BF), dma((1,))],
        input_output_aliases={0: 0},
        compiler_params=params(),
        name="finish",
    )(out, last, received[-1])


def solution(mesh):
    in_specs = (
        P("ctx", "head"),
        P("ctx", "head"),
        P("ctx", "head"),
        P(None, "head", "ctx"),
        P("head", None),
    )
    out_specs = P(("ctx", "head"), None)
    return jax.shard_map(
        on_device, mesh=mesh, in_specs=in_specs, out_specs=out_specs, check_vma=False
    )
```

time: 162 us -> 127 us (0.78)
  Pallas kernels: 73 us -> 45.2 us
  waiting for transfers between devices: 39 us -> 21.7 us
  local copies, waits for them, and re-layouts: 7.41 us -> 17 us
  starting transfers between devices: 36.8 us -> 39.9 us
  other arithmetic: 4.5 us -> 2.53 us
    pallas_call x12 -> x23, Pallas kernels: 73 us -> 45.2 us  [the longest x4 14.4 us: project(): pl.pallas_call(kernel, in_specs=[smem_spec] + [any_spec] * (7 + len(token...]
    unnamed x40 -> x74, local copies, waits for them, and re-layouts: 2.55 us -> 16.9 us
    ppermute x6, waiting for transfers between devices: 18.8 us -> 7.27 us  [near(): return lax.ppermute(array, 'head', [(i, i ^ 1) for i in range(4)])]
    ppermute x21, waiting for transfers between devices: 15.3 us -> 9.59 us  [ctx_swap(): return lax.ppermute(array, 'ctx', [(i, i ^ step) for i in range(ctx_size)])]
    ppermute x4, starting transfers between devices: 5.51 us -> 7.6 us  [across(): return lax.ppermute(array, 'head', [(i, 3 - i) for i in range(4)])]
    slice x1 -> x0, local copies, waits for them, and re-layouts: 1.88 us -> none  [on_device(): got_own = near(rest[1:2])]
    dynamic_slice x1 -> x0, local copies, waits for them, and re-layouts: 1.74 us -> none  [on_device(): lax.dynamic_slice(out_weight, (quarter * 256, i * chunk), (256, chunk))]
  transfers between devices with their start and end apart: 31 -> 31, of which waited for: 10 -> 11; matrix products, arithmetic and copies ran while one was open for 4% -> 2% of each run, Pallas kernels for 43% -> 32%
where the time goes in v3:
time: 127 us
  Pallas kernels  45.2 us (36%)
  starting transfers between devices  39.9 us (31%)
  waiting for transfers between devices  21.7 us (17%)
  local copies, waits for them, and re-layouts  17 us (13%)
  other arithmetic  2.53 us (2%)
    ppermute x21, starting transfers between devices, ctx_swap(): return lax.ppermute(array, 'ctx', [(i, i ^ step) for i in range(ctx_size)])  25.5 us
    unnamed x74, local copies, waits for them, and re-layouts  16.9 us
    pallas_call x4, Pallas kernels, project(): pl.pallas_call(kernel, in_specs=[smem_spec] + [any_spec] * (7 + len(token...  14.4 us
    ppermute x21, waiting for transfers between devices, ctx_swap(): return lax.ppermute(array, 'ctx', [(i, i ^ step) for i in range(ctx_size)])  9.59 us
    pallas_call x2, Pallas kernels, far_norm(): pl.pallas_call(far_first_kernel if first else far_rest_kernel, grid_spec=...  9.19 us
    pallas_call x1, Pallas kernels, on_device(): pl.pallas_call(local_kernel, in_specs=[smem_spec] + [any_spec] * 4 + [vme...  8.96 us
    pallas_call x1, Pallas kernels, on_device(): pl.pallas_call(own_kernel, in_specs=[smem_spec] + [any_spec] * (4 + 4 * C...  8.47 us
    ppermute x4, starting transfers between devices, across(): return lax.ppermute(array, 'head', [(i, 3 - i) for i in range(4)])  7.6 us
  transfers between devices with their start and end apart: 31, of which 11 were waited for; matrix products, arithmetic and copies ran while one was open for 2% of the time, Pallas kernels for 32%

profile of v3, /device:TPU:1, one launch (start us, length us, event | category | flops | bytes accessed | tf_op | source)
XLA Modules:
  0.0 126.7 jit_solution(7284830147405004189)
XLA Ops:
  0.1 3.3 %states.1 = (bf16[8,128,128]{2,1,0:T(8,128)(2,1)S(1)}, bf16[8,3,128,128]{3,2,1,0:T(8,128)(2,1)S(1)}, bf16[256,1024]{1,0:T(8,128)(2,1)S(1)}, bf16[256,1024]{1,0:T(8,128)(2,1)S(1)}) custom-call(s32[10]{0:T(128)S(1)} %stack.58.s_ref, bf16[1024,1024]{1,0:T(8,128)(2,1)} %k_hbm.3, bf16[1024,1024]{1,0:T(8,128)(2,1)} %v_hbm.3, bf16[1024,4096]{1,0:T(8,128)(2,1)} %w_hbm.5), custom_call_target="tpu_custom_call" | custom-call | flops 65536 | bytes 1792 | tf_op jit(solution)/shard_map/states/pallas_call | solution.py:330
  6.9 3.8 %collective-permute-start.4 = (bf16[4,128,128]{2,1,0:T(8,128)(2,1)S(1)}, bf16[4,128,128]{2,1,0:T(8,128)(2,1)S(1)}, u32[]{:S(2)}, u32[]{:S(2)}) collective-permute-start(bf16[4,128,128]{2,1,0:T(8,128)(2,1)S(1)} %add_convert_fusion.1.token_ref), channel_id=1, source_target_pairs={{0,24},{4,28},{8,16},{12,20},{16,8},{20,12},{24,0},{28,4},{32,56},... | collective-permute-start | bytes 393224 | tf_op jit(solution)/shard_map/ppermute | solution.py:311
  12.0 9.0 %local.1 = (f32[4,1024,256]{2,1,0:T(8,128)}, bf16[256,1024]{1,0:T(8,128)(2,1)S(1)}, bf16[256,1024]{1,0:T(8,128)(2,1)S(1)}) custom-call(s32[10]{0:T(128)S(1)} %stack.58.s_ref, bf16[1024,1024]{1,0:T(8,128)(2,1)} %refs_0_.3, bf16[1024,1024]{1,0:T(8,128)(2,1)} %k_hbm.3, bf16[1024,1024]{1,0:T(8,128)(2,1)} %v_hbm.3, bf16[1024,4096]{1,0:T(8,128)(2,1)} %w_hbm.5, ...), custom_call_target="tpu_custom_call" | custom-call | flops 393216 | bytes 3072 | tf_op jit(solution)/shard_map/local/pallas_call | solution.py:359
  24.0 2.9 %collective-permute-start.7 = (bf16[4,128,128]{2,1,0:T(8,128)(2,1)S(1)}, bf16[4,128,128]{2,1,0:T(8,128)(2,1)S(1)}, u32[]{:S(2)}, u32[]{:S(2)}) collective-permute-start(bf16[4,128,128]{2,1,0:T(8,128)(2,1)S(1)} %get-tuple-element.27), channel_id=1, source_target_pairs={{0,64},{4,68},{8,72},{12,76},{16,80},{20,84},{24,88},{28,92},{32,9... | collective-permute-start | bytes 393224 | tf_op jit(solution)/shard_map/ppermute | solution.py:311
  29.3 3.6 %collective-permute-done.8 = bf16[4,128,128]{2,1,0:T(8,128)(2,1)S(1)} collective-permute-done((bf16[4,128,128]{2,1,0:T(8,128)(2,1)S(1)}, bf16[4,128,128]{2,1,0:T(8,128)(2,1)S(1)}, u32[]{:S(2)}, u32[]{:S(2)}) %collective-permute-start.8) | collective-permute-done | bytes 131104 | tf_op jit(solution)/shard_map/ppermute | solution.py:311
  33.7 2.9 %collective-permute-done.5.data_ref = bf16[256,1024]{1,0:T(8,128)(2,1)S(1)} collective-permute-done((bf16[256,1024]{1,0:T(8,128)(2,1)}, bf16[256,1024]{1,0:T(8,128)(2,1)S(1)}, u32[]{:S(2)}, u32[]{:S(2)}) %collective-permute-start.5) | collective-permute-done | bytes 524320 | tf_op jit(solution)/shard_map/ppermute | solution.py:311
  43.0 2.3 %copy-done.1 = f32[4,1024,256]{2,1,0:T(8,128)S(1)} copy-done((f32[4,1024,256]{2,1,0:T(8,128)S(1)}, f32[4,1024,256]{2,1,0:T(8,128)}, u32[]{:S(2)}) %copy-start.1) | copy-done | bytes 4194328
  45.3 3.4 %far_first.1.token_ref = bf16[256,1024]{1,0:T(8,128)(2,1)} custom-call(s32[10]{0:T(128)S(1)} %stack.58.s_ref, bf16[256,1024]{1,0:T(8,128)(2,1)S(1)} %collective-permute-done.9.token_ref.refs_7_.refs_3_, bf16[1024,1024]{1,0:T(8,128)(2,1)} %refs_0_.3, f32[4,1024,256]{2,1,0:T(8,128)S(1)} %copy-done.1, f32[8,8,1024]{2,1,0:T(8,128)S(1)} %copy-done.23, ...), custom_call_target="tpu_custom_call" | custom-call | flops 81920 | bytes 512 | tf_op jit(solution)/shard_map/far_first/pallas_call | solution.py:395
  54.2 5.8 %far_rest.1 = (bf16[256,1024]{1,0:T(8,128)(2,1)}, bf16[2,256,1024]{2,1,0:T(8,128)(2,1)}) custom-call(s32[10]{0:T(128)S(1)} %stack.58.s_ref, bf16[256,1024]{1,0:T(8,128)(2,1)S(1)} %copy-done.25, bf16[1024,1024]{1,0:T(8,128)(2,1)} %refs_0_.3, f32[4,1024,256]{2,1,0:T(8,128)S(1)} %copy-done.1, f32[8,8,1024]{2,1,0:T(8,128)S(1)} %copy-done.23, ...), custom_call_target="tpu_custom_call" | custom-call | flops 245760 | bytes 1536 | tf_op jit(solution)/shard_map/far_rest/pallas_call | solution.py:395
  62.8 2.0 %collective-permute-done.12.refs_2_.refs_3_ = bf16[256,1024]{1,0:T(8,128)(2,1)S(1)} collective-permute-done((bf16[256,1024]{1,0:T(8,128)(2,1)}, bf16[256,1024]{1,0:T(8,128)(2,1)S(1)}, u32[]{:S(2)}, u32[]{:S(2)}) %collective-permute-start.12) | collective-permute-done | bytes 524320 | tf_op jit(solution)/shard_map/ppermute | solution.py:314
  65.8 3.5 %across0.1.refs_0_.token_ref = bf16[256,1024]{1,0:T(8,128)(2,1)S(1)} custom-call(s32[10]{0:T(128)S(1)} %stack.58.s_ref, bf16[2,256,1024]{2,1,0:T(8,128)(2,1)S(1)} %copy-done, bf16[2,256,1024]{2,1,0:T(8,128)(2,1)S(1)} %copy-done, bf16[256,1024]{1,0:T(8,128)(2,1)S(1)} %collective-permute-done.12.refs_2_.refs_3_, bf16[1024,4096]{1,0:T(8,128)(2,1)} %w_hbm.5, ...), custom_call_target="tpu_custom_call" | custom-call | flops 262144 | bytes 1280 | tf_op jit(solution)/shard_map/across0/pallas_call | solution.py:431
  72.3 1.8 %collective-permute-done.20.data_ref = bf16[256,1024]{1,0:T(8,128)(2,1)} collective-permute-done((bf16[256,1024]{1,0:T(8,128)(2,1)}, bf16[256,1024]{1,0:T(8,128)(2,1)}, u32[]{:S(2)}, u32[]{:S(2)}) %collective-permute-start.20) | collective-permute-done | bytes 524320 | tf_op jit(solution)/shard_map/ppermute | solution.py:311
  77.0 3.5 %across1.1.refs_0_.token_ref = bf16[256,1024]{1,0:T(8,128)(2,1)S(1)} custom-call(s32[10]{0:T(128)S(1)} %stack.58.s_ref, bf16[256,1024]{1,0:T(8,128)(2,1)S(1)} %copy-done.3, bf16[2,256,1024]{2,1,0:T(8,128)(2,1)S(1)} %copy-done, bf16[256,1024]{1,0:T(8,128)(2,1)S(1)} %collective-permute-done.12.refs_2_.refs_3_, bf16[1024,4096]{1,0:T(8,128)(2,1)} %w_hbm.5, ...), custom_call_target="tpu_custom_call" | custom-call | flops 262144 | bytes 1280 | tf_op jit(solution)/shard_map/across1/pallas_call | solution.py:431
  81.4 1.9 %collective-permute-done.24.data_ref = bf16[256,1024]{1,0:T(8,128)(2,1)} collective-permute-done((bf16[256,1024]{1,0:T(8,128)(2,1)}, bf16[256,1024]{1,0:T(8,128)(2,1)}, u32[]{:S(2)}, u32[]{:S(2)}) %collective-permute-start.24) | collective-permute-done | bytes 524320 | tf_op jit(solution)/shard_map/ppermute | solution.py:314
  84.6 2.4 %collective-permute-start.23 = (bf16[256,1024]{1,0:T(8,128)(2,1)}, bf16[256,1024]{1,0:T(8,128)(2,1)}, u32[]{:S(2)}, u32[]{:S(2)}) collective-permute-start(bf16[256,1024]{1,0:T(8,128)(2,1)} %copy-done.4), channel_id=1, source_target_pairs={{0,3},{1,2},{2,1},{3,0},{4,7},{5,6},{6,5},{7,4},{8,11},{9,10},{10,... | collective-permute-start | bytes 1572872 | tf_op jit(solution)/shard_map/ppermute | solution.py:317
  87.0 2.1 %collective-permute-start.26 = (bf16[256,1024]{1,0:T(8,128)(2,1)}, bf16[256,1024]{1,0:T(8,128)(2,1)}, u32[]{:S(2)}, u32[]{:S(2)}) collective-permute-start(bf16[256,1024]{1,0:T(8,128)(2,1)} %after.23.refs_5_.refs_12_), channel_id=1, source_target_pairs={{0,4},{4,0},{8,12},{12,8},{16,20},{20,16},{24,28},{28,24},{32,36},... | collective-permute-start | bytes 1572872 | tf_op jit(solution)/shard_map/ppermute | solution.py:311
  90.2 3.7 %across2.1.token_ref.refs_0_ = bf16[256,1024]{1,0:T(8,128)(2,1)S(1)} custom-call(s32[10]{0:T(128)S(1)} %stack.58.s_ref, bf16[256,1024]{1,0:T(8,128)(2,1)S(1)} %copy-done.5, bf16[256,1024]{1,0:T(8,128)(2,1)} %collective-permute-done.18.refs_1_.refs_16_, bf16[2,256,1024]{2,1,0:T(8,128)(2,1)S(1)} %copy-done, ...), custom_call_target="tpu_custom_call" | custom-call | flops 262144 | bytes 1280 | tf_op jit(solution)/shard_map/across2/pallas_call | solution.py:431
  96.3 2.4 %collective-permute-start.27 = (bf16[256,1024]{1,0:T(8,128)(2,1)}, bf16[256,1024]{1,0:T(8,128)(2,1)}, u32[]{:S(2)}, u32[]{:S(2)}) collective-permute-start(bf16[256,1024]{1,0:T(8,128)(2,1)} %after.24.refs_6_.refs_13_), channel_id=1, source_target_pairs={{0,4},{4,0},{8,12},{12,8},{16,20},{20,16},{24,28},{28,24},{32,36},... | collective-permute-start | bytes 1572872 | tf_op jit(solution)/shard_map/ppermute | solution.py:311
  99.8 1.8 %collective-permute-start.29 = (bf16[256,1024]{1,0:T(8,128)(2,1)}, bf16[256,1024]{1,0:T(8,128)(2,1)S(1)}, u32[]{:S(2)}, u32[]{:S(2)}) collective-permute-start(bf16[256,1024]{1,0:T(8,128)(2,1)} %copy-done.21), channel_id=1, source_target_pairs={{0,3},{1,2},{2,1},{3,0},{4,7},{5,6},{6,5},{7,4},{8,11},{9,10},{10,... | collective-permute-start | bytes 1572872 | tf_op jit(solution)/shard_map/ppermute | solution.py:317
  103.7 3.6 %across3.1.token_ref = bf16[256,1024]{1,0:T(8,128)(2,1)S(1)} custom-call(s32[10]{0:T(128)S(1)} %stack.58.s_ref, bf16[256,1024]{1,0:T(8,128)(2,1)S(1)} %copy-done.22, bf16[256,1024]{1,0:T(8,128)(2,1)} %collective-permute-done.23.refs_1_.refs_17_, bf16[2,256,1024]{2,1,0:T(8,128)(2,1)S(1)} %copy-done, ...), custom_call_target="tpu_custom_call" | custom-call | flops 262144 | bytes 1280 | tf_op jit(solution)/shard_map/across3/pallas_call | solution.py:431
  108.9 3.4 %collective-permute-done.28.got = bf16[256,1024]{1,0:T(8,128)(2,1)S(1)} collective-permute-done((bf16[256,1024]{1,0:T(8,128)(2,1)}, bf16[256,1024]{1,0:T(8,128)(2,1)S(1)}, u32[]{:S(2)}, u32[]{:S(2)}) %collective-permute-start.28) | collective-permute-done | bytes 524320 | tf_op jit(solution)/shard_map/ppermute | solution.py:314
  112.3 2.1 %collective-permute-done.29.refs_18_ = bf16[256,1024]{1,0:T(8,128)(2,1)S(1)} collective-permute-done((bf16[256,1024]{1,0:T(8,128)(2,1)}, bf16[256,1024]{1,0:T(8,128)(2,1)S(1)}, u32[]{:S(2)}, u32[]{:S(2)}) %collective-permute-start.29) | collective-permute-done | bytes 524320 | tf_op jit(solution)/shard_map/ppermute | solution.py:317
  114.4 8.5 %own.1 = (bf16[256,4096]{1,0:T(8,128)(2,1)}, f32[256,1024]{1,0:T(8,128)S(1)}) custom-call(s32[10]{0:T(128)S(1)} %stack.58.s_ref, bf16[256,1024]{1,0:T(8,128)(2,1)S(1)} %across3.1.token_ref, bf16[2,256,1024]{2,1,0:T(8,128)(2,1)S(1)} %copy-done, bf16[256,1024]{1,0:T(8,128)(2,1)S(1)} %collective-permute-done.28.got, bf16[1024,4096]{1,0:T(8,128)(2,1)} %w_hbm.5, ...), custom_call_target="tpu_custom_call" | custom-call | flops 1048576 | bytes 5120 | tf_op jit(solution)/shard_map/own/pallas_call | solution.py:460
  122.9 2.7 %collective-permute-done.30.got_ref = bf16[256,1024]{1,0:T(8,128)(2,1)S(1)} collective-permute-done((bf16[256,1024]{1,0:T(8,128)(2,1)S(1)}, bf16[256,1024]{1,0:T(8,128)(2,1)S(1)}, u32[]{:S(2)}, u32[]{:S(2)}) %collective-permute-start.30) | collective-permute-done | bytes 524320 | tf_op jit(solution)/shard_map/ppermute | solution.py:317
  (141 shorter events, 44.0 us)
Async XLA Ops:
  5.6 18.2 %collective-permute-start = (bf16[256,1024]{1,0:T(8,128)(2,1)S(1)}, bf16[256,1024]{1,0:T(8,128)(2,1)}, u32[]{:S(2)}, u32[]{:S(2)}) collective-permute-start(bf16[256,1024]{1,0:T(8,128)(2,1)S(1)} %get-tuple-element.16), channel_id=1, source_target_pairs={{0,1},{1,0},{2,3},{3,2},{4,5},{5,4},{6,7},{7,6},{8,9},{9,8},{10,11... | collective-permute-start | bytes 1572872 | tf_op jit(solution)/shard_map/ppermute | solution.py:314
  6.9 14.1 %collective-permute-start.4 = (bf16[4,128,128]{2,1,0:T(8,128)(2,1)S(1)}, bf16[4,128,128]{2,1,0:T(8,128)(2,1)S(1)}, u32[]{:S(2)}, u32[]{:S(2)}) collective-permute-start(bf16[4,128,128]{2,1,0:T(8,128)(2,1)S(1)} %add_convert_fusion.1.token_ref), channel_id=1, source_target_pairs={{0,24},{4,28},{8,16},{12,20},{16,8},{20,12},{24,0},{28,4},{32,56},... | collective-permute-start | bytes 393224 | tf_op jit(solution)/shard_map/ppermute | solution.py:311
  10.8 11.3 %collective-permute-start.2 = (bf16[4,128,128]{2,1,0:T(8,128)(2,1)S(1)}, bf16[4,128,128]{2,1,0:T(8,128)(2,1)S(1)}, u32[]{:S(2)}, u32[]{:S(2)}) collective-permute-start(bf16[4,128,128]{2,1,0:T(8,128)(2,1)S(1)} %add_convert_fusion.1.token_ref), channel_id=1, source_target_pairs={{0,8},{4,12},{8,0},{12,4},{16,24},{20,28},{24,16},{28,20},{32,40},... | collective-permute-start | bytes 393224 | tf_op jit(solution)/shard_map/ppermute | solution.py:311
  10.8 11.3 %collective-permute-start.3 = (bf16[4,128,128]{2,1,0:T(8,128)(2,1)S(1)}, bf16[4,128,128]{2,1,0:T(8,128)(2,1)S(1)}, u32[]{:S(2)}, u32[]{:S(2)}) collective-permute-start(bf16[4,128,128]{2,1,0:T(8,128)(2,1)S(1)} %add_convert_fusion.1.token_ref), channel_id=1, source_target_pairs={{0,16},{4,20},{8,24},{12,28},{16,0},{20,4},{24,8},{28,12},{32,48},... | collective-permute-start | bytes 393224 | tf_op jit(solution)/shard_map/ppermute | solution.py:311
  23.8 12.8 %collective-permute-start.5 = (bf16[256,1024]{1,0:T(8,128)(2,1)}, bf16[256,1024]{1,0:T(8,128)(2,1)S(1)}, u32[]{:S(2)}, u32[]{:S(2)}) collective-permute-start(bf16[256,1024]{1,0:T(8,128)(2,1)} %after.14.refs_4_.refs_0_), channel_id=1, source_target_pairs={{0,8},{4,12},{8,0},{12,4},{16,24},{20,28},{24,16},{28,20},{32,40},... | collective-permute-start | bytes 1572872 | tf_op jit(solution)/shard_map/ppermute | solution.py:311
  26.9 6.0 %collective-permute-start.8 = (bf16[4,128,128]{2,1,0:T(8,128)(2,1)S(1)}, bf16[4,128,128]{2,1,0:T(8,128)(2,1)S(1)}, u32[]{:S(2)}, u32[]{:S(2)}) collective-permute-start(bf16[4,128,128]{2,1,0:T(8,128)(2,1)S(1)} %get-tuple-element.27), channel_id=1, source_target_pairs={{0,96},{4,100},{8,104},{12,108},{16,112},{20,116},{24,120},{28,124... | collective-permute-start | bytes 393224 | tf_op jit(solution)/shard_map/ppermute | solution.py:311
  27.7 13.1 %collective-permute-start.14 = (bf16[256,1024]{1,0:T(8,128)(2,1)}, bf16[256,1024]{1,0:T(8,128)(2,1)S(1)}, u32[]{:S(2)}, u32[]{:S(2)}) collective-permute-start(bf16[256,1024]{1,0:T(8,128)(2,1)} %after.16), channel_id=1, source_target_pairs={{0,1},{1,0},{2,3},{3,2},{4,5},{5,4},{6,7},{7,6},{8,9},{9,8},{10,11... | collective-permute-start | bytes 1572872 | tf_op jit(solution)/shard_map/ppermute | solution.py:314
  39.7 20.4 %collective-permute-start.19 = (bf16[256,1024]{1,0:T(8,128)(2,1)}, bf16[256,1024]{1,0:T(8,128)(2,1)}, u32[]{:S(2)}, u32[]{:S(2)}) collective-permute-start(bf16[256,1024]{1,0:T(8,128)(2,1)} %after.19), channel_id=1, source_target_pairs={{0,1},{1,0},{2,3},{3,2},{4,5},{5,4},{6,7},{7,6},{8,9},{9,8},{10,11... | collective-permute-start | bytes 1572872 | tf_op jit(solution)/shard_map/ppermute | solution.py:314
  40.8 22.0 %collective-permute-start.13 = (bf16[256,1024]{1,0:T(8,128)(2,1)}, bf16[256,1024]{1,0:T(8,128)(2,1)}, u32[]{:S(2)}, u32[]{:S(2)}) collective-permute-start(bf16[256,1024]{1,0:T(8,128)(2,1)} %after.14.refs_4_.refs_0_), channel_id=1, source_target_pairs={{0,4},{4,0},{8,12},{12,8},{16,20},{20,16},{24,28},{28,24},{32,36},... | collective-permute-start | bytes 1572872 | tf_op jit(solution)/shard_map/ppermute | solution.py:311
  42.3 19.4 %collective-permute-start.15 = (bf16[256,1024]{1,0:T(8,128)(2,1)}, bf16[256,1024]{1,0:T(8,128)(2,1)S(1)}, u32[]{:S(2)}, u32[]{:S(2)}) collective-permute-start(bf16[256,1024]{1,0:T(8,128)(2,1)} %after.17.refs_4_), channel_id=1, source_target_pairs={{0,32},{4,36},{8,40},{12,44},{16,48},{20,52},{24,56},{28,60},{32,0... | collective-permute-start | bytes 1572872 | tf_op jit(solution)/shard_map/ppermute | solution.py:311
  48.7 16.1 %collective-permute-start.12 = (bf16[256,1024]{1,0:T(8,128)(2,1)}, bf16[256,1024]{1,0:T(8,128)(2,1)S(1)}, u32[]{:S(2)}, u32[]{:S(2)}) collective-permute-start(bf16[256,1024]{1,0:T(8,128)(2,1)} %far_first.1.token_ref), channel_id=1, source_target_pairs={{0,1},{1,0},{2,3},{3,2},{4,5},{5,4},{6,7},{7,6},{8,9},{9,8},{10,11... | collective-permute-start | bytes 1572872 | tf_op jit(solution)/shard_map/ppermute | solution.py:314
  49.5 26.4 %collective-permute-start.16 = (bf16[256,1024]{1,0:T(8,128)(2,1)S(1)}, bf16[256,1024]{1,0:T(8,128)(2,1)}, u32[]{:S(2)}, u32[]{:S(2)}) collective-permute-start(bf16[256,1024]{1,0:T(8,128)(2,1)S(1)} %copy-done.10), channel_id=1, source_target_pairs={{0,4},{4,0},{8,12},{12,8},{16,20},{20,16},{24,28},{28,24},{32,36},... | collective-permute-start | bytes 1572872 | tf_op jit(solution)/shard_map/ppermute | solution.py:311
  60.0 14.1 %collective-permute-start.20 = (bf16[256,1024]{1,0:T(8,128)(2,1)}, bf16[256,1024]{1,0:T(8,128)(2,1)}, u32[]{:S(2)}, u32[]{:S(2)}) collective-permute-start(bf16[256,1024]{1,0:T(8,128)(2,1)} %after.20.refs_5_.refs_8_), channel_id=1, source_target_pairs={{0,8},{4,12},{8,0},{12,4},{16,24},{20,28},{24,16},{28,20},{32,40},... | collective-permute-start | bytes 1572872 | tf_op jit(solution)/shard_map/ppermute | solution.py:311
  62.5 14.5 %collective-permute-start.17 = (bf16[256,1024]{1,0:T(8,128)(2,1)}, bf16[256,1024]{1,0:T(8,128)(2,1)}, u32[]{:S(2)}, u32[]{:S(2)}) collective-permute-start(bf16[256,1024]{1,0:T(8,128)(2,1)} %after.18.refs_5_), channel_id=1, source_target_pairs={{0,4},{4,0},{8,12},{12,8},{16,20},{20,16},{24,28},{28,24},{32,36},... | collective-permute-start | bytes 1572872 | tf_op jit(solution)/shard_map/ppermute | solution.py:311
  70.2 13.1 %collective-permute-start.24 = (bf16[256,1024]{1,0:T(8,128)(2,1)}, bf16[256,1024]{1,0:T(8,128)(2,1)}, u32[]{:S(2)}, u32[]{:S(2)}) collective-permute-start(bf16[256,1024]{1,0:T(8,128)(2,1)} %after.22), channel_id=1, source_target_pairs={{0,1},{1,0},{2,3},{3,2},{4,5},{5,4},{6,7},{7,6},{8,9},{9,8},{10,11... | collective-permute-start | bytes 1572872 | tf_op jit(solution)/shard_map/ppermute | solution.py:314
  71.3 15.7 %collective-permute-start.21 = (bf16[256,1024]{1,0:T(8,128)(2,1)}, bf16[256,1024]{1,0:T(8,128)(2,1)}, u32[]{:S(2)}, u32[]{:S(2)}) collective-permute-start(bf16[256,1024]{1,0:T(8,128)(2,1)} %after.20.refs_5_.refs_8_), channel_id=1, source_target_pairs={{0,4},{4,0},{8,12},{12,8},{16,20},{20,16},{24,28},{28,24},{32,36},... | collective-permute-start | bytes 1572872 | tf_op jit(solution)/shard_map/ppermute | solution.py:311
  74.1 15.0 %collective-permute-start.18 = (bf16[256,1024]{1,0:T(8,128)(2,1)}, bf16[256,1024]{1,0:T(8,128)(2,1)}, u32[]{:S(2)}, u32[]{:S(2)}) collective-permute-start(bf16[256,1024]{1,0:T(8,128)(2,1)} %copy-done.2), channel_id=1, source_target_pairs={{0,3},{1,2},{2,1},{3,0},{4,7},{5,6},{6,5},{7,4},{8,11},{9,10},{10,... | collective-permute-start | bytes 1572872 | tf_op jit(solution)/shard_map/ppermute | solution.py:317
  75.9 13.2 %collective-permute-start.22 = (bf16[256,1024]{1,0:T(8,128)(2,1)}, bf16[256,1024]{1,0:T(8,128)(2,1)}, u32[]{:S(2)}, u32[]{:S(2)}) collective-permute-start(bf16[256,1024]{1,0:T(8,128)(2,1)} %after.21.refs_6_.refs_9_), channel_id=1, source_target_pairs={{0,4},{4,0},{8,12},{12,8},{16,20},{20,16},{24,28},{28,24},{32,36},... | collective-permute-start | bytes 1572872 | tf_op jit(solution)/shard_map/ppermute | solution.py:311
  83.3 12.2 %collective-permute-start.25 = (bf16[256,1024]{1,0:T(8,128)(2,1)}, bf16[256,1024]{1,0:T(8,128)(2,1)S(1)}, u32[]{:S(2)}, u32[]{:S(2)}) collective-permute-start(bf16[256,1024]{1,0:T(8,128)(2,1)} %after.23.refs_5_.refs_12_), channel_id=1, source_target_pairs={{0,32},{4,36},{8,40},{12,44},{16,48},{20,52},{24,56},{28,60},{32,0... | collective-permute-start | bytes 1572872 | tf_op jit(solution)/shard_map/ppermute | solution.py:311
  84.6 17.0 %collective-permute-start.23 = (bf16[256,1024]{1,0:T(8,128)(2,1)}, bf16[256,1024]{1,0:T(8,128)(2,1)}, u32[]{:S(2)}, u32[]{:S(2)}) collective-permute-start(bf16[256,1024]{1,0:T(8,128)(2,1)} %copy-done.4), channel_id=1, source_target_pairs={{0,3},{1,2},{2,1},{3,0},{4,7},{5,6},{6,5},{7,4},{8,11},{9,10},{10,... | collective-permute-start | bytes 1572872 | tf_op jit(solution)/shard_map/ppermute | solution.py:317
  87.0 14.6 %collective-permute-start.26 = (bf16[256,1024]{1,0:T(8,128)(2,1)}, bf16[256,1024]{1,0:T(8,128)(2,1)}, u32[]{:S(2)}, u32[]{:S(2)}) collective-permute-start(bf16[256,1024]{1,0:T(8,128)(2,1)} %after.23.refs_5_.refs_12_), channel_id=1, source_target_pairs={{0,4},{4,0},{8,12},{12,8},{16,20},{20,16},{24,28},{28,24},{32,36},... | collective-permute-start | bytes 1572872 | tf_op jit(solution)/shard_map/ppermute | solution.py:311
  98.6 13.7 %collective-permute-start.28 = (bf16[256,1024]{1,0:T(8,128)(2,1)}, bf16[256,1024]{1,0:T(8,128)(2,1)S(1)}, u32[]{:S(2)}, u32[]{:S(2)}) collective-permute-start(bf16[256,1024]{1,0:T(8,128)(2,1)} %after.25), channel_id=1, source_target_pairs={{0,1},{1,0},{2,3},{3,2},{4,5},{5,4},{6,7},{7,6},{8,9},{9,8},{10,11... | collective-permute-start | bytes 1572872 | tf_op jit(solution)/shard_map/ppermute | solution.py:314
  99.8 14.6 %collective-permute-start.29 = (bf16[256,1024]{1,0:T(8,128)(2,1)}, bf16[256,1024]{1,0:T(8,128)(2,1)S(1)}, u32[]{:S(2)}, u32[]{:S(2)}) collective-permute-start(bf16[256,1024]{1,0:T(8,128)(2,1)} %copy-done.21), channel_id=1, source_target_pairs={{0,3},{1,2},{2,1},{3,0},{4,7},{5,6},{6,5},{7,4},{8,11},{9,10},{10,... | collective-permute-start | bytes 1572872 | tf_op jit(solution)/shard_map/ppermute | solution.py:317
  107.3 18.3 %collective-permute-start.30 = (bf16[256,1024]{1,0:T(8,128)(2,1)S(1)}, bf16[256,1024]{1,0:T(8,128)(2,1)S(1)}, u32[]{:S(2)}, u32[]{:S(2)}) collective-permute-start(bf16[256,1024]{1,0:T(8,128)(2,1)S(1)} %across3.1.token_ref), channel_id=1, source_target_pairs={{0,3},{1,2},{2,1},{3,0},{4,7},{5,6},{6,5},{7,4},{8,11},{9,10},{10,... | collective-permute-start | bytes 1572872 | tf_op jit(solution)/shard_map/ppermute | solution.py:317
  (44 other events, 230.9 us)

commit v4 on v3

--- a/solution.py
+++ b/solution.py
@@ -61,7 +61,7 @@
 
 
 def state_kernel(
-    s_ref, k_hbm, v_hbm, w_hbm, total_ref, local_ref, w0_hbm, w1_hbm, k_buf, v_buf, acc, sems
+    s_ref, k_hbm, v_hbm, w_hbm, total_ref, local_ref, w0_ref, w1_hbm, k_buf, v_buf, acc, w1_buf, sems
 ):
     heads = total_ref.shape[0]
     copies = []
@@ -75,7 +75,7 @@
                 ]
             )
         )
-    slices = start_all(slice_copies((0, 1), s_ref, w_hbm, (w0_hbm, w1_hbm), sems, 8))
+    slices = start_all(slice_copies((0, 1), s_ref, w_hbm, (w0_ref, w1_buf), sems, 8))
     for stretch in range(4):
         rows = slice(stretch * C, (stretch + 1) * C)
         wait_all(copies[stretch])
@@ -94,12 +94,16 @@
                 local_ref[head, 1] = state.astype(BF)
             else:
                 total_ref[head] = (acc[head] + state).astype(BF)
-    wait_all(slices)
+        if stretch == 1:
+            wait_all(slices)
+            store = pltpu.make_async_copy(w1_buf, w1_hbm, sems.at[10])
+            store.start()
+    store.wait()
 
 
 def local_kernel(
-    s_ref, q_hbm, k_hbm, v_hbm, w_hbm, g_ref, local_ref, token_ref, out_hbm, w2_ref, w3_ref,
-    q_buf, k_buf, v_buf, out_buf, sems
+    s_ref, q_hbm, k_hbm, v_hbm, w_hbm, g_ref, local_ref, token_ref, out_hbm, w2_hbm, w3_hbm,
+    q_buf, k_buf, v_buf, out_buf, w2_buf, w3_buf, sems
 ):
     copies = []
     for stretch in range(4):
@@ -114,7 +118,7 @@
                 ]
             )
         )
-    slices = start_all(slice_copies((2, 3), s_ref, w_hbm, (w2_ref, w3_ref), sems, 16))
+    slices = start_all(slice_copies((2, 3), s_ref, w_hbm, (w2_buf, w3_buf), sems, 16))
     causal = lax.broadcasted_iota(jnp.int32, (C, C), 0) <= lax.broadcasted_iota(
         jnp.int32, (C, C), 1
     )
@@ -138,8 +142,12 @@
         )
         store.start()
         stores.append(store)
+        if stretch == 1:
+            wait_all(slices)
+            for n, (buf, out) in enumerate(((w2_buf, w2_hbm), (w3_buf, w3_hbm))):
+                stores.append(pltpu.make_async_copy(buf, out, sems.at[18 + n]))
+                stores[-1].start()
     wait_all(stores)
-    wait_all(slices)
 
 
 def far_block(s_ref, q_ref, comb_ref, g_ref, core_ref, zo_ref, yo_ref, zs_ref, ys_ref, out_ref):
@@ -179,10 +187,6 @@
     @pl.when(pl.program_id(0) > 0)
     def _():
         keep_ref[0] = buf[...]
-
-
-def gate_kernel(data_ref, token_ref, out_ref):
-    pass
 
 
 def weight_copies(chunk, s_ref, w_hbm, pieces, dst, size, cols, sems, first):
@@ -316,32 +320,36 @@
     def across(array):
         return lax.ppermute(array, "head", [(i, 3 - i) for i in range(4)])
 
-    def after(array, token):
+    def after(array, *tokens, space=jax.ShapeDtypeStruct):
+        def kernel(*refs):
+            pass
+
         return pl.pallas_call(
-            gate_kernel,
-            in_specs=[any_spec, any_spec],
+            kernel,
+            in_specs=[any_spec] * (1 + len(tokens)),
             out_specs=any_spec,
-            out_shape=jax.ShapeDtypeStruct(array.shape, array.dtype),
+            out_shape=space(array.shape, array.dtype),
             input_output_aliases={0: 0},
             name="after",
-        )(array, token)
+        )(array, *tokens)
 
     piece_shape = jax.ShapeDtypeStruct((width // 4, chunk), BF)
     total, local, slice0, slice1 = pl.pallas_call(
         state_kernel,
         in_specs=[smem_spec, any_spec, any_spec, any_spec],
-        out_specs=[vmem_spec] * 4,
+        out_specs=[vmem_spec] * 3 + [any_spec],
         out_shape=[
             jax.ShapeDtypeStruct((heads, DH, DH), BF),
             jax.ShapeDtypeStruct((heads, 3, DH, DH), BF),
             piece_shape,
-            piece_shape,
+            pltpu.HBM((width // 4, chunk), BF),
         ],
         scratch_shapes=[
             pltpu.VMEM((tokens, width), BF),
             pltpu.VMEM((tokens, width), BF),
             pltpu.VMEM((heads, DH, DH), F32),
-            dma((10,)),
+            pltpu.VMEM((width // 4, chunk), BF),
+            dma((11,)),
         ],
         cost_estimate=cost(2 * tokens * width * DH, 7 << 20),
         compiler_params=params(),
@@ -354,26 +362,31 @@
     fetched = [near(slice0)]
     chip = add(pick(total), pick(sibling)).astype(BF)
     z1, z2, z3 = (ctx_swap(chip, step) for step in (2, 4, 6))
-    fetched.append(near(after(slice1, chip)))
+    fetched.append(near(after(slice1, chip, space=pltpu.HBM)))
 
     combined, slice2, slice3 = pl.pallas_call(
         local_kernel,
         in_specs=[smem_spec] + [any_spec] * 4 + [vmem_spec] * 2 + [any_spec],
-        out_specs=[any_spec, vmem_spec, vmem_spec],
-        out_shape=[pltpu.HBM((stretches, width, C), F32), piece_shape, piece_shape],
+        out_specs=[any_spec] * 3,
+        out_shape=[pltpu.HBM((stretches, width, C), F32)] + [pltpu.HBM((width // 4, chunk), BF)] * 2,
         scratch_shapes=[
             pltpu.VMEM((tokens, width), BF),
             pltpu.VMEM((tokens, width), BF),
             pltpu.VMEM((tokens, width), BF),
             pltpu.VMEM((stretches, width, C), F32),
-            dma((18,)),
+            pltpu.VMEM((width // 4, chunk), BF),
+            pltpu.VMEM((width // 4, chunk), BF),
+            dma((20,)),
         ],
         cost_estimate=cost(12 * tokens * width * DH, 12 << 20),
         compiler_params=params(),
         name="local",
     )(scalars, query_rows, key_rows, value_rows, out_weight, level_gate, local, chip)
+    combined = hbm(combined)
     z3 = after(z3, combined)
-    z_own = jnp.stack([z1, add(z2, z3).astype(BF)])
+    first_of_two = lax.broadcasted_iota(jnp.int32, (2, half, DH, DH), 0) == 0
+    pair = lambda one, *two: jnp.where(first_of_two, one[None], add(*two).astype(BF)[None])
+    z_own = pair(z1, z2, z3)
     row = add(chip, z1, z2, z3).astype(BF)
     y1, y2, y3 = (ctx_swap(row, step) for step in (8, 16, 24))
     z_sib = ctx_swap(z_own, 1)
@@ -383,15 +396,16 @@
         other = after(ctx_swap(mine, 1 << STEP_BITS[i]), second_token)
         return (mine, other, ctx_swap(mine, 1), ctx_swap(other, 1))
 
-    y_own = jnp.stack([y1, add(y2, y3).astype(BF)])
+    y_own = pair(y1, y2, y3)
     y_sib = ctx_swap(y_own, 1)
-    fetched.append(near(after(slice2, z_own)))
+    fetched.append(near(after(slice2, z_own, space=pltpu.HBM)))
     pieces = [gather(0, z_own, y_own)]
 
     def far_norm(first, token):
         count = 1 if first else 3
         base = 6 if first else 7
         block = (C, width)
+        full = lambda *shape: pl.BlockSpec(shape, lambda i, s: (0,) * len(shape))
         return pl.pallas_call(
             far_first_kernel if first else far_rest_kernel,
             grid_spec=pltpu.PrefetchScalarGridSpec(
@@ -403,7 +417,7 @@
                     pl.BlockSpec((1, width, C), lambda i, s: (s[base + i], 0, 0)),
                     pl.BlockSpec((levels, heads, C), lambda i, s: (0, 0, s[base + i])),
                 ]
-                + [vmem_spec] * 5,
+                + [full(heads, DH, DH)] + [full(2, half, DH, DH)] * 4,
                 out_specs=[pl.BlockSpec(block, lambda i, s: (0, 0))]
                 + (
                     []
@@ -421,8 +435,9 @@
         )
 
     (first,) = far_norm(True, pieces[0][3])
+    first = hbm(first)
     got_across = near(first)
-    near_rows, keep = far_norm(False, first)
+    near_rows, keep = map(hbm, far_norm(False, first))
 
     def project(i, tokens):
         def kernel(s_ref, *refs):
@@ -446,7 +461,7 @@
     partials = [project(0, [keep])]
     received = [across(partials[0])]
     pieces.append(gather(1, y_own, keep))
-    fetched.append(near(after(slice3, partials[0])))
+    fetched.append(near(after(slice3, partials[0], space=pltpu.HBM)))
     pieces.append(gather(2, keep, partials[0]))
     partials.append(project(1, [partials[0]]))
     received.append(across(partials[1]))

time: 127 us -> 141 us (1.11)
  waiting for transfers between devices: 21.7 us -> 38.9 us
  local copies, waits for them, and re-layouts: 17 us -> 13.3 us
  Pallas kernels: 45.2 us -> 47.6 us
  starting transfers between devices: 39.9 us -> 38.4 us
    ppermute x6, waiting for transfers between devices: 7.27 us -> 18.1 us  [near(): return lax.ppermute(array, 'head', [(i, i ^ 1) for i in range(4)])]
    ppermute x21, waiting for transfers between devices: 9.59 us -> 15.9 us  [ctx_swap(): return lax.ppermute(array, 'ctx', [(i, i ^ step) for i in range(ctx_size)])]
    unnamed x74 -> x68, local copies, waits for them, and re-layouts: 16.9 us -> 13.2 us
    ppermute x21, starting transfers between devices: 25.5 us -> 23.7 us  [ctx_swap(): return lax.ppermute(array, 'ctx', [(i, i ^ step) for i in range(ctx_size)])]
    another operation x3 -> x0, other arithmetic: 1.49 us -> none  [the longest x2 0.76 us: on_device(): y_own = jnp.stack([y1, add(y2, y3).astype(BF)])]
  transfers between devices with their start and end apart: 31 -> 31, of which waited for: 11 -> 11; matrix products, arithmetic and copies ran while one was open for 2% -> 1% of each run, Pallas kernels for 32% -> 30%
where the time goes in v4:
time: 141 us
  Pallas kernels  47.6 us (34%)
  waiting for transfers between devices  38.9 us (28%)
  starting transfers between devices  38.4 us (27%)
  local copies, waits for them, and re-layouts  13.3 us (9%)
  other arithmetic  1.98 us (1%)
    ppermute x21, starting transfers between devices, ctx_swap(): return lax.ppermute(array, 'ctx', [(i, i ^ step) for i in range(ctx_size)])  23.7 us
    ppermute x6, waiting for transfers between devices, near(): return lax.ppermute(array, 'head', [(i, i ^ 1) for i in range(4)])  18.1 us
    ppermute x21, waiting for transfers between devices, ctx_swap(): return lax.ppermute(array, 'ctx', [(i, i ^ step) for i in range(ctx_size)])  15.9 us
    pallas_call x4, Pallas kernels, project(): pl.pallas_call(kernel, in_specs=[smem_spec] + [any_spec] * (7 + len(token...  15.1 us
    unnamed x68, local copies, waits for them, and re-layouts  13.2 us
    pallas_call x2, Pallas kernels, far_norm(): pl.pallas_call(far_first_kernel if first else far_rest_kernel, grid_spec=...  10.3 us
    pallas_call x1, Pallas kernels, on_device(): pl.pallas_call(local_kernel, in_specs=[smem_spec] + [any_spec] * 4 + [vme...  8.98 us
    pallas_call x1, Pallas kernels, on_device(): pl.pallas_call(own_kernel, in_specs=[smem_spec] + [any_spec] * (4 + 4 * C...  8.41 us
  transfers between devices with their start and end apart: 31, of which 11 were waited for; matrix products, arithmetic and copies ran while one was open for 1% of the time, Pallas kernels for 30%

profile of v4, /device:TPU:1, one launch (start us, length us, event | category | flops | bytes accessed | tf_op | source)
XLA Modules:
  0.0 140.5 jit_solution(8037713548137835153)
XLA Ops:
  0.1 3.9 %states.1 = (bf16[8,128,128]{2,1,0:T(8,128)(2,1)S(1)}, bf16[8,3,128,128]{3,2,1,0:T(8,128)(2,1)S(1)}, bf16[256,1024]{1,0:T(8,128)(2,1)S(1)}, bf16[256,1024]{1,0:T(8,128)(2,1)}) custom-call(s32[10]{0:T(128)S(1)} %stack.40.s_ref, bf16[1024,1024]{1,0:T(8,128)(2,1)} %k_hbm.3, bf16[1024,1024]{1,0:T(8,128)(2,1)} %v_hbm.3, bf16[1024,4096]{1,0:T(8,128)(2,1)} %w_hbm.5), custom_call_target="tpu_custom_call" | custom-call | flops 65536 | bytes 1792 | tf_op jit(solution)/shard_map/states/pallas_call | solution.py:337
  6.7 3.9 %collective-permute-start.4 = (bf16[4,128,128]{2,1,0:T(8,128)(2,1)S(1)}, bf16[4,128,128]{2,1,0:T(8,128)(2,1)S(1)}, u32[]{:S(2)}, u32[]{:S(2)}) collective-permute-start(bf16[4,128,128]{2,1,0:T(8,128)(2,1)S(1)} %add_convert_fusion.1.token_ref.refs_1_), channel_id=1, source_target_pairs={{0,24},{4,28},{8,16},{12,20},{16,8},{20,12},{24,0},{28,4},{32,56},... | collective-permute-start | bytes 393224 | tf_op jit(solution)/shard_map/ppermute | solution.py:315
  11.3 9.0 %local.1 = (f32[4,1024,256]{2,1,0:T(8,128)}, bf16[256,1024]{1,0:T(8,128)(2,1)}, bf16[256,1024]{1,0:T(8,128)(2,1)}) custom-call(s32[10]{0:T(128)S(1)} %stack.40.s_ref, bf16[1024,1024]{1,0:T(8,128)(2,1)} %refs_0_.3, bf16[1024,1024]{1,0:T(8,128)(2,1)} %k_hbm.3, bf16[1024,1024]{1,0:T(8,128)(2,1)} %v_hbm.3, bf16[1024,4096]{1,0:T(8,128)(2,1)} %w_hbm.5, ...), custom_call_target="tpu_custom_call" | custom-call | flops 393216 | bytes 3072 | tf_op jit(solution)/shard_map/local/pallas_call | solution.py:367
  22.0 2.8 %collective-permute-start.8 = (bf16[4,128,128]{2,1,0:T(8,128)(2,1)S(1)}, bf16[4,128,128]{2,1,0:T(8,128)(2,1)S(1)}, u32[]{:S(2)}, u32[]{:S(2)}) collective-permute-start(bf16[4,128,128]{2,1,0:T(8,128)(2,1)S(1)} %get-tuple-element.27), channel_id=1, source_target_pairs={{0,96},{4,100},{8,104},{12,108},{16,112},{20,116},{24,120},{28,124... | collective-permute-start | bytes 393224 | tf_op jit(solution)/shard_map/ppermute | solution.py:315
  26.7 3.6 %collective-permute-done.8 = bf16[4,128,128]{2,1,0:T(8,128)(2,1)S(1)} collective-permute-done((bf16[4,128,128]{2,1,0:T(8,128)(2,1)S(1)}, bf16[4,128,128]{2,1,0:T(8,128)(2,1)S(1)}, u32[]{:S(2)}, u32[]{:S(2)}) %collective-permute-start.8) | collective-permute-done | bytes 131104 | tf_op jit(solution)/shard_map/ppermute | solution.py:315
  32.0 5.1 %collective-permute-done.refs_0_ = bf16[256,1024]{1,0:T(8,128)(2,1)S(1)} collective-permute-done((bf16[256,1024]{1,0:T(8,128)(2,1)S(1)}, bf16[256,1024]{1,0:T(8,128)(2,1)S(1)}, u32[]{:S(2)}, u32[]{:S(2)}) %collective-permute-start) | collective-permute-done | bytes 524320 | tf_op jit(solution)/shard_map/ppermute | solution.py:318
  39.9 9.2 %collective-permute-done.5.refs_0_ = bf16[256,1024]{1,0:T(8,128)(2,1)S(1)} collective-permute-done((bf16[256,1024]{1,0:T(8,128)(2,1)}, bf16[256,1024]{1,0:T(8,128)(2,1)S(1)}, u32[]{:S(2)}, u32[]{:S(2)}) %collective-permute-start.5) | collective-permute-done | bytes 524320 | tf_op jit(solution)/shard_map/ppermute | solution.py:315
  49.9 3.3 %collective-permute-start.9 = (bf16[256,1024]{1,0:T(8,128)(2,1)}, bf16[256,1024]{1,0:T(8,128)(2,1)S(1)}, u32[]{:S(2)}, u32[]{:S(2)}) collective-permute-start(bf16[256,1024]{1,0:T(8,128)(2,1)} %after.15.refs_5_.refs_1_), channel_id=1, source_target_pairs={{0,4},{4,0},{8,12},{12,8},{16,20},{20,16},{24,28},{28,24},{32,36},... | collective-permute-start | bytes 1572872 | tf_op jit(solution)/shard_map/ppermute | solution.py:315
  58.9 3.8 %far_first.1.token_ref = bf16[256,1024]{1,0:T(8,128)(2,1)} custom-call(s32[10]{0:T(128)S(1)} %stack.40.s_ref, bf16[256,1024]{1,0:T(8,128)(2,1)S(1)} %collective-permute-done.9.token_ref.refs_7_.refs_3_, bf16[1024,1024]{1,0:T(8,128)(2,1)} %refs_0_.3, f32[4,1024,256]{2,1,0:T(8,128)} %get-tuple-element.19.refs_1_, f32[8,8,1024]{2,1,0:T(8,128)S(1)} %copy-done.27, ...), custom_call_target="tpu_custom_call" | custom-call | flops 81920 | bytes 512 | tf_op jit(solution)/shard_map/far_first/pallas_call | solution.py:409
  64.2 6.6 %far_rest.1 = (bf16[256,1024]{1,0:T(8,128)(2,1)}, bf16[2,256,1024]{2,1,0:T(8,128)(2,1)}) custom-call(s32[10]{0:T(128)S(1)} %stack.40.s_ref, bf16[256,1024]{1,0:T(8,128)(2,1)} %far_first.1.token_ref, bf16[1024,1024]{1,0:T(8,128)(2,1)} %refs_0_.3, f32[4,1024,256]{2,1,0:T(8,128)} %get-tuple-element.19.refs_1_, f32[8,8,1024]{2,1,0:T(8,128)S(1)} %copy-done.27, ...), custom_call_target="tpu_custom_call" | custom-call | flops 245760 | bytes 1536 | tf_op jit(solution)/shard_map/far_rest/pallas_call | solution.py:409
  72.7 6.1 %collective-permute-done.12.refs_2_.refs_3_ = bf16[256,1024]{1,0:T(8,128)(2,1)} collective-permute-done((bf16[256,1024]{1,0:T(8,128)(2,1)}, bf16[256,1024]{1,0:T(8,128)(2,1)}, u32[]{:S(2)}, u32[]{:S(2)}) %collective-permute-start.12) | collective-permute-done | bytes 524320 | tf_op jit(solution)/shard_map/ppermute | solution.py:318
  78.8 3.7 %across0.1.refs_0_.refs_1_ = bf16[256,1024]{1,0:T(8,128)(2,1)S(1)} custom-call(s32[10]{0:T(128)S(1)} %stack.40.s_ref, bf16[2,256,1024]{2,1,0:T(8,128)(2,1)} %get-tuple-element.20.refs_0_.refs_1_.refs_2_.keep, bf16[2,256,1024]{2,1,0:T(8,128)(2,1)} %get-tuple-element.20.refs_0_.refs_1_.refs_2_.keep, bf16[256,1024]{1,0:T(8,128)(2,1)} %collective-permute-done.12.refs_2_.refs_3_, ...), custom_call_target="tpu_custom_call" | custom-call | flops 262144 | bytes 1280 | tf_op jit(solution)/shard_map/across0/pallas_call | solution.py:446
  85.7 1.8 %collective-permute-start.18 = (bf16[256,1024]{1,0:T(8,128)(2,1)}, bf16[256,1024]{1,0:T(8,128)(2,1)}, u32[]{:S(2)}, u32[]{:S(2)}) collective-permute-start(bf16[256,1024]{1,0:T(8,128)(2,1)} %copy-done), channel_id=1, source_target_pairs={{0,3},{1,2},{2,1},{3,0},{4,7},{5,6},{6,5},{7,4},{8,11},{9,10},{10,... | collective-permute-start | bytes 1572872 | tf_op jit(solution)/shard_map/ppermute | solution.py:321
  88.0 3.8 %across1.1.refs_0_.refs_1_ = bf16[256,1024]{1,0:T(8,128)(2,1)S(1)} custom-call(s32[10]{0:T(128)S(1)} %stack.40.s_ref, bf16[256,1024]{1,0:T(8,128)(2,1)S(1)} %copy-done.1, bf16[2,256,1024]{2,1,0:T(8,128)(2,1)} %get-tuple-element.20.refs_0_.refs_1_.refs_2_.keep, bf16[256,1024]{1,0:T(8,128)(2,1)} %collective-permute-done.12.refs_2_.refs_3_, ...), custom_call_target="tpu_custom_call" | custom-call | flops 262144 | bytes 1280 | tf_op jit(solution)/shard_map/across1/pallas_call | solution.py:446
  92.6 3.6 %collective-permute-done.24.refs_0_ = bf16[256,1024]{1,0:T(8,128)(2,1)S(1)} collective-permute-done((bf16[256,1024]{1,0:T(8,128)(2,1)}, bf16[256,1024]{1,0:T(8,128)(2,1)S(1)}, u32[]{:S(2)}, u32[]{:S(2)}) %collective-permute-start.24) | collective-permute-done | bytes 524320 | tf_op jit(solution)/shard_map/ppermute | solution.py:318
  97.5 2.5 %collective-permute-start.23 = (bf16[256,1024]{1,0:T(8,128)(2,1)}, bf16[256,1024]{1,0:T(8,128)(2,1)}, u32[]{:S(2)}, u32[]{:S(2)}) collective-permute-start(bf16[256,1024]{1,0:T(8,128)(2,1)} %copy-done.2), channel_id=1, source_target_pairs={{0,3},{1,2},{2,1},{3,0},{4,7},{5,6},{6,5},{7,4},{8,11},{9,10},{10,... | collective-permute-start | bytes 1572872 | tf_op jit(solution)/shard_map/ppermute | solution.py:321
  100.0 2.2 %collective-permute-start.26 = (bf16[256,1024]{1,0:T(8,128)(2,1)}, bf16[256,1024]{1,0:T(8,128)(2,1)}, u32[]{:S(2)}, u32[]{:S(2)}) collective-permute-start(bf16[256,1024]{1,0:T(8,128)(2,1)} %after.23.refs_5_.refs_12_), channel_id=1, source_target_pairs={{0,4},{4,0},{8,12},{12,8},{16,20},{20,16},{24,28},{28,24},{32,36},... | collective-permute-start | bytes 1572872 | tf_op jit(solution)/shard_map/ppermute | solution.py:315
  103.2 3.8 %across2.1.refs_1_.refs_0_ = bf16[256,1024]{1,0:T(8,128)(2,1)S(1)} custom-call(s32[10]{0:T(128)S(1)} %stack.40.s_ref, bf16[256,1024]{1,0:T(8,128)(2,1)S(1)} %copy-done.3, bf16[256,1024]{1,0:T(8,128)(2,1)} %collective-permute-done.18.refs_1_.refs_16_, bf16[2,256,1024]{2,1,0:T(8,128)(2,1)} %get-tuple-element.20.refs_0_.refs_1_.refs_2_.keep, ...), custom_call_target="tpu_custom_call" | custom-call | flops 262144 | bytes 1280 | tf_op jit(solution)/shard_map/across2/pallas_call | solution.py:446
  109.9 2.5 %collective-permute-start.27 = (bf16[256,1024]{1,0:T(8,128)(2,1)}, bf16[256,1024]{1,0:T(8,128)(2,1)}, u32[]{:S(2)}, u32[]{:S(2)}) collective-permute-start(bf16[256,1024]{1,0:T(8,128)(2,1)} %after.24.refs_6_.refs_13_), channel_id=1, source_target_pairs={{0,4},{4,0},{8,12},{12,8},{16,20},{20,16},{24,28},{28,24},{32,36},... | collective-permute-start | bytes 1572872 | tf_op jit(solution)/shard_map/ppermute | solution.py:315
  117.5 3.8 %across3.1.token_ref = bf16[256,1024]{1,0:T(8,128)(2,1)S(1)} custom-call(s32[10]{0:T(128)S(1)} %stack.40.s_ref, bf16[256,1024]{1,0:T(8,128)(2,1)S(1)} %copy-done.26, bf16[256,1024]{1,0:T(8,128)(2,1)} %collective-permute-done.23.refs_1_.refs_17_, bf16[2,256,1024]{2,1,0:T(8,128)(2,1)} %get-tuple-element.20.refs_0_.refs_1_.refs_2_.keep, ...), custom_call_target="tpu_custom_call" | custom-call | flops 262144 | bytes 1280 | tf_op jit(solution)/shard_map/across3/pallas_call | solution.py:446
  122.9 3.2 %collective-permute-done.28.got = bf16[256,1024]{1,0:T(8,128)(2,1)S(1)} collective-permute-done((bf16[256,1024]{1,0:T(8,128)(2,1)}, bf16[256,1024]{1,0:T(8,128)(2,1)S(1)}, u32[]{:S(2)}, u32[]{:S(2)}) %collective-permute-start.28) | collective-permute-done | bytes 524320 | tf_op jit(solution)/shard_map/ppermute | solution.py:318
  126.1 2.1 %collective-permute-done.29.refs_18_ = bf16[256,1024]{1,0:T(8,128)(2,1)S(1)} collective-permute-done((bf16[256,1024]{1,0:T(8,128)(2,1)}, bf16[256,1024]{1,0:T(8,128)(2,1)S(1)}, u32[]{:S(2)}, u32[]{:S(2)}) %collective-permute-start.29) | collective-permute-done | bytes 524320 | tf_op jit(solution)/shard_map/ppermute | solution.py:321
  128.2 8.4 %own.1 = (bf16[256,4096]{1,0:T(8,128)(2,1)}, f32[256,1024]{1,0:T(8,128)S(1)}) custom-call(s32[10]{0:T(128)S(1)} %stack.40.s_ref, bf16[256,1024]{1,0:T(8,128)(2,1)S(1)} %across3.1.token_ref, bf16[2,256,1024]{2,1,0:T(8,128)(2,1)} %get-tuple-element.20.refs_0_.refs_1_.refs_2_.keep, bf16[256,1024]{1,0:T(8,128)(2,1)S(1)} %collective-permute-done.28.got, ...), custom_call_target="tpu_custom_call" | custom-call | flops 1048576 | bytes 5120 | tf_op jit(solution)/shard_map/own/pallas_call | solution.py:475
  136.7 2.8 %collective-permute-done.30.got_ref = bf16[256,1024]{1,0:T(8,128)(2,1)S(1)} collective-permute-done((bf16[256,1024]{1,0:T(8,128)(2,1)S(1)}, bf16[256,1024]{1,0:T(8,128)(2,1)S(1)}, u32[]{:S(2)}, u32[]{:S(2)}) %collective-permute-start.30) | collective-permute-done | bytes 524320 | tf_op jit(solution)/shard_map/ppermute | solution.py:321
  (135 shorter events, 38.6 us)
Async XLA Ops:
  6.7 13.6 %collective-permute-start.4 = (bf16[4,128,128]{2,1,0:T(8,128)(2,1)S(1)}, bf16[4,128,128]{2,1,0:T(8,128)(2,1)S(1)}, u32[]{:S(2)}, u32[]{:S(2)}) collective-permute-start(bf16[4,128,128]{2,1,0:T(8,128)(2,1)S(1)} %add_convert_fusion.1.token_ref.refs_1_), channel_id=1, source_target_pairs={{0,24},{4,28},{8,16},{12,20},{16,8},{20,12},{24,0},{28,4},{32,56},... | collective-permute-start | bytes 393224 | tf_op jit(solution)/shard_map/ppermute | solution.py:315
  10.6 10.4 %collective-permute-start.3 = (bf16[4,128,128]{2,1,0:T(8,128)(2,1)S(1)}, bf16[4,128,128]{2,1,0:T(8,128)(2,1)S(1)}, u32[]{:S(2)}, u32[]{:S(2)}) collective-permute-start(bf16[4,128,128]{2,1,0:T(8,128)(2,1)S(1)} %add_convert_fusion.1.token_ref.refs_1_), channel_id=1, source_target_pairs={{0,16},{4,20},{8,24},{12,28},{16,0},{20,4},{24,8},{28,12},{32,48},... | collective-permute-start | bytes 393224 | tf_op jit(solution)/shard_map/ppermute | solution.py:315
  10.6 10.4 %collective-permute-start.2 = (bf16[4,128,128]{2,1,0:T(8,128)(2,1)S(1)}, bf16[4,128,128]{2,1,0:T(8,128)(2,1)S(1)}, u32[]{:S(2)}, u32[]{:S(2)}) collective-permute-start(bf16[4,128,128]{2,1,0:T(8,128)(2,1)S(1)} %add_convert_fusion.1.token_ref.refs_1_), channel_id=1, source_target_pairs={{0,8},{4,12},{8,0},{12,4},{16,24},{20,28},{24,16},{28,20},{32,40},... | collective-permute-start | bytes 393224 | tf_op jit(solution)/shard_map/ppermute | solution.py:315
  22.0 8.3 %collective-permute-start.8 = (bf16[4,128,128]{2,1,0:T(8,128)(2,1)S(1)}, bf16[4,128,128]{2,1,0:T(8,128)(2,1)S(1)}, u32[]{:S(2)}, u32[]{:S(2)}) collective-permute-start(bf16[4,128,128]{2,1,0:T(8,128)(2,1)S(1)} %get-tuple-element.27), channel_id=1, source_target_pairs={{0,96},{4,100},{8,104},{12,108},{16,112},{20,116},{24,120},{28,124... | collective-permute-start | bytes 393224 | tf_op jit(solution)/shard_map/ppermute | solution.py:315
  25.2 11.9 %collective-permute-start = (bf16[256,1024]{1,0:T(8,128)(2,1)S(1)}, bf16[256,1024]{1,0:T(8,128)(2,1)S(1)}, u32[]{:S(2)}, u32[]{:S(2)}) collective-permute-start(bf16[256,1024]{1,0:T(8,128)(2,1)S(1)} %get-tuple-element.16), channel_id=1, source_target_pairs={{0,1},{1,0},{2,3},{3,2},{4,5},{5,4},{6,7},{7,6},{8,9},{9,8},{10,11... | collective-permute-start | bytes 1572872 | tf_op jit(solution)/shard_map/ppermute | solution.py:318
  37.9 11.2 %collective-permute-start.5 = (bf16[256,1024]{1,0:T(8,128)(2,1)}, bf16[256,1024]{1,0:T(8,128)(2,1)S(1)}, u32[]{:S(2)}, u32[]{:S(2)}) collective-permute-start(bf16[256,1024]{1,0:T(8,128)(2,1)} %after.14.refs_4_.refs_0_), channel_id=1, source_target_pairs={{0,8},{4,12},{8,0},{12,4},{16,24},{20,28},{24,16},{28,20},{32,40},... | collective-permute-start | bytes 1572872 | tf_op jit(solution)/shard_map/ppermute | solution.py:315
  38.7 16.3 %collective-permute-start.14 = (bf16[256,1024]{1,0:T(8,128)(2,1)}, bf16[256,1024]{1,0:T(8,128)(2,1)S(1)}, u32[]{:S(2)}, u32[]{:S(2)}) collective-permute-start(bf16[256,1024]{1,0:T(8,128)(2,1)} %after.16), channel_id=1, source_target_pairs={{0,1},{1,0},{2,3},{3,2},{4,5},{5,4},{6,7},{7,6},{8,9},{9,8},{10,11... | collective-permute-start | bytes 1572872 | tf_op jit(solution)/shard_map/ppermute | solution.py:318
  53.8 17.0 %collective-permute-start.19 = (bf16[256,1024]{1,0:T(8,128)(2,1)}, bf16[256,1024]{1,0:T(8,128)(2,1)}, u32[]{:S(2)}, u32[]{:S(2)}) collective-permute-start(bf16[256,1024]{1,0:T(8,128)(2,1)} %after.19), channel_id=1, source_target_pairs={{0,1},{1,0},{2,3},{3,2},{4,5},{5,4},{6,7},{7,6},{8,9},{9,8},{10,11... | collective-permute-start | bytes 1572872 | tf_op jit(solution)/shard_map/ppermute | solution.py:318
  55.0 17.7 %collective-permute-start.13 = (bf16[256,1024]{1,0:T(8,128)(2,1)S(1)}, bf16[256,1024]{1,0:T(8,128)(2,1)}, u32[]{:S(2)}, u32[]{:S(2)}) collective-permute-start(bf16[256,1024]{1,0:T(8,128)(2,1)S(1)} %copy-done.20), channel_id=1, source_target_pairs={{0,4},{4,0},{8,12},{12,8},{16,20},{20,16},{24,28},{28,24},{32,36},... | collective-permute-start | bytes 1572872 | tf_op jit(solution)/shard_map/ppermute | solution.py:315
  56.5 15.1 %collective-permute-start.15 = (bf16[256,1024]{1,0:T(8,128)(2,1)}, bf16[256,1024]{1,0:T(8,128)(2,1)S(1)}, u32[]{:S(2)}, u32[]{:S(2)}) collective-permute-start(bf16[256,1024]{1,0:T(8,128)(2,1)} %after.17.refs_4_), channel_id=1, source_target_pairs={{0,32},{4,36},{8,40},{12,44},{16,48},{20,52},{24,56},{28,60},{32,0... | collective-permute-start | bytes 1572872 | tf_op jit(solution)/shard_map/ppermute | solution.py:315
  62.7 16.2 %collective-permute-start.12 = (bf16[256,1024]{1,0:T(8,128)(2,1)}, bf16[256,1024]{1,0:T(8,128)(2,1)}, u32[]{:S(2)}, u32[]{:S(2)}) collective-permute-start(bf16[256,1024]{1,0:T(8,128)(2,1)} %far_first.1.token_ref), channel_id=1, source_target_pairs={{0,1},{1,0},{2,3},{3,2},{4,5},{5,4},{6,7},{7,6},{8,9},{9,8},{10,11... | collective-permute-start | bytes 1572872 | tf_op jit(solution)/shard_map/ppermute | solution.py:318
  63.5 24.0 %collective-permute-start.16 = (bf16[256,1024]{1,0:T(8,128)(2,1)S(1)}, bf16[256,1024]{1,0:T(8,128)(2,1)}, u32[]{:S(2)}, u32[]{:S(2)}) collective-permute-start(bf16[256,1024]{1,0:T(8,128)(2,1)S(1)} %copy-done.9), channel_id=1, source_target_pairs={{0,4},{4,0},{8,12},{12,8},{16,20},{20,16},{24,28},{28,24},{32,36},... | collective-permute-start | bytes 1572872 | tf_op jit(solution)/shard_map/ppermute | solution.py:315
  70.8 14.9 %collective-permute-start.20 = (bf16[256,1024]{1,0:T(8,128)(2,1)}, bf16[256,1024]{1,0:T(8,128)(2,1)S(1)}, u32[]{:S(2)}, u32[]{:S(2)}) collective-permute-start(bf16[256,1024]{1,0:T(8,128)(2,1)} %after.20.refs_5_.refs_8_), channel_id=1, source_target_pairs={{0,8},{4,12},{8,0},{12,4},{16,24},{20,28},{24,16},{28,20},{32,40},... | collective-permute-start | bytes 1572872 | tf_op jit(solution)/shard_map/ppermute | solution.py:315
  72.5 15.5 %collective-permute-start.17 = (bf16[256,1024]{1,0:T(8,128)(2,1)}, bf16[256,1024]{1,0:T(8,128)(2,1)}, u32[]{:S(2)}, u32[]{:S(2)}) collective-permute-start(bf16[256,1024]{1,0:T(8,128)(2,1)} %after.18.refs_5_), channel_id=1, source_target_pairs={{0,4},{4,0},{8,12},{12,8},{16,20},{20,16},{24,28},{28,24},{32,36},... | collective-permute-start | bytes 1572872 | tf_op jit(solution)/shard_map/ppermute | solution.py:315
  83.3 12.9 %collective-permute-start.24 = (bf16[256,1024]{1,0:T(8,128)(2,1)}, bf16[256,1024]{1,0:T(8,128)(2,1)S(1)}, u32[]{:S(2)}, u32[]{:S(2)}) collective-permute-start(bf16[256,1024]{1,0:T(8,128)(2,1)} %after.22), channel_id=1, source_target_pairs={{0,1},{1,0},{2,3},{3,2},{4,5},{5,4},{6,7},{7,6},{8,9},{9,8},{10,11... | collective-permute-start | bytes 1572872 | tf_op jit(solution)/shard_map/ppermute | solution.py:318
  84.5 15.4 %collective-permute-start.21 = (bf16[256,1024]{1,0:T(8,128)(2,1)}, bf16[256,1024]{1,0:T(8,128)(2,1)}, u32[]{:S(2)}, u32[]{:S(2)}) collective-permute-start(bf16[256,1024]{1,0:T(8,128)(2,1)} %after.20.refs_5_.refs_8_), channel_id=1, source_target_pairs={{0,4},{4,0},{8,12},{12,8},{16,20},{20,16},{24,28},{28,24},{32,36},... | collective-permute-start | bytes 1572872 | tf_op jit(solution)/shard_map/ppermute | solution.py:315
  85.7 16.5 %collective-permute-start.18 = (bf16[256,1024]{1,0:T(8,128)(2,1)}, bf16[256,1024]{1,0:T(8,128)(2,1)}, u32[]{:S(2)}, u32[]{:S(2)}) collective-permute-start(bf16[256,1024]{1,0:T(8,128)(2,1)} %copy-done), channel_id=1, source_target_pairs={{0,3},{1,2},{2,1},{3,0},{4,7},{5,6},{6,5},{7,4},{8,11},{9,10},{10,... | collective-permute-start | bytes 1572872 | tf_op jit(solution)/shard_map/ppermute | solution.py:321
  87.5 14.7 %collective-permute-start.22 = (bf16[256,1024]{1,0:T(8,128)(2,1)}, bf16[256,1024]{1,0:T(8,128)(2,1)}, u32[]{:S(2)}, u32[]{:S(2)}) collective-permute-start(bf16[256,1024]{1,0:T(8,128)(2,1)} %after.21.refs_6_.refs_9_), channel_id=1, source_target_pairs={{0,4},{4,0},{8,12},{12,8},{16,20},{20,16},{24,28},{28,24},{32,36},... | collective-permute-start | bytes 1572872 | tf_op jit(solution)/shard_map/ppermute | solution.py:315
  97.0 12.1 %collective-permute-start.25 = (bf16[256,1024]{1,0:T(8,128)(2,1)}, bf16[256,1024]{1,0:T(8,128)(2,1)S(1)}, u32[]{:S(2)}, u32[]{:S(2)}) collective-permute-start(bf16[256,1024]{1,0:T(8,128)(2,1)} %after.23.refs_5_.refs_12_), channel_id=1, source_target_pairs={{0,32},{4,36},{8,40},{12,44},{16,48},{20,52},{24,56},{28,60},{32,0... | collective-permute-start | bytes 1572872 | tf_op jit(solution)/shard_map/ppermute | solution.py:315
  97.5 17.9 %collective-permute-start.23 = (bf16[256,1024]{1,0:T(8,128)(2,1)}, bf16[256,1024]{1,0:T(8,128)(2,1)}, u32[]{:S(2)}, u32[]{:S(2)}) collective-permute-start(bf16[256,1024]{1,0:T(8,128)(2,1)} %copy-done.2), channel_id=1, source_target_pairs={{0,3},{1,2},{2,1},{3,0},{4,7},{5,6},{6,5},{7,4},{8,11},{9,10},{10,... | collective-permute-start | bytes 1572872 | tf_op jit(solution)/shard_map/ppermute | solution.py:321
  100.0 15.4 %collective-permute-start.26 = (bf16[256,1024]{1,0:T(8,128)(2,1)}, bf16[256,1024]{1,0:T(8,128)(2,1)}, u32[]{:S(2)}, u32[]{:S(2)}) collective-permute-start(bf16[256,1024]{1,0:T(8,128)(2,1)} %after.23.refs_5_.refs_12_), channel_id=1, source_target_pairs={{0,4},{4,0},{8,12},{12,8},{16,20},{20,16},{24,28},{28,24},{32,36},... | collective-permute-start | bytes 1572872 | tf_op jit(solution)/shard_map/ppermute | solution.py:315
  112.4 13.8 %collective-permute-start.28 = (bf16[256,1024]{1,0:T(8,128)(2,1)}, bf16[256,1024]{1,0:T(8,128)(2,1)S(1)}, u32[]{:S(2)}, u32[]{:S(2)}) collective-permute-start(bf16[256,1024]{1,0:T(8,128)(2,1)} %after.25), channel_id=1, source_target_pairs={{0,1},{1,0},{2,3},{3,2},{4,5},{5,4},{6,7},{7,6},{8,9},{9,8},{10,11... | collective-permute-start | bytes 1572872 | tf_op jit(solution)/shard_map/ppermute | solution.py:318
  113.6 14.7 %collective-permute-start.29 = (bf16[256,1024]{1,0:T(8,128)(2,1)}, bf16[256,1024]{1,0:T(8,128)(2,1)S(1)}, u32[]{:S(2)}, u32[]{:S(2)}) collective-permute-start(bf16[256,1024]{1,0:T(8,128)(2,1)} %copy-done.25), channel_id=1, source_target_pairs={{0,3},{1,2},{2,1},{3,0},{4,7},{5,6},{6,5},{7,4},{8,11},{9,10},{10,... | collective-permute-start | bytes 1572872 | tf_op jit(solution)/shard_map/ppermute | solution.py:321
  121.3 18.2 %collective-permute-start.30 = (bf16[256,1024]{1,0:T(8,128)(2,1)S(1)}, bf16[256,1024]{1,0:T(8,128)(2,1)S(1)}, u32[]{:S(2)}, u32[]{:S(2)}) collective-permute-start(bf16[256,1024]{1,0:T(8,128)(2,1)S(1)} %across3.1.token_ref), channel_id=1, source_target_pairs={{0,3},{1,2},{2,1},{3,0},{4,7},{5,6},{6,5},{7,4},{8,11},{9,10},{10,... | collective-permute-start | bytes 1572872 | tf_op jit(solution)/shard_map/ppermute | solution.py:321
  (41 other events, 267.0 us)

commit v5 on v3

--- a/solution.py
+++ b/solution.py
@@ -372,6 +372,7 @@
         compiler_params=params(),
         name="local",
     )(scalars, query_rows, key_rows, value_rows, out_weight, level_gate, local, chip)
+    combined = hbm(combined)
     z3 = after(z3, combined)
     z_own = jnp.stack([z1, add(z2, z3).astype(BF)])
     row = add(chip, z1, z2, z3).astype(BF)
@@ -392,6 +393,7 @@
         count = 1 if first else 3
         base = 6 if first else 7
         block = (C, width)
+        full = lambda *shape: pl.BlockSpec(shape, lambda i, s: (0,) * len(shape))
         return pl.pallas_call(
             far_first_kernel if first else far_rest_kernel,
             grid_spec=pltpu.PrefetchScalarGridSpec(
@@ -403,7 +405,7 @@
                     pl.BlockSpec((1, width, C), lambda i, s: (s[base + i], 0, 0)),
                     pl.BlockSpec((levels, heads, C), lambda i, s: (0, 0, s[base + i])),
                 ]
-                + [vmem_spec] * 5,
+                + [full(heads, DH, DH)] + [full(2, half, DH, DH)] * 4,
                 out_specs=[pl.BlockSpec(block, lambda i, s: (0, 0))]
                 + (
                     []
@@ -420,9 +422,10 @@
             scalars, token, query_rows, combined, level_gate, sibling, z_own, y_own, z_sib, y_sib
         )
 
-    (first,) = far_norm(True, pieces[0][3])
+    (first,) = far_norm(True, y_own)
+    first = hbm(first)
     got_across = near(first)
-    near_rows, keep = far_norm(False, first)
+    near_rows, keep = map(hbm, far_norm(False, first))
 
     def project(i, tokens):
         def kernel(s_ref, *refs):

time: 127 us -> 127 us (level)
  local copies, waits for them, and re-layouts: 17 us -> 14.6 us
  Pallas kernels: 45.2 us -> 47.1 us
  waiting for transfers between devices: 21.7 us -> 23.5 us
    ppermute x21, starting transfers between devices: 25.5 us -> 28.4 us  [ctx_swap(): return lax.ppermute(array, 'ctx', [(i, i ^ step) for i in range(ctx_size)])]
    unnamed x74 -> x72, local copies, waits for them, and re-layouts: 16.9 us -> 14.5 us
    ppermute x4, starting transfers between devices: 7.6 us -> 5.19 us  [across(): return lax.ppermute(array, 'head', [(i, 3 - i) for i in range(4)])]
    ppermute x6, waiting for transfers between devices: 7.27 us -> 9.35 us  [near(): return lax.ppermute(array, 'head', [(i, i ^ 1) for i in range(4)])]
    pallas_call x2, Pallas kernels: 9.19 us -> 10.5 us  [far_norm(): pl.pallas_call(far_first_kernel if first else far_rest_kernel, grid_spec=...]
    ppermute x6, starting transfers between devices: 6.74 us -> 5.46 us  [near(): return lax.ppermute(array, 'head', [(i, i ^ 1) for i in range(4)])]
  transfers between devices with their start and end apart: 31 -> 31, of which waited for: 11 -> 11; matrix products, arithmetic and copies ran while one was open for 2% -> 1% of each run, Pallas kernels for 32% -> 34%
where the time goes in v5:
time: 127 us; the launch traced here: 126 us
  Pallas kernels  47.1 us (37%)
  starting transfers between devices  39 us (31%)
  waiting for transfers between devices  23.5 us (19%)
  local copies, waits for them, and re-layouts  14.6 us (11%)
  other arithmetic  1.83 us (1%)
    ppermute x21, starting transfers between devices, ctx_swap(): return lax.ppermute(array, 'ctx', [(i, i ^ step) for i in range(ctx_size)])  28.4 us
    pallas_call x4, Pallas kernels, project(): pl.pallas_call(kernel, in_specs=[smem_spec] + [any_spec] * (7 + len(token...  15.1 us
    unnamed x72, local copies, waits for them, and re-layouts  14.5 us
    pallas_call x2, Pallas kernels, far_norm(): pl.pallas_call(far_first_kernel if first else far_rest_kernel, grid_spec=...  10.5 us
    ppermute x6, waiting for transfers between devices, near(): return lax.ppermute(array, 'head', [(i, i ^ 1) for i in range(4)])  9.35 us
    ppermute x21, waiting for transfers between devices, ctx_swap(): return lax.ppermute(array, 'ctx', [(i, i ^ step) for i in range(ctx_size)])  9.06 us
    pallas_call x1, Pallas kernels, on_device(): pl.pallas_call(local_kernel, in_specs=[smem_spec] + [any_spec] * 4 + [vme...  8.96 us
    pallas_call x1, Pallas kernels, on_device(): pl.pallas_call(own_kernel, in_specs=[smem_spec] + [any_spec] * (4 + 4 * C...  8.41 us
  transfers between devices with their start and end apart: 31, of which 11 were waited for; matrix products, arithmetic and copies ran while one was open for 1% of the time, Pallas kernels for 34%

profile of v5, /device:TPU:1, one launch (start us, length us, event | category | flops | bytes accessed | tf_op | source)
XLA Modules:
  0.0 126.5 jit_solution(14230348150294088894)
XLA Ops:
  0.1 3.3 %states.1 = (bf16[8,128,128]{2,1,0:T(8,128)(2,1)S(1)}, bf16[8,3,128,128]{3,2,1,0:T(8,128)(2,1)S(1)}, bf16[256,1024]{1,0:T(8,128)(2,1)S(1)}, bf16[256,1024]{1,0:T(8,128)(2,1)S(1)}) custom-call(s32[10]{0:T(128)S(1)} %stack.58.s_ref, bf16[1024,1024]{1,0:T(8,128)(2,1)} %k_hbm.3, bf16[1024,1024]{1,0:T(8,128)(2,1)} %v_hbm.3, bf16[1024,4096]{1,0:T(8,128)(2,1)} %w_hbm.5), custom_call_target="tpu_custom_call" | custom-call | flops 65536 | bytes 1792 | tf_op jit(solution)/shard_map/states/pallas_call | solution.py:330
  6.9 3.8 %collective-permute-start.3 = (bf16[4,128,128]{2,1,0:T(8,128)(2,1)S(1)}, bf16[4,128,128]{2,1,0:T(8,128)(2,1)S(1)}, u32[]{:S(2)}, u32[]{:S(2)}) collective-permute-start(bf16[4,128,128]{2,1,0:T(8,128)(2,1)S(1)} %add_convert_fusion.1.token_ref), channel_id=1, source_target_pairs={{0,24},{4,28},{8,16},{12,20},{16,8},{20,12},{24,0},{28,4},{32,56},... | collective-permute-start | bytes 393224 | tf_op jit(solution)/shard_map/ppermute | solution.py:311
  12.0 9.0 %local.1 = (f32[4,1024,256]{2,1,0:T(8,128)}, bf16[256,1024]{1,0:T(8,128)(2,1)S(1)}, bf16[256,1024]{1,0:T(8,128)(2,1)S(1)}) custom-call(s32[10]{0:T(128)S(1)} %stack.58.s_ref, bf16[1024,1024]{1,0:T(8,128)(2,1)} %refs_0_.3, bf16[1024,1024]{1,0:T(8,128)(2,1)} %k_hbm.3, bf16[1024,1024]{1,0:T(8,128)(2,1)} %v_hbm.3, bf16[1024,4096]{1,0:T(8,128)(2,1)} %w_hbm.5, ...), custom_call_target="tpu_custom_call" | custom-call | flops 393216 | bytes 3072 | tf_op jit(solution)/shard_map/local/pallas_call | solution.py:359
  23.7 3.0 %collective-permute-start.5 = (bf16[4,128,128]{2,1,0:T(8,128)(2,1)S(1)}, bf16[4,128,128]{2,1,0:T(8,128)(2,1)S(1)}, u32[]{:S(2)}, u32[]{:S(2)}) collective-permute-start(bf16[4,128,128]{2,1,0:T(8,128)(2,1)S(1)} %get-tuple-element.28), channel_id=1, source_target_pairs={{0,64},{4,68},{8,72},{12,76},{16,80},{20,84},{24,88},{28,92},{32,9... | collective-permute-start | bytes 393224 | tf_op jit(solution)/shard_map/ppermute | solution.py:311
  29.3 1.8 %collective-permute-start.7 = (bf16[2,4,128,128]{3,2,1,0:T(8,128)(2,1)}, bf16[2,4,128,128]{3,2,1,0:T(8,128)(2,1)S(1)}, u32[]{:S(2)}, u32[]{:S(2)}) collective-permute-start(bf16[2,4,128,128]{3,2,1,0:T(8,128)(2,1)} %pad_maximum_fusion.1.refs_4_.token_ref), channel_id=1, source_target_pairs={{0,4},{4,0},{8,12},{12,8},{16,20},{20,16},{24,28},{28,24},{32,36},... | collective-permute-start | bytes 786440 | tf_op jit(solution)/shard_map/ppermute | solution.py:311
  32.9 2.6 %collective-permute-start.8 = (bf16[2,4,128,128]{3,2,1,0:T(8,128)(2,1)S(1)}, bf16[2,4,128,128]{3,2,1,0:T(8,128)(2,1)}, u32[]{:S(2)}, u32[]{:S(2)}) collective-permute-start(bf16[2,4,128,128]{3,2,1,0:T(8,128)(2,1)S(1)} %pad_maximum_fusion.token_ref.refs_5_), channel_id=1, source_target_pairs={{0,4},{4,0},{8,12},{12,8},{16,20},{20,16},{24,28},{28,24},{32,36},... | collective-permute-start | bytes 786440 | tf_op jit(solution)/shard_map/ppermute | solution.py:311
  35.7 3.9 %collective-permute-done.14.data_ref = bf16[256,1024]{1,0:T(8,128)(2,1)S(1)} collective-permute-done((bf16[256,1024]{1,0:T(8,128)(2,1)}, bf16[256,1024]{1,0:T(8,128)(2,1)S(1)}, u32[]{:S(2)}, u32[]{:S(2)}) %collective-permute-start.14) | collective-permute-done | bytes 524320 | tf_op jit(solution)/shard_map/ppermute | solution.py:314
  39.6 4.3 %collective-permute-start.12 = (bf16[256,1024]{1,0:T(8,128)(2,1)S(1)}, bf16[256,1024]{1,0:T(8,128)(2,1)S(1)}, u32[]{:S(2)}, u32[]{:S(2)}) collective-permute-start(bf16[256,1024]{1,0:T(8,128)(2,1)S(1)} %copy-done.19), channel_id=1, source_target_pairs={{0,4},{4,0},{8,12},{12,8},{16,20},{20,16},{24,28},{28,24},{32,36},... | collective-permute-start | bytes 1572872 | tf_op jit(solution)/shard_map/ppermute | solution.py:311
  46.6 3.8 %far_first.1.token_ref = bf16[256,1024]{1,0:T(8,128)(2,1)} custom-call(s32[10]{0:T(128)S(1)} %stack.58.s_ref, bf16[2,4,128,128]{3,2,1,0:T(8,128)(2,1)S(1)} %copy-done.1, bf16[1024,1024]{1,0:T(8,128)(2,1)} %refs_0_.3, f32[4,1024,256]{2,1,0:T(8,128)} %get-tuple-element.18.token_ref.refs_1_, f32[8,8,1024]{2,1,0:T(8,128)S(1)} %copy-done.25, ...), custom_call_target="tpu_custom_call" | custom-call | flops 81920 | bytes 512 | tf_op jit(solution)/shard_map/far_first/pallas_call | solution.py:397
  54.5 6.6 %far_rest.1 = (bf16[256,1024]{1,0:T(8,128)(2,1)}, bf16[2,256,1024]{2,1,0:T(8,128)(2,1)}) custom-call(s32[10]{0:T(128)S(1)} %stack.58.s_ref, bf16[256,1024]{1,0:T(8,128)(2,1)} %far_first.1.token_ref, bf16[1024,1024]{1,0:T(8,128)(2,1)} %refs_0_.3, f32[4,1024,256]{2,1,0:T(8,128)} %get-tuple-element.18.token_ref.refs_1_, f32[8,8,1024]{2,1,0:T(8,128)S(1)} %copy-done.25, ...), custom_call_target="tpu_custom_call" | custom-call | flops 245760 | bytes 1536 | tf_op jit(solution)/shard_map/far_rest/pallas_call | solution.py:397
  63.5 3.7 %across0.1.refs_0_.token_ref = bf16[256,1024]{1,0:T(8,128)(2,1)S(1)} custom-call(s32[10]{0:T(128)S(1)} %stack.58.s_ref, bf16[2,256,1024]{2,1,0:T(8,128)(2,1)} %get-tuple-element.19.refs_0_.refs_1_.token_ref.refs_2_.keep, bf16[2,256,1024]{2,1,0:T(8,128)(2,1)} %get-tuple-element.19.refs_0_.refs_1_.token_ref.refs_2_.keep, ...), custom_call_target="tpu_custom_call" | custom-call | flops 262144 | bytes 1280 | tf_op jit(solution)/shard_map/across0/pallas_call | solution.py:434
  69.2 1.9 %collective-permute-start.21 = (bf16[256,1024]{1,0:T(8,128)(2,1)}, bf16[256,1024]{1,0:T(8,128)(2,1)}, u32[]{:S(2)}, u32[]{:S(2)}) collective-permute-start(bf16[256,1024]{1,0:T(8,128)(2,1)} %after.20.refs_5_.refs_8_), channel_id=1, source_target_pairs={{0,4},{4,0},{8,12},{12,8},{16,20},{20,16},{24,28},{28,24},{32,36},... | collective-permute-start | bytes 1572872 | tf_op jit(solution)/shard_map/ppermute | solution.py:311
  71.1 3.5 %collective-permute-done.20.data_ref = bf16[256,1024]{1,0:T(8,128)(2,1)S(1)} collective-permute-done((bf16[256,1024]{1,0:T(8,128)(2,1)}, bf16[256,1024]{1,0:T(8,128)(2,1)S(1)}, u32[]{:S(2)}, u32[]{:S(2)}) %collective-permute-start.20) | collective-permute-done | bytes 524320 | tf_op jit(solution)/shard_map/ppermute | solution.py:311
  74.6 1.8 %collective-permute-start.18 = (bf16[256,1024]{1,0:T(8,128)(2,1)}, bf16[256,1024]{1,0:T(8,128)(2,1)}, u32[]{:S(2)}, u32[]{:S(2)}) collective-permute-start(bf16[256,1024]{1,0:T(8,128)(2,1)} %copy-done.3), channel_id=1, source_target_pairs={{0,3},{1,2},{2,1},{3,0},{4,7},{5,6},{6,5},{7,4},{8,11},{9,10},{10,... | collective-permute-start | bytes 1572872 | tf_op jit(solution)/shard_map/ppermute | solution.py:317
  76.5 1.6 %collective-permute-start.22 = (bf16[256,1024]{1,0:T(8,128)(2,1)}, bf16[256,1024]{1,0:T(8,128)(2,1)}, u32[]{:S(2)}, u32[]{:S(2)}) collective-permute-start(bf16[256,1024]{1,0:T(8,128)(2,1)} %after.21.refs_6_.refs_9_), channel_id=1, source_target_pairs={{0,4},{4,0},{8,12},{12,8},{16,20},{20,16},{24,28},{28,24},{32,36},... | collective-permute-start | bytes 1572872 | tf_op jit(solution)/shard_map/ppermute | solution.py:311
  78.1 3.8 %across1.1.refs_0_.token_ref = bf16[256,1024]{1,0:T(8,128)(2,1)S(1)} custom-call(s32[10]{0:T(128)S(1)} %stack.58.s_ref, bf16[256,1024]{1,0:T(8,128)(2,1)S(1)} %copy-done.4, bf16[2,256,1024]{2,1,0:T(8,128)(2,1)} %get-tuple-element.19.refs_0_.refs_1_.token_ref.refs_2_.keep, bf16[256,1024]{1,0:T(8,128)(2,1)} %collective-permute-done.9.refs_2_.refs_3_, ...), custom_call_target="tpu_custom_call" | custom-call | flops 262144 | bytes 1280 | tf_op jit(solution)/shard_map/across1/pallas_call | solution.py:434
  83.5 1.7 %collective-permute-start.25 = (bf16[256,1024]{1,0:T(8,128)(2,1)}, bf16[256,1024]{1,0:T(8,128)(2,1)S(1)}, u32[]{:S(2)}, u32[]{:S(2)}) collective-permute-start(bf16[256,1024]{1,0:T(8,128)(2,1)} %after.23.refs_5_.refs_12_), channel_id=1, source_target_pairs={{0,32},{4,36},{8,40},{12,44},{16,48},{20,52},{24,56},{28,60},{32,0... | collective-permute-start | bytes 1572872 | tf_op jit(solution)/shard_map/ppermute | solution.py:311
  89.3 3.8 %across2.1.token_ref.refs_0_ = bf16[256,1024]{1,0:T(8,128)(2,1)S(1)} custom-call(s32[10]{0:T(128)S(1)} %stack.58.s_ref, bf16[256,1024]{1,0:T(8,128)(2,1)S(1)} %copy-done.6, bf16[256,1024]{1,0:T(8,128)(2,1)} %collective-permute-done.18.refs_1_.refs_16_, bf16[2,256,1024]{2,1,0:T(8,128)(2,1)} %get-tuple-element.19.refs_0_.refs_1_.token_ref.refs_2_.keep, ...), custom_call_target="tpu_custom_call" | custom-call | flops 262144 | bytes 1280 | tf_op jit(solution)/shard_map/across2/pallas_call | solution.py:434
  94.0 3.9 %collective-permute-done.25.data_ref = bf16[256,1024]{1,0:T(8,128)(2,1)S(1)} collective-permute-done((bf16[256,1024]{1,0:T(8,128)(2,1)}, bf16[256,1024]{1,0:T(8,128)(2,1)S(1)}, u32[]{:S(2)}, u32[]{:S(2)}) %collective-permute-start.25) | collective-permute-done | bytes 524320 | tf_op jit(solution)/shard_map/ppermute | solution.py:311
  103.1 3.8 %across3.1.token_ref = bf16[256,1024]{1,0:T(8,128)(2,1)S(1)} custom-call(s32[10]{0:T(128)S(1)} %stack.58.s_ref, bf16[256,1024]{1,0:T(8,128)(2,1)S(1)} %copy-done.24, bf16[256,1024]{1,0:T(8,128)(2,1)} %collective-permute-done.23.refs_1_.refs_17_, bf16[2,256,1024]{2,1,0:T(8,128)(2,1)} %get-tuple-element.19.refs_0_.refs_1_.token_ref.refs_2_.keep, ...), custom_call_target="tpu_custom_call" | custom-call | flops 262144 | bytes 1280 | tf_op jit(solution)/shard_map/across3/pallas_call | solution.py:434
  106.9 1.5 %collective-permute-start.30 = (bf16[256,1024]{1,0:T(8,128)(2,1)S(1)}, bf16[256,1024]{1,0:T(8,128)(2,1)S(1)}, u32[]{:S(2)}, u32[]{:S(2)}) collective-permute-start(bf16[256,1024]{1,0:T(8,128)(2,1)S(1)} %across3.1.token_ref), channel_id=1, source_target_pairs={{0,3},{1,2},{2,1},{3,0},{4,7},{5,6},{6,5},{7,4},{8,11},{9,10},{10,... | collective-permute-start | bytes 1572872 | tf_op jit(solution)/shard_map/ppermute | solution.py:317
  108.4 4.5 %collective-permute-done.28.got = bf16[256,1024]{1,0:T(8,128)(2,1)S(1)} collective-permute-done((bf16[256,1024]{1,0:T(8,128)(2,1)}, bf16[256,1024]{1,0:T(8,128)(2,1)S(1)}, u32[]{:S(2)}, u32[]{:S(2)}) %collective-permute-start.28) | collective-permute-done | bytes 524320 | tf_op jit(solution)/shard_map/ppermute | solution.py:314
  114.2 8.4 %own.1 = (bf16[256,4096]{1,0:T(8,128)(2,1)}, f32[256,1024]{1,0:T(8,128)S(1)}) custom-call(s32[10]{0:T(128)S(1)} %stack.58.s_ref, bf16[256,1024]{1,0:T(8,128)(2,1)S(1)} %across3.1.token_ref, bf16[2,256,1024]{2,1,0:T(8,128)(2,1)} %get-tuple-element.19.refs_0_.refs_1_.token_ref.refs_2_.keep, bf16[256,1024]{1,0:T(8,128)(2,1)S(1)} %collective-permute-done.28.got, ...), custom_call_target="tpu_custom_call" | custom-call | flops 1048576 | bytes 5120 | tf_op jit(solution)/shard_map/own/pallas_call | solution.py:463
  122.6 2.8 %collective-permute-done.30.got_ref = bf16[256,1024]{1,0:T(8,128)(2,1)S(1)} collective-permute-done((bf16[256,1024]{1,0:T(8,128)(2,1)S(1)}, bf16[256,1024]{1,0:T(8,128)(2,1)S(1)}, u32[]{:S(2)}, u32[]{:S(2)}) %collective-permute-start.30) | collective-permute-done | bytes 524320 | tf_op jit(solution)/shard_map/ppermute | solution.py:317
  (139 shorter events, 37.1 us)
Async XLA Ops:
  5.6 23.8 %collective-permute-start.10 = (bf16[256,1024]{1,0:T(8,128)(2,1)S(1)}, bf16[256,1024]{1,0:T(8,128)(2,1)S(1)}, u32[]{:S(2)}, u32[]{:S(2)}) collective-permute-start(bf16[256,1024]{1,0:T(8,128)(2,1)S(1)} %get-tuple-element.20), channel_id=1, source_target_pairs={{0,1},{1,0},{2,3},{3,2},{4,5},{5,4},{6,7},{7,6},{8,9},{9,8},{10,11... | collective-permute-start | bytes 1572872 | tf_op jit(solution)/shard_map/ppermute | solution.py:314
  6.9 14.9 %collective-permute-start.3 = (bf16[4,128,128]{2,1,0:T(8,128)(2,1)S(1)}, bf16[4,128,128]{2,1,0:T(8,128)(2,1)S(1)}, u32[]{:S(2)}, u32[]{:S(2)}) collective-permute-start(bf16[4,128,128]{2,1,0:T(8,128)(2,1)S(1)} %add_convert_fusion.1.token_ref), channel_id=1, source_target_pairs={{0,24},{4,28},{8,16},{12,20},{16,8},{20,12},{24,0},{28,4},{32,56},... | collective-permute-start | bytes 393224 | tf_op jit(solution)/shard_map/ppermute | solution.py:311
  10.8 11.9 %collective-permute-start.1 = (bf16[4,128,128]{2,1,0:T(8,128)(2,1)S(1)}, bf16[4,128,128]{2,1,0:T(8,128)(2,1)S(1)}, u32[]{:S(2)}, u32[]{:S(2)}) collective-permute-start(bf16[4,128,128]{2,1,0:T(8,128)(2,1)S(1)} %add_convert_fusion.1.token_ref), channel_id=1, source_target_pairs={{0,8},{4,12},{8,0},{12,4},{16,24},{20,28},{24,16},{28,20},{32,40},... | collective-permute-start | bytes 393224 | tf_op jit(solution)/shard_map/ppermute | solution.py:311
  10.8 11.9 %collective-permute-start.2 = (bf16[4,128,128]{2,1,0:T(8,128)(2,1)S(1)}, bf16[4,128,128]{2,1,0:T(8,128)(2,1)S(1)}, u32[]{:S(2)}, u32[]{:S(2)}) collective-permute-start(bf16[4,128,128]{2,1,0:T(8,128)(2,1)S(1)} %add_convert_fusion.1.token_ref), channel_id=1, source_target_pairs={{0,16},{4,20},{8,24},{12,28},{16,0},{20,4},{24,8},{28,12},{32,48},... | collective-permute-start | bytes 393224 | tf_op jit(solution)/shard_map/ppermute | solution.py:311
  27.4 12.2 %collective-permute-start.14 = (bf16[256,1024]{1,0:T(8,128)(2,1)}, bf16[256,1024]{1,0:T(8,128)(2,1)S(1)}, u32[]{:S(2)}, u32[]{:S(2)}) collective-permute-start(bf16[256,1024]{1,0:T(8,128)(2,1)} %after.16), channel_id=1, source_target_pairs={{0,1},{1,0},{2,3},{3,2},{4,5},{5,4},{6,7},{7,6},{8,9},{9,8},{10,11... | collective-permute-start | bytes 1572872 | tf_op jit(solution)/shard_map/ppermute | solution.py:314
  29.3 14.6 %collective-permute-start.7 = (bf16[2,4,128,128]{3,2,1,0:T(8,128)(2,1)}, bf16[2,4,128,128]{3,2,1,0:T(8,128)(2,1)S(1)}, u32[]{:S(2)}, u32[]{:S(2)}) collective-permute-start(bf16[2,4,128,128]{3,2,1,0:T(8,128)(2,1)} %pad_maximum_fusion.1.refs_4_.token_ref), channel_id=1, source_target_pairs={{0,4},{4,0},{8,12},{12,8},{16,20},{20,16},{24,28},{28,24},{32,36},... | collective-permute-start | bytes 786440 | tf_op jit(solution)/shard_map/ppermute | solution.py:311
  31.1 20.6 %collective-permute-start.11 = (bf16[256,1024]{1,0:T(8,128)(2,1)}, bf16[256,1024]{1,0:T(8,128)(2,1)S(1)}, u32[]{:S(2)}, u32[]{:S(2)}) collective-permute-start(bf16[256,1024]{1,0:T(8,128)(2,1)} %after.14.refs_4_.refs_0_), channel_id=1, source_target_pairs={{0,8},{4,12},{8,0},{12,4},{16,24},{20,28},{24,16},{28,20},{32,40},... | collective-permute-start | bytes 1572872 | tf_op jit(solution)/shard_map/ppermute | solution.py:311
  32.9 11.8 %collective-permute-start.8 = (bf16[2,4,128,128]{3,2,1,0:T(8,128)(2,1)S(1)}, bf16[2,4,128,128]{3,2,1,0:T(8,128)(2,1)}, u32[]{:S(2)}, u32[]{:S(2)}) collective-permute-start(bf16[2,4,128,128]{3,2,1,0:T(8,128)(2,1)S(1)} %pad_maximum_fusion.token_ref.refs_5_), channel_id=1, source_target_pairs={{0,4},{4,0},{8,12},{12,8},{16,20},{20,16},{24,28},{28,24},{32,36},... | collective-permute-start | bytes 786440 | tf_op jit(solution)/shard_map/ppermute | solution.py:311
  35.5 25.7 %collective-permute-start.19 = (bf16[256,1024]{1,0:T(8,128)(2,1)}, bf16[256,1024]{1,0:T(8,128)(2,1)}, u32[]{:S(2)}, u32[]{:S(2)}) collective-permute-start(bf16[256,1024]{1,0:T(8,128)(2,1)} %after.19), channel_id=1, source_target_pairs={{0,1},{1,0},{2,3},{3,2},{4,5},{5,4},{6,7},{7,6},{8,9},{9,8},{10,11... | collective-permute-start | bytes 1572872 | tf_op jit(solution)/shard_map/ppermute | solution.py:314
  39.6 22.5 %collective-permute-start.12 = (bf16[256,1024]{1,0:T(8,128)(2,1)S(1)}, bf16[256,1024]{1,0:T(8,128)(2,1)S(1)}, u32[]{:S(2)}, u32[]{:S(2)}) collective-permute-start(bf16[256,1024]{1,0:T(8,128)(2,1)S(1)} %copy-done.19), channel_id=1, source_target_pairs={{0,4},{4,0},{8,12},{12,8},{16,20},{20,16},{24,28},{28,24},{32,36},... | collective-permute-start | bytes 1572872 | tf_op jit(solution)/shard_map/ppermute | solution.py:311
  44.7 16.6 %collective-permute-start.15 = (bf16[256,1024]{1,0:T(8,128)(2,1)}, bf16[256,1024]{1,0:T(8,128)(2,1)S(1)}, u32[]{:S(2)}, u32[]{:S(2)}) collective-permute-start(bf16[256,1024]{1,0:T(8,128)(2,1)} %after.17.refs_4_), channel_id=1, source_target_pairs={{0,32},{4,36},{8,40},{12,44},{16,48},{20,52},{24,56},{28,60},{32,0... | collective-permute-start | bytes 1572872 | tf_op jit(solution)/shard_map/ppermute | solution.py:311
  50.5 13.0 %collective-permute-start.9 = (bf16[256,1024]{1,0:T(8,128)(2,1)}, bf16[256,1024]{1,0:T(8,128)(2,1)}, u32[]{:S(2)}, u32[]{:S(2)}) collective-permute-start(bf16[256,1024]{1,0:T(8,128)(2,1)} %far_first.1.token_ref), channel_id=1, source_target_pairs={{0,1},{1,0},{2,3},{3,2},{4,5},{5,4},{6,7},{7,6},{8,9},{9,8},{10,11... | collective-permute-start | bytes 1572872 | tf_op jit(solution)/shard_map/ppermute | solution.py:314
  61.1 15.3 %collective-permute-start.16 = (bf16[256,1024]{1,0:T(8,128)(2,1)S(1)}, bf16[256,1024]{1,0:T(8,128)(2,1)}, u32[]{:S(2)}, u32[]{:S(2)}) collective-permute-start(bf16[256,1024]{1,0:T(8,128)(2,1)S(1)} %copy-done.8), channel_id=1, source_target_pairs={{0,4},{4,0},{8,12},{12,8},{16,20},{20,16},{24,28},{28,24},{32,36},... | collective-permute-start | bytes 1572872 | tf_op jit(solution)/shard_map/ppermute | solution.py:311
  61.3 13.3 %collective-permute-start.20 = (bf16[256,1024]{1,0:T(8,128)(2,1)}, bf16[256,1024]{1,0:T(8,128)(2,1)S(1)}, u32[]{:S(2)}, u32[]{:S(2)}) collective-permute-start(bf16[256,1024]{1,0:T(8,128)(2,1)} %after.20.refs_5_.refs_8_), channel_id=1, source_target_pairs={{0,8},{4,12},{8,0},{12,4},{16,24},{20,28},{24,16},{28,20},{32,40},... | collective-permute-start | bytes 1572872 | tf_op jit(solution)/shard_map/ppermute | solution.py:311
  62.1 16.0 %collective-permute-start.17 = (bf16[256,1024]{1,0:T(8,128)(2,1)}, bf16[256,1024]{1,0:T(8,128)(2,1)}, u32[]{:S(2)}, u32[]{:S(2)}) collective-permute-start(bf16[256,1024]{1,0:T(8,128)(2,1)} %after.18.refs_5_), channel_id=1, source_target_pairs={{0,4},{4,0},{8,12},{12,8},{16,20},{20,16},{24,28},{28,24},{32,36},... | collective-permute-start | bytes 1572872 | tf_op jit(solution)/shard_map/ppermute | solution.py:311
  68.0 14.8 %collective-permute-start.24 = (bf16[256,1024]{1,0:T(8,128)(2,1)}, bf16[256,1024]{1,0:T(8,128)(2,1)S(1)}, u32[]{:S(2)}, u32[]{:S(2)}) collective-permute-start(bf16[256,1024]{1,0:T(8,128)(2,1)} %after.22), channel_id=1, source_target_pairs={{0,1},{1,0},{2,3},{3,2},{4,5},{5,4},{6,7},{7,6},{8,9},{9,8},{10,11... | collective-permute-start | bytes 1572872 | tf_op jit(solution)/shard_map/ppermute | solution.py:314
  69.2 16.9 %collective-permute-start.21 = (bf16[256,1024]{1,0:T(8,128)(2,1)}, bf16[256,1024]{1,0:T(8,128)(2,1)}, u32[]{:S(2)}, u32[]{:S(2)}) collective-permute-start(bf16[256,1024]{1,0:T(8,128)(2,1)} %after.20.refs_5_.refs_8_), channel_id=1, source_target_pairs={{0,4},{4,0},{8,12},{12,8},{16,20},{20,16},{24,28},{28,24},{32,36},... | collective-permute-start | bytes 1572872 | tf_op jit(solution)/shard_map/ppermute | solution.py:311
  74.6 13.7 %collective-permute-start.18 = (bf16[256,1024]{1,0:T(8,128)(2,1)}, bf16[256,1024]{1,0:T(8,128)(2,1)}, u32[]{:S(2)}, u32[]{:S(2)}) collective-permute-start(bf16[256,1024]{1,0:T(8,128)(2,1)} %copy-done.3), channel_id=1, source_target_pairs={{0,3},{1,2},{2,1},{3,0},{4,7},{5,6},{6,5},{7,4},{8,11},{9,10},{10,... | collective-permute-start | bytes 1572872 | tf_op jit(solution)/shard_map/ppermute | solution.py:317
  83.5 14.3 %collective-permute-start.25 = (bf16[256,1024]{1,0:T(8,128)(2,1)}, bf16[256,1024]{1,0:T(8,128)(2,1)S(1)}, u32[]{:S(2)}, u32[]{:S(2)}) collective-permute-start(bf16[256,1024]{1,0:T(8,128)(2,1)} %after.23.refs_5_.refs_12_), channel_id=1, source_target_pairs={{0,32},{4,36},{8,40},{12,44},{16,48},{20,52},{24,56},{28,60},{32,0... | collective-permute-start | bytes 1572872 | tf_op jit(solution)/shard_map/ppermute | solution.py:311
  85.3 15.5 %collective-permute-start.23 = (bf16[256,1024]{1,0:T(8,128)(2,1)}, bf16[256,1024]{1,0:T(8,128)(2,1)}, u32[]{:S(2)}, u32[]{:S(2)}) collective-permute-start(bf16[256,1024]{1,0:T(8,128)(2,1)} %copy-done.5), channel_id=1, source_target_pairs={{0,3},{1,2},{2,1},{3,0},{4,7},{5,6},{6,5},{7,4},{8,11},{9,10},{10,... | collective-permute-start | bytes 1572872 | tf_op jit(solution)/shard_map/ppermute | solution.py:317
  86.1 14.7 %collective-permute-start.26 = (bf16[256,1024]{1,0:T(8,128)(2,1)}, bf16[256,1024]{1,0:T(8,128)(2,1)}, u32[]{:S(2)}, u32[]{:S(2)}) collective-permute-start(bf16[256,1024]{1,0:T(8,128)(2,1)} %after.23.refs_5_.refs_12_), channel_id=1, source_target_pairs={{0,4},{4,0},{8,12},{12,8},{16,20},{20,16},{24,28},{28,24},{32,36},... | collective-permute-start | bytes 1572872 | tf_op jit(solution)/shard_map/ppermute | solution.py:311
  99.2 13.8 %collective-permute-start.28 = (bf16[256,1024]{1,0:T(8,128)(2,1)}, bf16[256,1024]{1,0:T(8,128)(2,1)S(1)}, u32[]{:S(2)}, u32[]{:S(2)}) collective-permute-start(bf16[256,1024]{1,0:T(8,128)(2,1)} %after.25), channel_id=1, source_target_pairs={{0,1},{1,0},{2,3},{3,2},{4,5},{5,4},{6,7},{7,6},{8,9},{9,8},{10,11... | collective-permute-start | bytes 1572872 | tf_op jit(solution)/shard_map/ppermute | solution.py:314
  99.5 14.7 %collective-permute-start.29 = (bf16[256,1024]{1,0:T(8,128)(2,1)}, bf16[256,1024]{1,0:T(8,128)(2,1)S(1)}, u32[]{:S(2)}, u32[]{:S(2)}) collective-permute-start(bf16[256,1024]{1,0:T(8,128)(2,1)} %copy-done.23), channel_id=1, source_target_pairs={{0,3},{1,2},{2,1},{3,0},{4,7},{5,6},{6,5},{7,4},{8,11},{9,10},{10,... | collective-permute-start | bytes 1572872 | tf_op jit(solution)/shard_map/ppermute | solution.py:317
  106.9 18.5 %collective-permute-start.30 = (bf16[256,1024]{1,0:T(8,128)(2,1)S(1)}, bf16[256,1024]{1,0:T(8,128)(2,1)S(1)}, u32[]{:S(2)}, u32[]{:S(2)}) collective-permute-start(bf16[256,1024]{1,0:T(8,128)(2,1)S(1)} %across3.1.token_ref), channel_id=1, source_target_pairs={{0,3},{1,2},{2,1},{3,0},{4,7},{5,6},{6,5},{7,4},{8,11},{9,10},{10,... | collective-permute-start | bytes 1572872 | tf_op jit(solution)/shard_map/ppermute | solution.py:317
  (43 other events, 214.7 us)
